TPU v7x, 128 devices: a whole 4x4x4 slice. The times are simulated.
128 devices in a mesh: tm: 32 (over x, y, core), seq: 4 (over z).
Axes of the slice: x: 4, y: 4, z: 4, core: 2. Of those that a mesh axis runs over, the one named last changes fastest.
Arguments:
- latents: bfloat16 [128, 16, 2048], P('tm', None, 'seq'), may hold values from -6 to 6
- hidden: bfloat16 [65536, 3072], P(('tm', 'seq')), may hold values from -6 to 6
- grad_out: bfloat16 [128, 512, 2048], P('tm', None, 'seq'), may hold values from -6 to 6
- conv_in_w: bfloat16 [3, 512, 16], replicated, may hold values from -0.875 to 0.875
- conv_in_b: float32 [512], replicated, may hold values from -4 to 4
- conv_w: bfloat16 [3, 512, 512], replicated, may hold values from -0.15625 to 0.15625
- final_w: bfloat16 [3072, 64], replicated, may hold values from -0.109375 to 0.109375
- modulation: float32 [2, 3072], replicated, may hold values from -3 to 3
- clip_start: int32 [128], replicated, may hold values from 0 to 127, as said below
Outputs:
- hidden_input_gradient: bfloat16 [65536, 3072], P(('tm', 'seq'))
- convolution_weight_gradient: float32 [512, 3, 512], P(('tm', 'seq'))
- input_convolution_gradient: float32 [3, 512, 16], replicated
- input_bias_gradient: float32 [512], replicated
- final_grad: float32 [3072, 64], replicated
- modulation_grad: float32 [2, 3072], replicated
Inputs may be any that keep to these rules, and one draw needn't show every extreme that they name: Clips are consecutive runs of frames: clip_start never falls, clip_start[t] <= t, clip_start[t] == t at each clip's first frame; every clip has 9 to 33 frames except the last two, which are cut by the bin's end; the bin's last frame begins a clip of its own.
All inputs are finite; a program needn't handle non-finite values.
Results may differ from a plain program's by a relative error of at most 0.012.
Values may be sent and summed in bfloat16 or wider, within the bound.
No kernel may reach another device: no remote copies, remote signals or barrier semaphores. Data moves between devices by JAX's collectives and lax.ppermute only.
A program may use at most 128 MiB of HBM per device.

v0:
```python
import jax
import jax.numpy as jnp
from jax import lax
from jax.experimental import pallas as pl
from jax.experimental.pallas import tpu as pltpu
from jax.sharding import PartitionSpec as P

BF = jnp.bfloat16
F32 = jnp.float32
VMEM = pl.BlockSpec(memory_space=pltpu.VMEM)
SMEM = pl.BlockSpec(memory_space=pltpu.SMEM)
EDGE = 4
TAPS = 3
SLAB = 4
CL = 16
C = 512
PX = 512
D = 3072
E = 64
NTOK = 512
FRAMES = 128
BOTH = ("tm", "seq")


def params(mib):
    return pltpu.CompilerParams(vmem_limit_bytes=mib * 1024 * 1024)


def cost(flops, nbytes, trans=0):
    return pl.CostEstimate(flops=flops, bytes_accessed=nbytes, transcendentals=trans)


def mm(a, b, ca, cb):
    return lax.dot_general(a, b, (((ca,), (cb,)), ((), ())), preferred_element_type=F32)


def clip_rel(clip_ref, first, frame):
    whole = first + frame
    start = clip_ref[jnp.clip(whole, 0, FRAMES - 1)]
    return jnp.where(whole >= FRAMES, frame, start - first)


def source(clip_ref, first, frame, tap):
    return jnp.maximum(frame - tap, clip_rel(clip_ref, first, frame))


def k_prep(hidden_ref, conv_w_ref, normed_ref, conv_t_ref):
    gain = 1.0 / D

    def rows(i, _):
        at = pl.ds(pl.multiple_of(i * 64, 64), 64)
        h = hidden_ref[at, :].astype(F32)
        center = h - jnp.sum(h, axis=1, keepdims=True) * gain
        var = jnp.sum(center * center, axis=1, keepdims=True) * gain
        normed_ref[at, :] = (center * lax.rsqrt(var + 1e-06)).astype(BF)
        return 0

    lax.fori_loop(0, NTOK // 64, rows, 0)
    for k in range(TAPS):
        conv_t_ref[k] = conv_w_ref[k].T


def load_taps(clip_ref, first, lat_ref, z_ref, slot, frame, base):
    for k in range(TAPS):
        src = jnp.clip(source(clip_ref, first, frame, k) + base, 0, lat_ref.shape[0] - 1)
        z_ref[slot, k * CL : (k + 1) * CL, :] = lat_ref[src]


def k_first(
    clip_ref, prev_ref, lat_ref, win_ref, bias_ref, grad_ref, conv_t_ref,
    act_ref, slope_ref, acc_out_ref, part_ref, halo_ref, icg_ref,
    all_ref, z_ref, wcat_ref, acc_ref, sl_ref, lacc_ref, icg_acc,
):
    first = lax.axis_index("tm") * SLAB
    all_ref[:SLAB] = prev_ref[...]
    all_ref[SLAB:] = lat_ref[...]
    for k in range(TAPS):
        wcat_ref[k * CL : (k + 1) * CL, :] = win_ref[k]
    bias = bias_ref[...]
    high = bias.astype(BF)
    rest = bias - high.astype(F32)
    mid = rest.astype(BF)
    low = (rest - mid.astype(F32)).astype(BF)
    row = lax.broadcasted_iota(jnp.int32, (CL, C), 0)
    tail = jnp.where(row == 0, high.astype(F32), 0.0)
    tail = jnp.where(row == 1, mid.astype(F32), tail)
    tail = jnp.where(row == 2, low.astype(F32), tail)
    wcat_ref[TAPS * CL :, :] = tail.astype(BF)
    wcol = wcat_ref[...].T
    acc_ref[...] = jnp.zeros_like(acc_ref)
    lacc_ref[...] = jnp.zeros_like(lacc_ref)
    icg_acc[...] = jnp.zeros_like(icg_acc)

    def pre_step(j, _):
        load_taps(clip_ref, first, all_ref, z_ref, j, j - 2, SLAB)
        z_ref[j, TAPS * CL :, :] = jnp.ones((CL, PX), BF)
        pre = mm(wcol, z_ref[j], 1, 0)
        sig = 0.5 * jnp.tanh(0.5 * pre) + 0.5
        act_ref[j] = (pre * sig).astype(BF)
        sl_ref[j] = sig * (1.0 + pre * (1.0 - sig))
        return 0

    lax.fori_loop(0, SLAB + 2, pre_step, 0)

    def act_step(t, _):
        for k in range(TAPS):
            src = source(clip_ref, first, t, k)
            src = jnp.where(src < 0, SLAB, src)
            acc_ref[src] += mm(conv_t_ref[k], grad_ref[t], 1, 0)
        return 0

    lax.fori_loop(0, SLAB, act_step, 0)

    def pre_grad(t, _):
        gp = (acc_ref[t] * sl_ref[t + 2]).astype(BF)
        back = mm(wcat_ref[...], gp, 1, 0)
        for k in range(TAPS):
            src = source(clip_ref, first, t, k) + 2
            lacc_ref[src] += back[k * CL : (k + 1) * CL]
        icg_acc[...] += mm(z_ref[t + 2], gp, 1, 1)
        return 0

    lax.fori_loop(0, 2, pre_grad, 0)
    halo_ref[...] = lacc_ref[:2]
    part_ref[...] = lacc_ref[2:]
    icg_ref[...] = icg_acc[...]
    slope_ref[...] = sl_ref[SLAB:]
    acc_out_ref[...] = acc_ref[2:SLAB]


def k_weight(clip_ref, grad_ref, act_ref, out_ref, acc_ref):
    first = lax.axis_index("tm") * SLAB
    acc_ref[...] = jnp.zeros_like(acc_ref)

    def step(t, _):
        for k in range(TAPS):
            src = jnp.maximum(source(clip_ref, first, t, k), -2) + 2
            acc_ref[:, k * C : (k + 1) * C] += mm(grad_ref[t], act_ref[src], 1, 1)
        return 0

    lax.fori_loop(0, SLAB, step, 0)
    upper = lax.broadcasted_iota(jnp.int32, (64, 8, 128), 1) < 4
    for jj in range(0, TAPS * C // 128, 4):
        even, odd = [], []
        for h in range(2):
            at = (jj + 2 * h) * 128
            a = acc_ref[:, at : at + 128].reshape(64, 8, 128)
            b = acc_ref[:, at + 128 : at + 256].reshape(64, 8, 128)
            even.append(jnp.where(upper, a, pltpu.roll(b, 4, 1)))
            odd.append(jnp.where(upper, pltpu.roll(a, 4, 1), b))
        out_ref[:, 0, jj * 4 : jj * 4 + 16, :] = jnp.concatenate(even, axis=1).astype(BF)
        out_ref[:, 1, jj * 4 : jj * 4 + 16, :] = jnp.concatenate(odd, axis=1).astype(BF)


def k_second(
    clip_ref, next_ref, lat_ref, win_ref, conv_t_ref, acc_in_ref, slope_ref, part_ref, halo_ref, icg_in_ref,
    tok_ref, icg_ref, acc_ref, z_ref, wcat_ref, lacc_ref, icg_acc, low_ref,
):
    first = lax.axis_index("tm") * SLAB
    acc_ref[:2] = acc_in_ref[...]
    for k in range(TAPS):
        wcat_ref[k * CL : (k + 1) * CL, :] = win_ref[k]
    for t, k in ((0, 1), (0, 2), (1, 2)):
        src = source(clip_ref, first, SLAB + t, k) - 2
        acc_ref[jnp.minimum(src, 2)] += mm(conv_t_ref[k], next_ref[t], 1, 0)
    lacc_ref[...] = jnp.zeros_like(lacc_ref)
    lacc_ref[:SLAB] = part_ref[...]
    lacc_ref[2:SLAB] += halo_ref[...]
    icg = icg_in_ref[...]
    for t in range(2):
        gp = (acc_ref[t] * slope_ref[t]).astype(BF)
        load_taps(clip_ref, first, lat_ref, z_ref, t, t + 2, 0)
        z_ref[t, TAPS * CL :, :] = jnp.ones((CL, PX), BF)
        back = mm(wcat_ref[...], gp, 1, 0)
        for k in range(TAPS):
            src = source(clip_ref, first, t + 2, k)
            lacc_ref[src] += back[k * CL : (k + 1) * CL]
        icg = icg + mm(z_ref[t], gp, 1, 1)
    icg_acc[...] = icg
    for f in range(SLAB):
        low_ref[f * CL : (f + 1) * CL, :] = lacc_ref[f].astype(BF)
    r = lax.broadcasted_iota(jnp.int32, (PX, PX), 0)
    c = lax.broadcasted_iota(jnp.int32, (PX, PX), 1)
    pick = (((r & 3) << 7) + (r >> 2) == c).astype(F32).astype(BF)
    tok_ref[...] = mm(low_ref[...], pick, 1, 0).astype(BF)
    for rb in range(4):
        for lb in range(4):
            icg_ref[rb * 4 + lb] = icg_acc[rb * 16 : (rb + 1) * 16, lb * 128 : (lb + 1) * 128].astype(BF)


def k_grad(recv_ref, normed_ref, icg_ref, pack_ref, tok_ref, raw_ref, g_ref):
    for s in range(4):
        for q in range(EDGE):
            raw_ref[q * CL : (q + 1) * CL, s * 128 : (s + 1) * 128] = recv_ref[
                s, :, q * 128 : (q + 1) * 128
            ]
    r = lax.broadcasted_iota(jnp.int32, (E, E), 0)
    c = lax.broadcasted_iota(jnp.int32, (E, E), 1)
    order = (((r & 3) << 4) + (r >> 2) == c).astype(F32).astype(BF)
    tok = mm(order, raw_ref[...], 1, 0)
    tok_ref[...] = tok.astype(BF)
    total = jnp.broadcast_to(jnp.sum(tok, axis=1, keepdims=True), (E, 128)).astype(BF)
    for lb in range(D // 512):
        g = mm(tok_ref[...], normed_ref[:, lb * 512 : (lb + 1) * 512], 1, 0).astype(BF)
        for u in range(4):
            for rb in range(4):
                pack_ref[rb * 24 + lb * 4 + u] = g[rb * 16 : (rb + 1) * 16, u * 128 : (u + 1) * 128]
    pack_ref[96:112] = icg_ref[...]
    for rb in range(4):
        pack_ref[112 + rb] = total[rb * 16 : (rb + 1) * 16]
    pack_ref[116:] = jnp.zeros((12, 16, 128), BF)


def k_hidden(tok_ref, hidden_ref, wt_ref, mod_ref, out_ref):
    gain = 1.0 / D
    h = hidden_ref[...].astype(F32)
    center = h - jnp.sum(h, axis=1, keepdims=True) * gain
    var = jnp.sum(center * center, axis=1, keepdims=True) * gain
    inv = lax.rsqrt(var + 1e-06)
    normed = center * inv
    mod_in = mm(tok_ref[...].T, wt_ref[...], 1, 0)
    ng = mod_in * (1.0 + mod_ref[1:2, :])
    m1 = jnp.sum(ng, axis=1, keepdims=True) * gain
    m2 = jnp.sum(ng * normed, axis=1, keepdims=True) * gain
    out_ref[...] = (inv * (ng - m1 - normed * m2)).astype(BF)


def k_sum(recv_ref, out_ref):
    total = jnp.sum(recv_ref[...].astype(F32), axis=0).astype(BF)
    out_ref[...] = jnp.broadcast_to(total[None], out_ref.shape)


def k_last(all_ref, wt_ref, mod_ref, final_ref, modg_ref, icg_ref, bias_ref):
    tot = [all_ref[112 + rb].astype(F32) for rb in range(4)]
    for lb in range(D // 128):
        at = slice(lb * 128, (lb + 1) * 128)
        scale = 1.0 + mod_ref[1:2, at]
        shift = mod_ref[0:1, at]
        s0 = jnp.zeros((1, 128), F32)
        s1 = jnp.zeros((1, 128), F32)
        for rb in range(4):
            rows = slice(rb * 16, (rb + 1) * 16)
            g = all_ref[rb * 24 + lb].astype(F32)
            w = wt_ref[rows, at].astype(F32)
            final_ref[rows, at] = g * scale + shift * tot[rb]
            s0 = s0 + jnp.sum(w * tot[rb], axis=0, keepdims=True)
            s1 = s1 + jnp.sum(w * g, axis=0, keepdims=True)
        modg_ref[0:1, at] = s0
        modg_ref[1:2, at] = s1
    for rb in range(3):
        for lb in range(4):
            icg_ref[rb * 16 : (rb + 1) * 16, lb * 128 : (lb + 1) * 128] = all_ref[96 + rb * 4 + lb].astype(F32)
    for lb in range(4):
        bias_ref[:, lb * 128 : (lb + 1) * 128] = all_ref[96 + 12 + lb].astype(F32)[0:1]


def k_weight_sum(recv_ref, out_ref):
    total = jnp.sum(recv_ref[...].astype(F32), axis=0)
    for k in range(TAPS):
        for u in range(4):
            j = k * 4 + u
            out_ref[k, :, u * 128 : (u + 1) * 128] = total[j * 4 : (j + 1) * 4]


def call(fn, outs, specs, scratch=(), mib=40, est=None, name=None):
    return pl.pallas_call(
        fn,
        out_shape=outs,
        in_specs=specs,
        out_specs=jax.tree.map(lambda _: VMEM, outs),
        scratch_shapes=list(scratch),
        compiler_params=params(mib),
        cost_estimate=est,
        name=name,
    )


def sds(shape, dtype):
    return jax.ShapeDtypeStruct(shape, dtype)


def shifted(block, distance):
    n = lax.axis_size("tm")
    route = [(i - distance, i) for i in range(n) if 0 <= i - distance < n]
    return lax.ppermute(block, "tm", route)


def exchange(block, axes):
    return lax.all_to_all(block, axes, split_axis=0, concat_axis=0, tiled=True)


def local(latents, hidden, grad_out, conv_in_w, conv_in_b, conv_w, final_w, modulation, clip_start):
    win = conv_in_w.transpose(0, 2, 1)
    wt = final_w.T
    bias = conv_in_b.reshape(1, C)
    grad_next = shifted(grad_out[:2], -1)
    lat_prev = shifted(latents, 1)
    unit = 2 * C * C * PX
    normed, conv_t = call(
        k_prep, (sds((NTOK, D), BF), sds((TAPS, C, C), BF)), [VMEM] * 2,
        est=cost(10 * NTOK * D, 10 << 20), name="prep",
    )(hidden, conv_w)
    act, slope, acc, part, halo, icg_part = call(
        k_first,
        (
            sds((SLAB + 2, C, PX), BF), sds((2, C, PX), F32), sds((2, C, PX), F32),
            sds((SLAB, CL, PX), F32), sds((2, CL, PX), F32), sds((E, C), F32),
        ),
        [SMEM] + [VMEM] * 6,
        [
            pltpu.VMEM((2 * SLAB, CL, PX), BF), pltpu.VMEM((SLAB + 2, E, PX), BF), pltpu.VMEM((E, C), BF),
            pltpu.VMEM((SLAB + 1, C, PX), F32), pltpu.VMEM((SLAB + 2, C, PX), F32),
            pltpu.VMEM((SLAB + 2, CL, PX), F32), pltpu.VMEM((E, C), F32),
        ],
        est=cost(16 * unit, 10 << 20), name="first",
    )(clip_start, lat_prev, latents, win, bias, grad_out, conv_t)
    halo_recv = shifted(halo, -1)
    weight_pack = call(
        k_weight, sds((64, 2, 48, 128), BF), [SMEM] + [VMEM] * 2,
        [pltpu.VMEM((C, TAPS * C), F32)], est=cost(12 * unit, 7 << 20), name="weight",
    )(clip_start, grad_out, act)
    tok_part, icg_blocks = call(
        k_second, (sds((SLAB * CL, PX), BF), sds((16, 16, 128), BF)), [SMEM] + [VMEM] * 9,
        [
            pltpu.VMEM((3, C, PX), F32), pltpu.VMEM((2, E, PX), BF), pltpu.VMEM((TAPS * CL, C), BF),
            pltpu.VMEM((SLAB, CL, PX), F32), pltpu.VMEM((E, C), F32), pltpu.VMEM((SLAB * CL, PX), BF),
        ],
        est=cost(6 * unit, 8 << 20), name="second",
    )(clip_start, grad_next, latents, win, conv_t, acc, slope, part, halo_recv, icg_part)
    tok_recv = exchange(tok_part, "seq").reshape(4, CL, PX)
    pack, tok = call(
        k_grad, (sds((128, 16, 128), BF), sds((E, NTOK), BF)), [VMEM] * 3,
        [pltpu.VMEM((E, NTOK), BF), pltpu.VMEM((E, D), F32)],
        est=cost(2 * NTOK * D * E, 5 << 20), name="grad",
    )(tok_recv, normed, icg_blocks)
    recv = exchange(pack, BOTH)
    hidden_grad = pl.pallas_call(
        k_hidden,
        grid=(4,),
        out_shape=sds((NTOK, D), BF),
        in_specs=[
            pl.BlockSpec((E, 128), lambda i: (0, i)),
            pl.BlockSpec((128, D), lambda i: (i, 0)),
            pl.BlockSpec((E, D), lambda i: (0, 0)),
            pl.BlockSpec((2, D), lambda i: (0, 0)),
        ],
        out_specs=pl.BlockSpec((128, D), lambda i: (i, 0)),
        compiler_params=params(40),
        cost_estimate=cost(2 * NTOK * D * E, 6 << 20),
        name="hidden",
    )(tok, hidden, wt, modulation)
    weight_recv = exchange(weight_pack.reshape(128, 48, 128), BOTH)
    copies = call(k_sum, sds((128, 16, 128), BF), [VMEM], est=cost(1 << 18, 1 << 20), name="sum")(recv)
    everything = exchange(copies, BOTH)
    weight_grad = call(
        k_weight_sum, sds((TAPS, 4, C), F32), [VMEM], est=cost(1 << 20, 1536 << 10), name="weight_sum"
    )(weight_recv)
    final_t, mod_grad, icg, bias_grad = call(
        k_last, (sds((E, D), F32), sds((2, D), F32), sds((TAPS * CL, C), F32), sds((1, C), F32)), [VMEM] * 3,
        est=cost(1 << 20, 2 << 20), name="last",
    )(everything, wt, modulation)
    return (
        hidden_grad,
        weight_grad.transpose(1, 0, 2),
        icg.reshape(TAPS, CL, C).transpose(0, 2, 1),
        bias_grad.reshape(C),
        final_t.T,
        mod_grad,
    )


def solution(mesh):
    return jax.shard_map(
        local,
        mesh=mesh,
        in_specs=(
            P("tm", None, "seq"),
            P(("tm", "seq"), None),
            P("tm", None, "seq"),
            P(), P(), P(), P(), P(), P(),
        ),
        out_specs=(P(("tm", "seq"), None), P(("tm", "seq"), None, None), P(), P(), P(), P()),
        check_vma=False,
    )
```

profile of v0, /device:TPU:1, one launch (start us, length us, event | category | flops | bytes accessed | tf_op | source)
XLA Modules:
  0.0 121.6 jit_solution(8317660890803938833)
XLA Ops:
  0.6 0.0 copy-start.11
  0.6 0.0 copy-start.7
  0.7 0.0 copy-start.14
  0.7 0.0 copy-start.15
  0.7 0.0 copy-start.16
  0.7 1.4 %slice.3 = bf16[2,512,512]{2,1,0:T(8,128)(2,1)S(1)} slice(bf16[4,512,512]{2,1,0:T(8,128)(2,1)} %grad_ref.3), slice={[0:2], [0:512], [0:512]} | slice | bytes 2097152 | tf_op jit(solution)/shard_map/slice | solution.py:296
  2.1 3.3 %collective-permute-start = (bf16[2,512,512]{2,1,0:T(8,128)(2,1)S(1)}, bf16[2,512,512]{2,1,0:T(8,128)(2,1)S(1)}, u32[]{:S(2)}, u32[]{:S(2)}) collective-permute-start(bf16[2,512,512]{2,1,0:T(8,128)(2,1)S(1)} %slice.3), channel_id=1, source_target_pairs={{4,0},{8,4},{12,8},{16,12},{20,16},{24,20},{28,24},{32,28},{36,32}... | collective-permute-start | bytes 3145736 | tf_op jit(solution)/shard_map/ppermute | solution.py:285
  5.4 3.2 %collective-permute-start.1 = (bf16[4,16,512]{2,1,0:T(8,128)(2,1)S(1)}, bf16[4,16,512]{2,1,0:T(8,128)(2,1)S(1)}, u32[]{:S(2)}, u32[]{:S(2)}) collective-permute-start(bf16[4,16,512]{2,1,0:T(8,128)(2,1)S(1)} %copy-done.11), channel_id=1, source_target_pairs={{0,4},{4,8},{8,12},{12,16},{16,20},{20,24},{24,28},{28,32},{32,36}... | collective-permute-start | bytes 196616 | tf_op jit(solution)/shard_map/ppermute | solution.py:285
  8.6 0.0 copy-start
  8.7 1.9 %copy-done = bf16[512,3072]{1,0:T(8,128)(2,1)S(1)} copy-done((bf16[512,3072]{1,0:T(8,128)(2,1)S(1)}, bf16[512,3072]{1,0:T(8,128)(2,1)}, u32[]{:S(2)}) %copy-start) | copy-done | bytes 3145752
  10.5 3.0 %prep.1 = (bf16[512,3072]{1,0:T(8,128)(2,1)S(1)}, bf16[3,512,512]{2,1,0:T(8,128)(2,1)S(1)}) custom-call(bf16[512,3072]{1,0:T(8,128)(2,1)S(1)} %copy-done, bf16[3,512,512]{2,1,0:T(8,128)(2,1)S(1)} %copy-done.7), custom_call_target="tpu_custom_call" | custom-call | flops 15728640 | bytes 10485760 | tf_op jit(solution)/shard_map/prep/pallas_call | solution.py:299
  13.6 0.0 collective-permute-done.1.prev_ref
  13.6 9.0 %first.1 = (bf16[6,512,512]{2,1,0:T(8,128)(2,1)S(1)}, f32[2,512,512]{2,1,0:T(8,128)S(1)}, f32[2,512,512]{2,1,0:T(8,128)S(1)}, f32[4,16,512]{2,1,0:T(8,128)S(1)},...) custom-call(s32[128]{0:T(128)S(1)} %copy-done.15, bf16[4,16,512]{2,1,0:T(8,128)(2,1)S(1)} %collective-permute-done.1.prev_ref, ...), custom_call_target="tpu_custom_call" | custom-call | flops 4294967296 | bytes 10485760 | tf_op jit(solution)/shard_map/first/pallas_call | solution.py:303
  22.6 0.0 copy-start.17
  22.7 1.7 %copy-done.17 = bf16[6,512,512]{2,1,0:T(8,128)(2,1)} copy-done((bf16[6,512,512]{2,1,0:T(8,128)(2,1)}, bf16[6,512,512]{2,1,0:T(8,128)(2,1)S(1)}, u32[]{:S(2)}) %copy-start.17) | copy-done | bytes 3145752
  24.3 1.9 %collective-permute-start.2 = (f32[2,16,512]{2,1,0:T(8,128)S(1)}, f32[2,16,512]{2,1,0:T(8,128)S(1)}, u32[]{:S(2)}, u32[]{:S(2)}) collective-permute-start(f32[2,16,512]{2,1,0:T(8,128)S(1)} %get-tuple-element.26), channel_id=1, source_target_pairs={{4,0},{8,4},{12,8},{16,12},{20,16},{24,20},{28,24},{32,28},{36,32}... | collective-permute-start | bytes 196616 | tf_op jit(solution)/shard_map/ppermute | solution.py:285
  26.2 3.7 %collective-permute-done.2.halo_ref = f32[2,16,512]{2,1,0:T(8,128)S(1)} collective-permute-done((f32[2,16,512]{2,1,0:T(8,128)S(1)}, f32[2,16,512]{2,1,0:T(8,128)S(1)}, u32[]{:S(2)}, u32[]{:S(2)}) %collective-permute-start.2) | collective-permute-done | bytes 65568 | tf_op jit(solution)/shard_map/ppermute | solution.py:285
  29.9 0.0 collective-permute-done.next_ref
  29.9 2.3 %second.1 = (bf16[64,512]{1,0:T(8,128)(2,1)S(1)}, bf16[16,16,128]{2,1,0:T(8,128)(2,1)S(1)}) custom-call(s32[128]{0:T(128)S(1)} %copy-done.15, bf16[2,512,512]{2,1,0:T(8,128)(2,1)S(1)} %collective-permute-done.next_ref, bf16[4,16,512]{2,1,0:T(8,128)(2,1)S(1)} %copy-done.11, bf16[3,16,512]{2,1,0:T(8,128)(2,1)S(1)} %bitcast.16, ...), custom_call_target="tpu_custom_call" | custom-call | flops 1610612736 | bytes 8388608 | tf_op jit(solution)/shard_map/second/pallas_call | solution.py:322
  32.2 9.3 %all_to_all.24.recv_ref = bf16[4,16,512]{2,1,0:T(8,128)(2,1)S(1)} all-to-all(bf16[4,16,512]{2,1,0:T(8,128)(2,1)S(1)} %bitcast.14), channel_id=1, replica_groups=mesh['tm'=32,'seq'=4] {'seq'}, dimensions={0} | all-to-all | bytes 131072 | tf_op jit(solution)/shard_map/all_to_all | solution.py:289
  41.5 1.6 %grad.1 = (bf16[128,16,128]{2,1,0:T(8,128)(2,1)}, bf16[64,512]{1,0:T(8,128)(2,1)S(1)}) custom-call(bf16[4,16,512]{2,1,0:T(8,128)(2,1)S(1)} %all_to_all.24.recv_ref, bf16[512,3072]{1,0:T(8,128)(2,1)S(1)} %get-tuple-element.29.normed_ref, bf16[16,16,128]{2,1,0:T(8,128)(2,1)S(1)} %get-tuple-element.30.icg_ref), custom_call_target="tpu_custom_call" | custom-call | flops 201326592 | bytes 5242880 | tf_op jit(solution)/shard_map/grad/pallas_call | solution.py:331
  43.1 0.6 copy-done.12
  43.7 11.2 %all-to-all-start.2 = ((bf16[128,16,128]{2,1,0:T(8,128)(2,1)}), bf16[128,16,128]{2,1,0:T(8,128)(2,1)S(1)}, u32[]{:S(2)}, u32[]{:S(2)}) async-start(bf16[128,16,128]{2,1,0:T(8,128)(2,1)} %get-tuple-element.33), calls=%async_computation.2 | async-start | bytes 1048576 | tf_op jit(solution)/shard_map/all_to_all | solution.py:289
  54.9 0.0 copy-start.18
  54.9 1.9 %copy-done.18 = bf16[6,512,512]{2,1,0:T(8,128)(2,1)S(1)} copy-done((bf16[6,512,512]{2,1,0:T(8,128)(2,1)S(1)}, bf16[6,512,512]{2,1,0:T(8,128)(2,1)}, u32[]{:S(2)}) %copy-start.18) | copy-done | bytes 3145752
  56.8 5.2 %weight.1 = bf16[64,2,48,128]{3,2,1,0:T(8,128)(2,1)S(1)} custom-call(s32[128]{0:T(128)S(1)} %copy-done.15, bf16[4,512,512]{2,1,0:T(8,128)(2,1)S(1)} %copy-done.8, bf16[6,512,512]{2,1,0:T(8,128)(2,1)S(1)} %copy-done.18), custom_call_target="tpu_custom_call" | custom-call | flops 3221225472 | bytes 7340032 | tf_op jit(solution)/shard_map/weight/pallas_call | solution.py:318
  62.0 0.0 copy-start.6
  62.0 1.1 copy-done.6
  63.1 5.8 %all-to-all-done.2.recv_ref = bf16[128,16,128]{2,1,0:T(8,128)(2,1)S(1)} async-done(((bf16[128,16,128]{2,1,0:T(8,128)(2,1)}), bf16[128,16,128]{2,1,0:T(8,128)(2,1)S(1)}, u32[]{:S(2)}, u32[]{:S(2)}) %all-to-all-start.2) | async-done | bytes 524320 | tf_op jit(solution)/shard_map/all_to_all | solution.py:289
  68.9 0.8 copy-done.2
  69.7 5.2 %all-to-all-start.1 = ((bf16[128,48,128]{2,1,0:T(8,128)(2,1)}), bf16[128,48,128]{2,1,0:T(8,128)(2,1)}, u32[]{:S(2)}, u32[]{:S(2)}) async-start(bf16[128,48,128]{2,1,0:T(8,128)(2,1)} %bitcast.13), calls=%async_computation.1 | async-start | bytes 3145728 | tf_op jit(solution)/shard_map/all_to_all | solution.py:289
  74.9 0.0 copy-start.3
  74.9 1.0 copy-done.3
  75.9 0.2 sum.1
  76.1 0.0 copy-start.4
  76.1 0.8 copy-done.4
  76.9 23.0 %all-to-all-done.1.recv_ref = bf16[128,48,128]{2,1,0:T(8,128)(2,1)} async-done(((bf16[128,48,128]{2,1,0:T(8,128)(2,1)}), bf16[128,48,128]{2,1,0:T(8,128)(2,1)}, u32[]{:S(2)}, u32[]{:S(2)}) %all-to-all-start.1) | async-done | bytes 1572896 | tf_op jit(solution)/shard_map/all_to_all | solution.py:289
  99.9 4.9 %all-to-all-start.3 = ((bf16[128,16,128]{2,1,0:T(8,128)(2,1)}), bf16[128,16,128]{2,1,0:T(8,128)(2,1)}, u32[]{:S(2)}, u32[]{:S(2)}) async-start(bf16[128,16,128]{2,1,0:T(8,128)(2,1)} %copy-done.4), calls=%async_computation.3 | async-start | bytes 1048576 | tf_op jit(solution)/shard_map/all_to_all | solution.py:289
  104.8 0.0 copy-done.1
  104.8 0.0 copy-done.5
  104.8 0.0 copy-start.9
  104.8 0.7 copy-done.9
  105.5 0.8 copy-done.13
  106.4 5.3 %hidden.1 = bf16[512,3072]{1,0:T(8,128)(2,1)} custom-call(bf16[64,512]{1,0:T(8,128)(2,1)S(1)} %copy-done.13, bf16[512,3072]{1,0:T(8,128)(2,1)S(1)} %copy-done.1, bf16[64,3072]{1,0:T(8,128)(2,1)S(1)} %bitcast.11, f32[2,3072]{1,0:T(2,128)S(1)} %copy-done.9), custom_call_target="tpu_custom_call" | custom-call | flops 201326592 | bytes 6291456 | tf_op jit(solution)/shard_map/hidden/pallas_call | solution.py:337
  111.7 2.3 %weight_sum.1 = f32[3,4,512]{2,1,0:T(4,128)} custom-call(bf16[128,48,128]{2,1,0:T(8,128)(2,1)} %all-to-all-done.1.recv_ref), custom_call_target="tpu_custom_call" | custom-call | flops 1048576 | bytes 1572864 | tf_op jit(solution)/shard_map/weight_sum/pallas_call | solution.py:355
  114.0 4.5 %all-to-all-done.3.all_ref = bf16[128,16,128]{2,1,0:T(8,128)(2,1)} async-done(((bf16[128,16,128]{2,1,0:T(8,128)(2,1)}), bf16[128,16,128]{2,1,0:T(8,128)(2,1)}, u32[]{:S(2)}, u32[]{:S(2)}) %all-to-all-start.3) | async-done | bytes 524320 | tf_op jit(solution)/shard_map/all_to_all | solution.py:289
  118.5 0.7 copy-done.10
  119.3 2.4 %last.1 = (f32[64,3072]{1,0:T(8,128)}, f32[2,3072]{1,0:T(2,128)}, f32[48,512]{1,0:T(8,128)}, f32[1,512]{1,0:T(1,128)}) custom-call(bf16[128,16,128]{2,1,0:T(8,128)(2,1)} %all-to-all-done.3.all_ref, bf16[64,3072]{1,0:T(8,128)(2,1)S(1)} %bitcast.12, f32[2,3072]{1,0:T(2,128)S(1)} %copy-done.10), custom_call_target="tpu_custom_call" | custom-call | flops 1048576 | bytes 2097152 | tf_op jit(solution)/shard_map/last/pallas_call | solution.py:358
  (13 shorter events, 0.0 us)
Async XLA Ops:
  0.6 4.8 %copy-start.11 = (bf16[4,16,512]{2,1,0:T(8,128)(2,1)S(1)}, bf16[4,16,512]{2,1,0:T(8,128)(2,1)}, u32[]{:S(2)}) copy-start(bf16[4,16,512]{2,1,0:T(8,128)(2,1)} %lat_ref.3) | copy-start | bytes 196612
  0.6 8.0 %copy-start.7 = (bf16[3,512,512]{2,1,0:T(8,128)(2,1)S(1)}, bf16[3,512,512]{2,1,0:T(8,128)(2,1)}, u32[]{:S(2)}) copy-start(bf16[3,512,512]{2,1,0:T(8,128)(2,1)} %conv_w_ref.1) | copy-start | bytes 4718596
  0.7 12.9 %copy-start.14 = (bf16[3,512,16]{1,2,0:T(8,128)(2,1)S(1)}, bf16[3,512,16]{1,2,0:T(8,128)(2,1)}, u32[]{:S(2)}) copy-start(bf16[3,512,16]{1,2,0:T(8,128)(2,1)} %param.12) | copy-start | bytes 147460
  0.7 12.9 %copy-start.15 = (s32[128]{0:T(128)S(1)}, s32[128]{0:T(128)}, u32[]{:S(2)}) copy-start(s32[128]{0:T(128)} %clip_ref.5) | copy-start | bytes 1540
  0.7 12.9 %copy-start.16 = (f32[512]{0:T(512)S(1)}, f32[512]{0:T(512)}, u32[]{:S(2)}) copy-start(f32[512]{0:T(512)} %param.13) | copy-start | bytes 6148
  2.1 27.8 %collective-permute-start = (bf16[2,512,512]{2,1,0:T(8,128)(2,1)S(1)}, bf16[2,512,512]{2,1,0:T(8,128)(2,1)S(1)}, u32[]{:S(2)}, u32[]{:S(2)}) collective-permute-start(bf16[2,512,512]{2,1,0:T(8,128)(2,1)S(1)} %slice.3), channel_id=1, source_target_pairs={{4,0},{8,4},{12,8},{16,12},{20,16},{24,20},{28,24},{32,28},{36,32}... | collective-permute-start | bytes 3145736 | tf_op jit(solution)/shard_map/ppermute | solution.py:285
  5.4 8.1 %collective-permute-start.1 = (bf16[4,16,512]{2,1,0:T(8,128)(2,1)S(1)}, bf16[4,16,512]{2,1,0:T(8,128)(2,1)S(1)}, u32[]{:S(2)}, u32[]{:S(2)}) collective-permute-start(bf16[4,16,512]{2,1,0:T(8,128)(2,1)S(1)} %copy-done.11), channel_id=1, source_target_pairs={{0,4},{4,8},{8,12},{12,16},{16,20},{20,24},{24,28},{28,32},{32,36}... | collective-permute-start | bytes 196616 | tf_op jit(solution)/shard_map/ppermute | solution.py:285
  8.6 1.9 %copy-start = (bf16[512,3072]{1,0:T(8,128)(2,1)S(1)}, bf16[512,3072]{1,0:T(8,128)(2,1)}, u32[]{:S(2)}) copy-start(bf16[512,3072]{1,0:T(8,128)(2,1)} %hidden_ref.3) | copy-start | bytes 9437188
  10.5 3.1 %copy-start.8 = (bf16[4,512,512]{2,1,0:T(8,128)(2,1)S(1)}, bf16[4,512,512]{2,1,0:T(8,128)(2,1)}, u32[]{:S(2)}) copy-start(bf16[4,512,512]{2,1,0:T(8,128)(2,1)} %grad_ref.3) | copy-start | bytes 6291460
  22.6 1.7 %copy-start.17 = (bf16[6,512,512]{2,1,0:T(8,128)(2,1)}, bf16[6,512,512]{2,1,0:T(8,128)(2,1)S(1)}, u32[]{:S(2)}) copy-start(bf16[6,512,512]{2,1,0:T(8,128)(2,1)S(1)} %get-tuple-element.32.act_ref) | copy-start | bytes 9437188
  24.3 5.6 %collective-permute-start.2 = (f32[2,16,512]{2,1,0:T(8,128)S(1)}, f32[2,16,512]{2,1,0:T(8,128)S(1)}, u32[]{:S(2)}, u32[]{:S(2)}) collective-permute-start(f32[2,16,512]{2,1,0:T(8,128)S(1)} %get-tuple-element.26), channel_id=1, source_target_pairs={{4,0},{8,4},{12,8},{16,12},{20,16},{24,20},{28,24},{32,28},{36,32}... | collective-permute-start | bytes 196616 | tf_op jit(solution)/shard_map/ppermute | solution.py:285
  43.1 0.6 copy-start.12
  43.7 25.2 %all-to-all-start.2 = ((bf16[128,16,128]{2,1,0:T(8,128)(2,1)}), bf16[128,16,128]{2,1,0:T(8,128)(2,1)S(1)}, u32[]{:S(2)}, u32[]{:S(2)}) async-start(bf16[128,16,128]{2,1,0:T(8,128)(2,1)} %get-tuple-element.33), calls=%async_computation.2 | async-start | bytes 1048576 | tf_op jit(solution)/shard_map/all_to_all | solution.py:289
  54.9 1.9 %copy-start.18 = (bf16[6,512,512]{2,1,0:T(8,128)(2,1)S(1)}, bf16[6,512,512]{2,1,0:T(8,128)(2,1)}, u32[]{:S(2)}) copy-start(bf16[6,512,512]{2,1,0:T(8,128)(2,1)} %copy-done.17) | copy-start | bytes 9437188
  62.0 1.1 copy-start.6
  68.9 0.8 copy-start.2
  69.7 35.1 %copy-start.1 = (bf16[512,3072]{1,0:T(8,128)(2,1)S(1)}, bf16[512,3072]{1,0:T(8,128)(2,1)}, u32[]{:S(2)}) copy-start(bf16[512,3072]{1,0:T(8,128)(2,1)} %hidden_ref.3) | copy-start | bytes 9437188
  69.7 30.2 %all-to-all-start.1 = ((bf16[128,48,128]{2,1,0:T(8,128)(2,1)}), bf16[128,48,128]{2,1,0:T(8,128)(2,1)}, u32[]{:S(2)}, u32[]{:S(2)}) async-start(bf16[128,48,128]{2,1,0:T(8,128)(2,1)} %bitcast.13), calls=%async_computation.1 | async-start | bytes 3145728 | tf_op jit(solution)/shard_map/all_to_all | solution.py:289
  74.9 1.0 copy-start.3
  75.9 28.9 %copy-start.5 = (bf16[3072,64]{0,1:T(8,128)(2,1)S(1)}, bf16[3072,64]{0,1:T(8,128)(2,1)}, u32[]{:S(2)}) copy-start(bf16[3072,64]{0,1:T(8,128)(2,1)} %param.15) | copy-start | bytes 1179652
  76.1 0.8 copy-start.4
  99.9 18.6 %all-to-all-start.3 = ((bf16[128,16,128]{2,1,0:T(8,128)(2,1)}), bf16[128,16,128]{2,1,0:T(8,128)(2,1)}, u32[]{:S(2)}, u32[]{:S(2)}) async-start(bf16[128,16,128]{2,1,0:T(8,128)(2,1)} %copy-done.4), calls=%async_computation.3 | async-start | bytes 1048576 | tf_op jit(solution)/shard_map/all_to_all | solution.py:289
  104.8 0.7 copy-start.9
  105.5 0.8 copy-start.13
  118.5 0.7 copy-start.10
where the time goes:
time: 122 us
  waiting for transfers between devices  37 us (30%)
  Pallas kernels  31.3 us (26%)
  starting transfers between devices  29.6 us (24%)
  local copies, waits for them, and re-layouts  13.6 us (11%)
  blocking collectives  9.3 us (8%)
    all_to_all x3, waiting for transfers between devices, exchange(): return lax.all_to_all(block, axes, split_axis=0, concat_axis=0, tiled=True)  33.3 us
    all_to_all x3, starting transfers between devices, exchange(): return lax.all_to_all(block, axes, split_axis=0, concat_axis=0, tiled=True)  21.2 us
    unnamed x38, local copies, waits for them, and re-layouts  12.2 us
    all_to_all x1, blocking collectives, exchange(): return lax.all_to_all(block, axes, split_axis=0, concat_axis=0, tiled=True)  9.3 us
    pallas_call x1, Pallas kernels, local(): call(k_first, (sds((SLAB + 2, C, PX), BF), sds((2, C, PX), F32), sds((2,...  9.01 us
    ppermute x3, starting transfers between devices, shifted(): return lax.ppermute(block, 'tm', route)  8.42 us
    pallas_call x1, Pallas kernels, local(): pl.pallas_call(k_hidden, grid=(4,), out_shape=sds((NTOK, D), BF), in_spec...  5.32 us
    pallas_call x1, Pallas kernels, local(): call(k_weight, sds((64, 2, 48, 128), BF), [SMEM] + [VMEM] * 2, [pltpu.VME...  5.15 us
  transfers between devices with their start and end apart: 6, of which 4 were waited for; matrix products, arithmetic and copies ran while one was open for 0% of the time, Pallas kernels for 21%

commit v1 on v0

--- a/solution.py
+++ b/solution.py
@@ -9,6 +9,7 @@
 F32 = jnp.float32
 VMEM = pl.BlockSpec(memory_space=pltpu.VMEM)
 SMEM = pl.BlockSpec(memory_space=pltpu.SMEM)
+HERE = pl.BlockSpec(memory_space=pl.ANY)
 EDGE = 4
 TAPS = 3
 SLAB = 4
@@ -44,7 +45,7 @@
     return jnp.maximum(frame - tap, clip_rel(clip_ref, first, frame))
 
 
-def k_prep(hidden_ref, conv_w_ref, normed_ref, conv_t_ref):
+def k_prep(hidden_ref, after_ref, normed_ref):
     gain = 1.0 / D
 
     def rows(i, _):
@@ -56,8 +57,35 @@
         return 0
 
     lax.fori_loop(0, NTOK // 64, rows, 0)
-    for k in range(TAPS):
-        conv_t_ref[k] = conv_w_ref[k].T
+
+
+def only(keep, value):
+    return jnp.where(keep, value, jnp.zeros_like(value))
+
+
+def k_back(clip_ref, grad_ref, conv_ref, acc_ref):
+    first = lax.axis_index("tm") * SLAB
+    start = [clip_rel(clip_ref, first, t) for t in range(SLAB)]
+    for s in range(SLAB):
+        total = mm(conv_ref[0], grad_ref[s], 0, 0)
+        for k in range(1, min(TAPS, SLAB - s)):
+            total = total + mm(conv_ref[k], only(start[s + k] <= s, grad_ref[s + k]), 0, 0)
+        acc_ref[s] = total
+
+    def opens(s, _):
+        @pl.when(clip_rel(clip_ref, first, s) == s)
+        def _():
+            later = jnp.minimum(s + 1, SLAB - 1)
+            keep = (s + 1 < SLAB) & (clip_rel(clip_ref, first, s + 1) <= s)
+            acc_ref[s] += (
+                mm(conv_ref[1], grad_ref[s], 0, 0)
+                + mm(conv_ref[2], grad_ref[s], 0, 0)
+                + mm(conv_ref[2], only(keep, grad_ref[later]), 0, 0)
+            )
+
+        return 0
+
+    lax.fori_loop(0, SLAB, opens, 0)
 
 
 def load_taps(clip_ref, first, lat_ref, z_ref, slot, frame, base):
@@ -67,9 +95,9 @@
 
 
 def k_first(
-    clip_ref, prev_ref, lat_ref, win_ref, bias_ref, grad_ref, conv_t_ref,
-    act_ref, slope_ref, acc_out_ref, part_ref, halo_ref, icg_ref,
-    all_ref, z_ref, wcat_ref, acc_ref, sl_ref, lacc_ref, icg_acc,
+    clip_ref, prev_ref, lat_ref, win_ref, bias_ref, acc_ref,
+    act_ref, slope_ref, part_ref, halo_ref, icg_ref,
+    all_ref, z_ref, wcat_ref, sl_ref, lacc_ref,
 ):
     first = lax.axis_index("tm") * SLAB
     all_ref[:SLAB] = prev_ref[...]
@@ -87,83 +115,84 @@
     tail = jnp.where(row == 2, low.astype(F32), tail)
     wcat_ref[TAPS * CL :, :] = tail.astype(BF)
     wcol = wcat_ref[...].T
-    acc_ref[...] = jnp.zeros_like(acc_ref)
     lacc_ref[...] = jnp.zeros_like(lacc_ref)
-    icg_acc[...] = jnp.zeros_like(icg_acc)
-
-    def pre_step(j, _):
+
+    def pre_of(j):
         load_taps(clip_ref, first, all_ref, z_ref, j, j - 2, SLAB)
         z_ref[j, TAPS * CL :, :] = jnp.ones((CL, PX), BF)
         pre = mm(wcol, z_ref[j], 1, 0)
         sig = 0.5 * jnp.tanh(0.5 * pre) + 0.5
         act_ref[j] = (pre * sig).astype(BF)
-        sl_ref[j] = sig * (1.0 + pre * (1.0 - sig))
+        return pre, sig
+
+    def before(j, _):
+        pre_of(j)
         return 0
 
-    lax.fori_loop(0, SLAB + 2, pre_step, 0)
-
-    def act_step(t, _):
-        for k in range(TAPS):
-            src = source(clip_ref, first, t, k)
-            src = jnp.where(src < 0, SLAB, src)
-            acc_ref[src] += mm(conv_t_ref[k], grad_ref[t], 1, 0)
+    def own(j, _):
+        pre, sig = pre_of(j)
+        sl_ref[j - 2] = sig * (1.0 + pre * (1.0 - sig))
         return 0
 
-    lax.fori_loop(0, SLAB, act_step, 0)
-
-    def pre_grad(t, _):
-        gp = (acc_ref[t] * sl_ref[t + 2]).astype(BF)
+    lax.fori_loop(0, 2, before, 0)
+    lax.fori_loop(2, SLAB + 2, own, 0)
+    icg = jnp.zeros((E, C), F32)
+    for t in range(2):
+        gp = (acc_ref[t] * sl_ref[t]).astype(BF)
         back = mm(wcat_ref[...], gp, 1, 0)
         for k in range(TAPS):
             src = source(clip_ref, first, t, k) + 2
             lacc_ref[src] += back[k * CL : (k + 1) * CL]
-        icg_acc[...] += mm(z_ref[t + 2], gp, 1, 1)
-        return 0
-
-    lax.fori_loop(0, 2, pre_grad, 0)
+        icg = icg + mm(z_ref[t + 2], gp, 1, 1)
     halo_ref[...] = lacc_ref[:2]
     part_ref[...] = lacc_ref[2:]
-    icg_ref[...] = icg_acc[...]
-    slope_ref[...] = sl_ref[SLAB:]
-    acc_out_ref[...] = acc_ref[2:SLAB]
-
-
-def k_weight(clip_ref, grad_ref, act_ref, out_ref, acc_ref):
+    icg_ref[...] = icg
+    slope_ref[...] = sl_ref[2:]
+
+
+def k_weight(clip_ref, grad_ref, act_ref, after_ref, keep_ref, send_ref, acc_ref):
     first = lax.axis_index("tm") * SLAB
-    acc_ref[...] = jnp.zeros_like(acc_ref)
-
-    def step(t, _):
-        for k in range(TAPS):
+    core = lax.axis_index("tm") % 2
+    for k in range(TAPS):
+        total = None
+        for t in range(SLAB):
             src = jnp.maximum(source(clip_ref, first, t, k), -2) + 2
-            acc_ref[:, k * C : (k + 1) * C] += mm(grad_ref[t], act_ref[src], 1, 1)
-        return 0
-
-    lax.fori_loop(0, SLAB, step, 0)
-    upper = lax.broadcasted_iota(jnp.int32, (64, 8, 128), 1) < 4
-    for jj in range(0, TAPS * C // 128, 4):
-        even, odd = [], []
-        for h in range(2):
-            at = (jj + 2 * h) * 128
-            a = acc_ref[:, at : at + 128].reshape(64, 8, 128)
-            b = acc_ref[:, at + 128 : at + 256].reshape(64, 8, 128)
-            even.append(jnp.where(upper, a, pltpu.roll(b, 4, 1)))
-            odd.append(jnp.where(upper, pltpu.roll(a, 4, 1), b))
-        out_ref[:, 0, jj * 4 : jj * 4 + 16, :] = jnp.concatenate(even, axis=1).astype(BF)
-        out_ref[:, 1, jj * 4 : jj * 4 + 16, :] = jnp.concatenate(odd, axis=1).astype(BF)
+            part = mm(grad_ref[t], act_ref[src], 1, 1)
+            total = part if total is None else total + part
+        acc_ref[:, :, :, k * C : (k + 1) * C] = total.reshape(16, 2, 16, C)
+    upper = lax.broadcasted_iota(jnp.int32, (32, 8, 128), 1) < 4
+    for ref, half in ((keep_ref, core), (send_ref, 1 - core)):
+        for jj in range(0, TAPS * C // 128, 4):
+            even, odd = [], []
+            for h in range(2):
+                at = (jj + 2 * h) * 128
+                a = acc_ref[:, half, :, at : at + 128].reshape(32, 8, 128)
+                b = acc_ref[:, half, :, at + 128 : at + 256].reshape(32, 8, 128)
+                even.append(jnp.where(upper, a, pltpu.roll(b, 4, 1)))
+                odd.append(jnp.where(upper, pltpu.roll(a, 4, 1), b))
+            ref[:, 0, jj * 4 : jj * 4 + 16, :] = jnp.concatenate(even, axis=1).astype(BF)
+            ref[:, 1, jj * 4 : jj * 4 + 16, :] = jnp.concatenate(odd, axis=1).astype(BF)
 
 
 def k_second(
-    clip_ref, next_ref, lat_ref, win_ref, conv_t_ref, acc_in_ref, slope_ref, part_ref, halo_ref, icg_in_ref,
+    clip_ref, next_ref, lat_ref, win_ref, conv_ref, acc_in_ref, slope_ref, part_ref, halo_ref, icg_in_ref, after_ref,
     tok_ref, icg_ref, acc_ref, z_ref, wcat_ref, lacc_ref, icg_acc, low_ref,
 ):
     first = lax.axis_index("tm") * SLAB
-    acc_ref[:2] = acc_in_ref[...]
+    start = [clip_rel(clip_ref, first, SLAB + t) for t in range(2)]
     for k in range(TAPS):
         wcat_ref[k * CL : (k + 1) * CL, :] = win_ref[k]
-    for t, k in ((0, 1), (0, 2), (1, 2)):
-        src = source(clip_ref, first, SLAB + t, k) - 2
-        acc_ref[jnp.minimum(src, 2)] += mm(conv_t_ref[k], next_ref[t], 1, 0)
-    lacc_ref[...] = jnp.zeros_like(lacc_ref)
+    acc_ref[0] = acc_in_ref[2] + mm(conv_ref[2], only(start[0] <= 2, next_ref[0]), 0, 0)
+    acc_ref[1] = (
+        acc_in_ref[3]
+        + mm(conv_ref[1], only(start[0] <= 3, next_ref[0]), 0, 0)
+        + mm(conv_ref[2], only(start[1] <= 3, next_ref[1]), 0, 0)
+    )
+
+    @pl.when((clip_rel(clip_ref, first, 3) == 3) & (start[0] <= 3))
+    def _():
+        acc_ref[1] += mm(conv_ref[2], next_ref[0], 0, 0)
+
     lacc_ref[:SLAB] = part_ref[...]
     lacc_ref[2:SLAB] += halo_ref[...]
     icg = icg_in_ref[...]
@@ -188,7 +217,7 @@
             icg_ref[rb * 4 + lb] = icg_acc[rb * 16 : (rb + 1) * 16, lb * 128 : (lb + 1) * 128].astype(BF)
 
 
-def k_grad(recv_ref, normed_ref, icg_ref, pack_ref, tok_ref, raw_ref, g_ref):
+def k_grad(recv_ref, normed_ref, icg_ref, keep_ref, other_ref, pack_ref, tok_ref, raw_ref):
     for s in range(4):
         for q in range(EDGE):
             raw_ref[q * CL : (q + 1) * CL, s * 128 : (s + 1) * 128] = recv_ref[
@@ -204,11 +233,17 @@
         g = mm(tok_ref[...], normed_ref[:, lb * 512 : (lb + 1) * 512], 1, 0).astype(BF)
         for u in range(4):
             for rb in range(4):
-                pack_ref[rb * 24 + lb * 4 + u] = g[rb * 16 : (rb + 1) * 16, u * 128 : (u + 1) * 128]
-    pack_ref[96:112] = icg_ref[...]
+                pack_ref[rb * 24 + lb * 4 + u, :16, :] = g[rb * 16 : (rb + 1) * 16, u * 128 : (u + 1) * 128]
+    pack_ref[96:112, :16, :] = icg_ref[...]
     for rb in range(4):
-        pack_ref[112 + rb] = total[rb * 16 : (rb + 1) * 16]
-    pack_ref[116:] = jnp.zeros((12, 16, 128), BF)
+        pack_ref[112 + rb, :16, :] = total[rb * 16 : (rb + 1) * 16]
+    pack_ref[116:, :16, :] = jnp.zeros((12, 16, 128), BF)
+    for xy in range(16):
+        for half in range(2):
+            at = pl.ds((xy * 2 + half) * 4, 4)
+            rows = slice(half * 24, half * 24 + 24)
+            both = keep_ref[xy * 4 : xy * 4 + 4].astype(F32) + other_ref[xy * 4 : xy * 4 + 4].astype(F32)
+            pack_ref[at, 16:, :] = both[:, rows, :].astype(BF)
 
 
 def k_hidden(tok_ref, hidden_ref, wt_ref, mod_ref, out_ref):
@@ -225,9 +260,16 @@
     out_ref[...] = (inv * (ng - m1 - normed * m2)).astype(BF)
 
 
-def k_sum(recv_ref, out_ref):
-    total = jnp.sum(recv_ref[...].astype(F32), axis=0).astype(BF)
+def k_sum(recv_ref, out_ref, keep_ref, send_ref):
+    core = lax.axis_index("tm") % 2
+    total = jnp.sum(recv_ref[:, :16, :].astype(F32), axis=0).astype(BF)
     out_ref[...] = jnp.broadcast_to(total[None], out_ref.shape)
+    sums = [jnp.zeros((24, 128), F32)] * 2
+    for d in range(128):
+        c = (d // 4) % 2
+        sums[c] = sums[c] + recv_ref[d, 16:, :].astype(F32)
+    keep_ref[...] = jnp.where(core == 0, sums[0], sums[1])
+    send_ref[...] = jnp.where(core == 0, sums[1], sums[0])
 
 
 def k_last(all_ref, wt_ref, mod_ref, final_ref, modg_ref, icg_ref, bias_ref):
@@ -254,12 +296,13 @@
         bias_ref[:, lb * 128 : (lb + 1) * 128] = all_ref[96 + 12 + lb].astype(F32)[0:1]
 
 
-def k_weight_sum(recv_ref, out_ref):
-    total = jnp.sum(recv_ref[...].astype(F32), axis=0)
-    for k in range(TAPS):
-        for u in range(4):
-            j = k * 4 + u
-            out_ref[k, :, u * 128 : (u + 1) * 128] = total[j * 4 : (j + 1) * 4]
+def k_weight_out(keep_ref, other_ref, out_ref):
+    core = lax.axis_index("tm") % 2
+    mine, other = keep_ref[...], other_ref[...]
+    halves = [jnp.where(core == 0, mine, other), jnp.where(core == 0, other, mine)]
+    for j in range(12):
+        rows = halves[j // 6][(j % 6) * 4 : (j % 6) * 4 + 4]
+        out_ref[j // 4, :, (j % 4) * 128 : (j % 4 + 1) * 128] = rows
 
 
 def call(fn, outs, specs, scratch=(), mib=40, est=None, name=None):
@@ -285,6 +328,10 @@
     return lax.ppermute(block, "tm", route)
 
 
+def swapped(block):
+    return lax.ppermute(block, "tm", [(i, i ^ 1) for i in range(lax.axis_size("tm"))])
+
+
 def exchange(block, axes):
     return lax.all_to_all(block, axes, split_axis=0, concat_axis=0, tiled=True)
 
@@ -296,43 +343,45 @@
     grad_next = shifted(grad_out[:2], -1)
     lat_prev = shifted(latents, 1)
     unit = 2 * C * C * PX
-    normed, conv_t = call(
-        k_prep, (sds((NTOK, D), BF), sds((TAPS, C, C), BF)), [VMEM] * 2,
-        est=cost(10 * NTOK * D, 10 << 20), name="prep",
-    )(hidden, conv_w)
-    act, slope, acc, part, halo, icg_part = call(
+    acc = call(
+        k_back, sds((SLAB, C, PX), F32), [SMEM, VMEM, VMEM], mib=16, est=cost(9 * unit, 8 << 20), name="back"
+    )(clip_start, grad_out, conv_w)
+    act, slope, part, halo, icg_part = call(
         k_first,
         (
-            sds((SLAB + 2, C, PX), BF), sds((2, C, PX), F32), sds((2, C, PX), F32),
+            sds((SLAB + 2, C, PX), BF), sds((2, C, PX), F32),
             sds((SLAB, CL, PX), F32), sds((2, CL, PX), F32), sds((E, C), F32),
         ),
-        [SMEM] + [VMEM] * 6,
+        [SMEM] + [VMEM] * 5,
         [
             pltpu.VMEM((2 * SLAB, CL, PX), BF), pltpu.VMEM((SLAB + 2, E, PX), BF), pltpu.VMEM((E, C), BF),
-            pltpu.VMEM((SLAB + 1, C, PX), F32), pltpu.VMEM((SLAB + 2, C, PX), F32),
-            pltpu.VMEM((SLAB + 2, CL, PX), F32), pltpu.VMEM((E, C), F32),
+            pltpu.VMEM((SLAB, C, PX), F32), pltpu.VMEM((SLAB + 2, CL, PX), F32),
         ],
-        est=cost(16 * unit, 10 << 20), name="first",
-    )(clip_start, lat_prev, latents, win, bias, grad_out, conv_t)
+        mib=24, est=cost(4 * unit, 10 << 20), name="first",
+    )(clip_start, lat_prev, latents, win, bias, acc)
     halo_recv = shifted(halo, -1)
-    weight_pack = call(
-        k_weight, sds((64, 2, 48, 128), BF), [SMEM] + [VMEM] * 2,
-        [pltpu.VMEM((C, TAPS * C), F32)], est=cost(12 * unit, 7 << 20), name="weight",
-    )(clip_start, grad_out, act)
+    normed = call(
+        k_prep, sds((NTOK, D), BF), [VMEM, HERE], mib=16, est=cost(10 * NTOK * D, 6 << 20), name="prep"
+    )(hidden, halo)
     tok_part, icg_blocks = call(
-        k_second, (sds((SLAB * CL, PX), BF), sds((16, 16, 128), BF)), [SMEM] + [VMEM] * 9,
+        k_second, (sds((SLAB * CL, PX), BF), sds((16, 16, 128), BF)), [SMEM] + [VMEM] * 9 + [HERE],
         [
-            pltpu.VMEM((3, C, PX), F32), pltpu.VMEM((2, E, PX), BF), pltpu.VMEM((TAPS * CL, C), BF),
+            pltpu.VMEM((2, C, PX), F32), pltpu.VMEM((2, E, PX), BF), pltpu.VMEM((TAPS * CL, C), BF),
             pltpu.VMEM((SLAB, CL, PX), F32), pltpu.VMEM((E, C), F32), pltpu.VMEM((SLAB * CL, PX), BF),
         ],
-        est=cost(6 * unit, 8 << 20), name="second",
-    )(clip_start, grad_next, latents, win, conv_t, acc, slope, part, halo_recv, icg_part)
+        mib=16, est=cost(6 * unit, 8 << 20), name="second",
+    )(clip_start, grad_next, latents, win, conv_w, acc, slope, part, halo_recv, icg_part, normed)
     tok_recv = exchange(tok_part, "seq").reshape(4, CL, PX)
+    keep, send = call(
+        k_weight, (sds((32, 2, 48, 128), BF),) * 2, [SMEM] + [VMEM] * 2 + [HERE],
+        [pltpu.VMEM((16, 2, 16, TAPS * C), F32)], mib=16, est=cost(12 * unit, 7 << 20), name="weight",
+    )(clip_start, grad_out, act, icg_blocks)
+    other = swapped(send)
     pack, tok = call(
-        k_grad, (sds((128, 16, 128), BF), sds((E, NTOK), BF)), [VMEM] * 3,
-        [pltpu.VMEM((E, NTOK), BF), pltpu.VMEM((E, D), F32)],
-        est=cost(2 * NTOK * D * E, 5 << 20), name="grad",
-    )(tok_recv, normed, icg_blocks)
+        k_grad, (sds((128, 40, 128), BF), sds((E, NTOK), BF)), [VMEM] * 5,
+        [pltpu.VMEM((E, NTOK), BF)],
+        mib=16, est=cost(2 * NTOK * D * E, 5 << 20), name="grad",
+    )(tok_recv, normed, icg_blocks, keep.reshape(64, 48, 128), other.reshape(64, 48, 128))
     recv = exchange(pack, BOTH)
     hidden_grad = pl.pallas_call(
         k_hidden,
@@ -345,19 +394,21 @@
             pl.BlockSpec((2, D), lambda i: (0, 0)),
         ],
         out_specs=pl.BlockSpec((128, D), lambda i: (i, 0)),
-        compiler_params=params(40),
+        compiler_params=params(16),
         cost_estimate=cost(2 * NTOK * D * E, 6 << 20),
         name="hidden",
     )(tok, hidden, wt, modulation)
-    weight_recv = exchange(weight_pack.reshape(128, 48, 128), BOTH)
-    copies = call(k_sum, sds((128, 16, 128), BF), [VMEM], est=cost(1 << 18, 1 << 20), name="sum")(recv)
+    copies, own, away = call(
+        k_sum, (sds((128, 16, 128), BF), sds((24, 128), F32), sds((24, 128), F32)), [VMEM],
+        mib=16, est=cost(1 << 20, 2 << 20), name="sum",
+    )(recv)
     everything = exchange(copies, BOTH)
     weight_grad = call(
-        k_weight_sum, sds((TAPS, 4, C), F32), [VMEM], est=cost(1 << 20, 1536 << 10), name="weight_sum"
-    )(weight_recv)
+        k_weight_out, sds((TAPS, 4, C), F32), [VMEM] * 2, mib=16, est=cost(1 << 12, 1 << 16), name="weight_out"
+    )(own, swapped(away))
     final_t, mod_grad, icg, bias_grad = call(
         k_last, (sds((E, D), F32), sds((2, D), F32), sds((TAPS * CL, C), F32), sds((1, C), F32)), [VMEM] * 3,
-        est=cost(1 << 20, 2 << 20), name="last",
+        mib=16, est=cost(1 << 20, 2 << 20), name="last",
     )(everything, wt, modulation)
     return (
         hidden_grad,

time: 122 us -> 102 us (0.84)
  blocking collectives: 9.3 us -> 44.5 us
  waiting for transfers between devices: 37 us -> 5.73 us
  starting transfers between devices: 29.6 us -> 15.1 us
  local copies, waits for them, and re-layouts: 13.6 us -> 8.74 us
  Pallas kernels: 31.3 us -> 26.5 us
    all_to_all x1 -> x2, blocking collectives: 9.3 us -> 44.5 us  [exchange(): return lax.all_to_all(block, axes, split_axis=0, concat_axis=0, tiled=True)]
    all_to_all x3 -> x1, waiting for transfers between devices: 33.3 us -> 4.89 us  [exchange(): return lax.all_to_all(block, axes, split_axis=0, concat_axis=0, tiled=True)]
    all_to_all x3 -> x1, starting transfers between devices: 21.2 us -> 4.86 us  [exchange(): return lax.all_to_all(block, axes, split_axis=0, concat_axis=0, tiled=True)]
    pallas_call x6 -> x7, Pallas kernels: 21.3 us -> 16.4 us  [the longest x1 4.68 us: local(): call(k_weight, (sds((32, 2, 48, 128), BF),) * 2, [SMEM] + [VMEM] * 2 + [H...]
    unnamed x38 -> x34, local copies, waits for them, and re-layouts: 12.2 us -> 7.4 us
    ppermute x3, waiting for transfers between devices: 3.66 us -> 0.83 us  [shifted(): return lax.ppermute(block, 'tm', route)]
    ppermute x0 -> x2, starting transfers between devices: none -> 1.44 us  [swapped(): lax.ppermute(block, 'tm', [(i, i ^ 1) for i in range(lax.axis_size('tm'))])]
  transfers between devices with their start and end apart: 6 -> 6, of which waited for: 4 -> 2; matrix products, arithmetic and copies ran while one was open for 0% -> 0% of each run, Pallas kernels for 21% -> 16%
where the time goes in v1:
time: 102 us; the launch traced here: 101 us
  blocking collectives  44.5 us (44%)
  Pallas kernels  26.5 us (26%)
  starting transfers between devices  15.1 us (15%)
  local copies, waits for them, and re-layouts  8.74 us (9%)
  waiting for transfers between devices  5.73 us (6%)
    all_to_all x2, blocking collectives, exchange(): return lax.all_to_all(block, axes, split_axis=0, concat_axis=0, tiled=True)  44.5 us
    ppermute x3, starting transfers between devices, shifted(): return lax.ppermute(block, 'tm', route)  8.79 us
    unnamed x34, local copies, waits for them, and re-layouts  7.4 us
    pallas_call x1, Pallas kernels, local(): pl.pallas_call(k_hidden, grid=(4,), out_shape=sds((NTOK, D), BF), in_spec...  5.32 us
    all_to_all x1, waiting for transfers between devices, exchange(): return lax.all_to_all(block, axes, split_axis=0, concat_axis=0, tiled=True)  4.89 us
    all_to_all x1, starting transfers between devices, exchange(): return lax.all_to_all(block, axes, split_axis=0, concat_axis=0, tiled=True)  4.86 us
    pallas_call x1, Pallas kernels, local(): call(k_weight, (sds((32, 2, 48, 128), BF),) * 2, [SMEM] + [VMEM] * 2 + [H...  4.68 us
    pallas_call x1, Pallas kernels, local(): call(k_first, (sds((SLAB + 2, C, PX), BF), sds((2, C, PX), F32), sds((SLA...  4.18 us
  transfers between devices with their start and end apart: 6, of which 2 were waited for; matrix products, arithmetic and copies ran while one was open for 0% of the time, Pallas kernels for 16%

profile of v1, /device:TPU:1, one launch (start us, length us, event | category | flops | bytes accessed | tf_op | source)
XLA Modules:
  0.0 101.5 jit_solution(18193263585282896222)
XLA Ops:
  0.6 0.0 copy-start.7
  0.6 0.0 copy-start.8
  0.7 0.0 copy-start.13
  0.7 0.0 copy-start.15
  0.7 1.3 %slice.3 = bf16[2,512,512]{2,1,0:T(8,128)(2,1)S(1)} slice(bf16[4,512,512]{2,1,0:T(8,128)(2,1)} %grad_ref.3), slice={[0:2], [0:512], [0:512]} | slice | bytes 2097152 | tf_op jit(solution)/shard_map/slice | solution.py:343
  2.0 3.3 %collective-permute-start = (bf16[2,512,512]{2,1,0:T(8,128)(2,1)S(1)}, bf16[2,512,512]{2,1,0:T(8,128)(2,1)S(1)}, u32[]{:S(2)}, u32[]{:S(2)}) collective-permute-start(bf16[2,512,512]{2,1,0:T(8,128)(2,1)S(1)} %slice.3), channel_id=1, source_target_pairs={{4,0},{8,4},{12,8},{16,12},{20,16},{24,20},{28,24},{32,28},{36,32}... | collective-permute-start | bytes 3145736 | tf_op jit(solution)/shard_map/ppermute | solution.py:328
  5.4 3.2 %collective-permute-start.1 = (bf16[4,16,512]{2,1,0:T(8,128)(2,1)}, bf16[4,16,512]{2,1,0:T(8,128)(2,1)S(1)}, u32[]{:S(2)}, u32[]{:S(2)}) collective-permute-start(bf16[4,16,512]{2,1,0:T(8,128)(2,1)} %lat_ref.3), channel_id=1, source_target_pairs={{0,4},{4,8},{8,12},{12,16},{16,20},{20,24},{24,28},{28,32},{32,36}... | collective-permute-start | bytes 196616 | tf_op jit(solution)/shard_map/ppermute | solution.py:328
  8.5 0.0 copy-start.1
  8.6 1.4 %copy-done.1 = bf16[3,512,512]{2,1,0:T(8,128)(2,1)S(1)} copy-done((bf16[3,512,512]{2,1,0:T(8,128)(2,1)S(1)}, bf16[3,512,512]{2,1,0:T(8,128)(2,1)}, u32[]{:S(2)}) %copy-start.1) | copy-done | bytes 1572888
  10.0 1.6 %copy-done.4 = bf16[4,512,512]{2,1,0:T(8,128)(2,1)S(1)} copy-done((bf16[4,512,512]{2,1,0:T(8,128)(2,1)S(1)}, bf16[4,512,512]{2,1,0:T(8,128)(2,1)}, u32[]{:S(2)}) %copy-start.4) | copy-done | bytes 2097176
  11.6 0.7 copy-done.14
  12.2 3.2 %back.1.acc_ref.acc_in_ref = f32[4,512,512]{2,1,0:T(8,128)S(1)} custom-call(s32[128]{0:T(128)S(1)} %copy-done.14, bf16[4,512,512]{2,1,0:T(8,128)(2,1)S(1)} %copy-done.4, bf16[3,512,512]{2,1,0:T(8,128)(2,1)S(1)} %copy-done.1), custom_call_target="tpu_custom_call" | custom-call | flops 2415919104 | bytes 8388608 | tf_op jit(solution)/shard_map/back/pallas_call | solution.py:346
  15.5 0.0 copy-start
  15.5 0.0 collective-permute-done.1.prev_ref
  15.5 0.0 copy-done.7
  15.5 0.0 copy-done.8
  15.5 4.2 %first.1 = (bf16[6,512,512]{2,1,0:T(8,128)(2,1)S(1)}, f32[2,512,512]{2,1,0:T(8,128)S(1)}, f32[4,16,512]{2,1,0:T(8,128)S(1)}, f32[2,16,512]{2,1,0:T(8,128)S(1)}, f32[64,512]{1,0:T(8,128)S(1)}) custom-call(s32[128]{0:T(128)S(1)} %copy-done.15, bf16[4,16,512]{2,1,0:T(8,128)(2,1)S(1)} %collective-permute-done.1.prev_ref, bf16[4,16,512]{2,1,0:T(8,128)(2,1)S(1)} %copy-done.7, ...), custom_call_target="tpu_custom_call" | custom-call | flops 1073741824 | bytes 10485760 | tf_op jit(solution)/shard_map/first/pallas_call | solution.py:349
  19.7 0.0 copy-start.2
  19.7 2.3 %collective-permute-start.2 = (f32[2,16,512]{2,1,0:T(8,128)S(1)}, f32[2,16,512]{2,1,0:T(8,128)S(1)}, u32[]{:S(2)}, u32[]{:S(2)}) collective-permute-start(f32[2,16,512]{2,1,0:T(8,128)S(1)} %get-tuple-element.26.after_ref), channel_id=1, source_target_pairs={{4,0},{8,4},{12,8},{16,12},{20,16},{24,20},{28,24},{32,28},{36,32}... | collective-permute-start | bytes 196616 | tf_op jit(solution)/shard_map/ppermute | solution.py:328
  22.0 0.0 copy-done
  22.0 2.6 %prep.1.after_ref.normed_ref = bf16[512,3072]{1,0:T(8,128)(2,1)S(1)} custom-call(bf16[512,3072]{1,0:T(8,128)(2,1)S(1)} %copy-done, f32[2,16,512]{2,1,0:T(8,128)S(1)} %get-tuple-element.26.after_ref), custom_call_target="tpu_custom_call" | custom-call | flops 15728640 | bytes 6291456 | tf_op jit(solution)/shard_map/prep/pallas_call | solution.py:363
  24.6 0.8 collective-permute-done.2.halo_ref
  25.4 0.0 collective-permute-done.next_ref
  25.4 2.4 %second.1 = (bf16[64,512]{1,0:T(8,128)(2,1)S(1)}, bf16[16,16,128]{2,1,0:T(8,128)(2,1)S(1)}) custom-call(s32[128]{0:T(128)S(1)} %copy-done.15, bf16[2,512,512]{2,1,0:T(8,128)(2,1)S(1)} %collective-permute-done.next_ref, bf16[4,16,512]{2,1,0:T(8,128)(2,1)S(1)} %copy-done.7, bf16[3,16,512]{2,1,0:T(8,128)(2,1)S(1)} %bitcast.17, ...), custom_call_target="tpu_custom_call" | custom-call | flops 1610612736 | bytes 8388608 | tf_op jit(solution)/shard_map/second/pallas_call | solution.py:366
  27.9 0.0 copy-done.5
  27.9 4.7 %weight.1 = (bf16[32,2,48,128]{3,2,1,0:T(8,128)(2,1)S(1)}, bf16[32,2,48,128]{3,2,1,0:T(8,128)(2,1)S(1)}) custom-call(s32[128]{0:T(128)S(1)} %copy-done.15, bf16[4,512,512]{2,1,0:T(8,128)(2,1)S(1)} %copy-done.5, bf16[6,512,512]{2,1,0:T(8,128)(2,1)S(1)} %get-tuple-element.30.act_ref, bf16[16,16,128]{2,1,0:T(8,128)(2,1)S(1)} %get-tuple-element.29.after_ref.icg_ref), custom_call_target="tpu_custom_call" | custom-call | flops 3221225472 | bytes 7340032 | tf_op jit(solution)/shard_map/weight/pallas_call | solution.py:375
  32.6 0.1 collective-permute-start.3
  32.7 9.3 %all_to_all.19.recv_ref = bf16[4,16,512]{2,1,0:T(8,128)(2,1)S(1)} all-to-all(bf16[4,16,512]{2,1,0:T(8,128)(2,1)S(1)} %bitcast.18), channel_id=1, replica_groups=mesh['tm'=32,'seq'=4] {'seq'}, dimensions={0} | all-to-all | bytes 131072 | tf_op jit(solution)/shard_map/all_to_all | solution.py:336
  42.0 0.0 collective-permute-done.3
  42.0 0.9 grad.1
  42.9 0.0 copy-start.11
  42.9 0.0 copy-start.3
  42.9 35.2 %all_to_all.20.recv_ref = bf16[128,40,128]{2,1,0:T(8,128)(2,1)S(1)} all-to-all(bf16[128,40,128]{2,1,0:T(8,128)(2,1)S(1)} %get-tuple-element.34), channel_id=1, replica_groups=mesh['tm'=32,'seq'=4] {'tm','seq'}, dimensions={0} | all-to-all | bytes 2621440 | tf_op jit(solution)/shard_map/all_to_all | solution.py:336
  78.1 0.2 sum.1
  78.3 0.0 copy-start.6
  78.3 0.8 copy-done.6
  79.1 0.6 copy-done.16
  79.7 4.9 %all-to-all-start.2 = ((bf16[128,16,128]{2,1,0:T(8,128)(2,1)}), bf16[128,16,128]{2,1,0:T(8,128)(2,1)}, u32[]{:S(2)}, u32[]{:S(2)}) async-start(bf16[128,16,128]{2,1,0:T(8,128)(2,1)} %copy-done.6), calls=%async_computation.2 | async-start | bytes 1048576 | tf_op jit(solution)/shard_map/all_to_all | solution.py:336
  84.6 1.4 %collective-permute-start.4 = (f32[24,128]{1,0:T(8,128)}, f32[24,128]{1,0:T(8,128)S(1)}, u32[]{:S(2)}, u32[]{:S(2)}) collective-permute-start(f32[24,128]{1,0:T(8,128)} %copy-done.16), channel_id=1, source_target_pairs={{0,4},{4,0},{8,12},{12,8},{16,20},{20,16},{24,28},{28,24},{32,36},... | collective-permute-start | bytes 36872 | tf_op jit(solution)/shard_map/ppermute | solution.py:332
  86.0 0.0 copy-done.3
  86.0 0.7 copy-done.9
  86.7 0.8 copy-done.12
  87.5 5.3 %hidden.1 = bf16[512,3072]{1,0:T(8,128)(2,1)} custom-call(bf16[64,512]{1,0:T(8,128)(2,1)S(1)} %copy-done.12, bf16[512,3072]{1,0:T(8,128)(2,1)S(1)} %copy-done, bf16[64,3072]{1,0:T(8,128)(2,1)S(1)} %bitcast.12, f32[2,3072]{1,0:T(2,128)S(1)} %copy-done.9), custom_call_target="tpu_custom_call" | custom-call | flops 201326592 | bytes 6291456 | tf_op jit(solution)/shard_map/hidden/pallas_call | solution.py:386
  92.9 0.0 collective-permute-done.4.other_ref
  92.9 0.6 weight_out.1
  93.5 4.9 %all-to-all-done.2.all_ref = bf16[128,16,128]{2,1,0:T(8,128)(2,1)} async-done(((bf16[128,16,128]{2,1,0:T(8,128)(2,1)}), bf16[128,16,128]{2,1,0:T(8,128)(2,1)}, u32[]{:S(2)}, u32[]{:S(2)}) %all-to-all-start.2) | async-done | bytes 524320 | tf_op jit(solution)/shard_map/all_to_all | solution.py:336
  98.4 0.7 copy-done.10
  99.1 2.4 %last.1 = (f32[64,3072]{1,0:T(8,128)}, f32[2,3072]{1,0:T(2,128)}, f32[48,512]{1,0:T(8,128)}, f32[1,512]{1,0:T(1,128)}) custom-call(bf16[128,16,128]{2,1,0:T(8,128)(2,1)} %all-to-all-done.2.all_ref, bf16[64,3072]{1,0:T(8,128)(2,1)S(1)} %bitcast.13, f32[2,3072]{1,0:T(2,128)S(1)} %copy-done.10), custom_call_target="tpu_custom_call" | custom-call | flops 1048576 | bytes 2097152 | tf_op jit(solution)/shard_map/last/pallas_call | solution.py:409
  (11 shorter events, 0.0 us)
Async XLA Ops:
  0.6 14.8 %copy-start.7 = (bf16[4,16,512]{2,1,0:T(8,128)(2,1)S(1)}, bf16[4,16,512]{2,1,0:T(8,128)(2,1)}, u32[]{:S(2)}) copy-start(bf16[4,16,512]{2,1,0:T(8,128)(2,1)} %lat_ref.3) | copy-start | bytes 196612
  0.6 14.8 %copy-start.8 = (bf16[3,512,16]{1,2,0:T(8,128)(2,1)S(1)}, bf16[3,512,16]{1,2,0:T(8,128)(2,1)}, u32[]{:S(2)}) copy-start(bf16[3,512,16]{1,2,0:T(8,128)(2,1)} %param.12) | copy-start | bytes 147460
  0.7 14.8 %copy-start.13 = (f32[512]{0:T(512)S(1)}, f32[512]{0:T(512)}, u32[]{:S(2)}) copy-start(f32[512]{0:T(512)} %param.13) | copy-start | bytes 6148
  0.7 14.8 %copy-start.15 = (s32[128]{0:T(128)S(1)}, s32[128]{0:T(128)}, u32[]{:S(2)}) copy-start(s32[128]{0:T(128)} %clip_ref.7) | copy-start | bytes 1540
  2.0 23.4 %collective-permute-start = (bf16[2,512,512]{2,1,0:T(8,128)(2,1)S(1)}, bf16[2,512,512]{2,1,0:T(8,128)(2,1)S(1)}, u32[]{:S(2)}, u32[]{:S(2)}) collective-permute-start(bf16[2,512,512]{2,1,0:T(8,128)(2,1)S(1)} %slice.3), channel_id=1, source_target_pairs={{4,0},{8,4},{12,8},{16,12},{20,16},{24,20},{28,24},{32,28},{36,32}... | collective-permute-start | bytes 3145736 | tf_op jit(solution)/shard_map/ppermute | solution.py:328
  5.4 10.1 %collective-permute-start.1 = (bf16[4,16,512]{2,1,0:T(8,128)(2,1)}, bf16[4,16,512]{2,1,0:T(8,128)(2,1)S(1)}, u32[]{:S(2)}, u32[]{:S(2)}) collective-permute-start(bf16[4,16,512]{2,1,0:T(8,128)(2,1)} %lat_ref.3), channel_id=1, source_target_pairs={{0,4},{4,8},{8,12},{12,16},{16,20},{20,24},{24,28},{28,32},{32,36}... | collective-permute-start | bytes 196616 | tf_op jit(solution)/shard_map/ppermute | solution.py:328
  8.5 1.4 %copy-start.1 = (bf16[3,512,512]{2,1,0:T(8,128)(2,1)S(1)}, bf16[3,512,512]{2,1,0:T(8,128)(2,1)}, u32[]{:S(2)}) copy-start(bf16[3,512,512]{2,1,0:T(8,128)(2,1)} %conv_ref.3) | copy-start | bytes 4718596
  10.0 1.6 %copy-start.4 = (bf16[4,512,512]{2,1,0:T(8,128)(2,1)S(1)}, bf16[4,512,512]{2,1,0:T(8,128)(2,1)}, u32[]{:S(2)}) copy-start(bf16[4,512,512]{2,1,0:T(8,128)(2,1)} %grad_ref.3) | copy-start | bytes 6291460
  11.6 0.7 copy-start.14
  15.5 6.6 %copy-start = (bf16[512,3072]{1,0:T(8,128)(2,1)S(1)}, bf16[512,3072]{1,0:T(8,128)(2,1)}, u32[]{:S(2)}) copy-start(bf16[512,3072]{1,0:T(8,128)(2,1)} %hidden_ref.3) | copy-start | bytes 9437188
  19.7 5.7 %copy-start.2 = (bf16[3,512,512]{2,1,0:T(8,128)(2,1)S(1)}, bf16[3,512,512]{2,1,0:T(8,128)(2,1)}, u32[]{:S(2)}) copy-start(bf16[3,512,512]{2,1,0:T(8,128)(2,1)} %conv_ref.3) | copy-start | bytes 4718596
  19.7 5.7 %collective-permute-start.2 = (f32[2,16,512]{2,1,0:T(8,128)S(1)}, f32[2,16,512]{2,1,0:T(8,128)S(1)}, u32[]{:S(2)}, u32[]{:S(2)}) collective-permute-start(f32[2,16,512]{2,1,0:T(8,128)S(1)} %get-tuple-element.26.after_ref), channel_id=1, source_target_pairs={{4,0},{8,4},{12,8},{16,12},{20,16},{24,20},{28,24},{32,28},{36,32}... | collective-permute-start | bytes 196616 | tf_op jit(solution)/shard_map/ppermute | solution.py:328
  25.4 2.5 %copy-start.5 = (bf16[4,512,512]{2,1,0:T(8,128)(2,1)S(1)}, bf16[4,512,512]{2,1,0:T(8,128)(2,1)}, u32[]{:S(2)}) copy-start(bf16[4,512,512]{2,1,0:T(8,128)(2,1)} %grad_ref.3) | copy-start | bytes 6291460
  32.6 9.4 %collective-permute-start.3 = (bf16[32,2,48,128]{3,2,1,0:T(8,128)(2,1)S(1)}, bf16[32,2,48,128]{3,2,1,0:T(8,128)(2,1)S(1)}, u32[]{:S(2)}, u32[]{:S(2)}) collective-permute-start(bf16[32,2,48,128]{3,2,1,0:T(8,128)(2,1)S(1)} %get-tuple-element.32), channel_id=1, source_target_pairs={{0,4},{4,0},{8,12},{12,8},{16,20},{20,16},{24,28},{28,24},{32,36},... | collective-permute-start | bytes 2359304 | tf_op jit(solution)/shard_map/ppermute | solution.py:332
  42.9 35.4 %copy-start.11 = (bf16[64,512]{1,0:T(8,128)(2,1)}, bf16[64,512]{1,0:T(8,128)(2,1)S(1)}, u32[]{:S(2)}) copy-start(bf16[64,512]{1,0:T(8,128)(2,1)S(1)} %get-tuple-element.33.tok_ref) | copy-start | bytes 196612
  42.9 43.1 %copy-start.3 = (bf16[3072,64]{0,1:T(8,128)(2,1)S(1)}, bf16[3072,64]{0,1:T(8,128)(2,1)}, u32[]{:S(2)}) copy-start(bf16[3072,64]{0,1:T(8,128)(2,1)} %param.15) | copy-start | bytes 1179652
  78.3 0.8 copy-start.6
  79.1 0.6 copy-start.16
  79.7 18.6 %all-to-all-start.2 = ((bf16[128,16,128]{2,1,0:T(8,128)(2,1)}), bf16[128,16,128]{2,1,0:T(8,128)(2,1)}, u32[]{:S(2)}, u32[]{:S(2)}) async-start(bf16[128,16,128]{2,1,0:T(8,128)(2,1)} %copy-done.6), calls=%async_computation.2 | async-start | bytes 1048576 | tf_op jit(solution)/shard_map/all_to_all | solution.py:336
  84.6 8.3 %collective-permute-start.4 = (f32[24,128]{1,0:T(8,128)}, f32[24,128]{1,0:T(8,128)S(1)}, u32[]{:S(2)}, u32[]{:S(2)}) collective-permute-start(f32[24,128]{1,0:T(8,128)} %copy-done.16), channel_id=1, source_target_pairs={{0,4},{4,0},{8,12},{12,8},{16,20},{20,16},{24,28},{28,24},{32,36},... | collective-permute-start | bytes 36872 | tf_op jit(solution)/shard_map/ppermute | solution.py:332
  86.0 0.7 copy-start.9
  86.7 0.8 copy-start.12
  98.4 0.7 copy-start.10

commit v2 on v1

--- a/solution.py
+++ b/solution.py
@@ -10,6 +10,7 @@
 VMEM = pl.BlockSpec(memory_space=pltpu.VMEM)
 SMEM = pl.BlockSpec(memory_space=pltpu.SMEM)
 HERE = pl.BlockSpec(memory_space=pl.ANY)
+PIN = pl.BlockSpec(memory_space=pltpu.HBM)
 EDGE = 4
 TAPS = 3
 SLAB = 4
@@ -63,8 +64,18 @@
     return jnp.where(keep, value, jnp.zeros_like(value))
 
 
-def k_back(clip_ref, grad_ref, conv_ref, acc_ref):
+def k_back(clip_hbm, conv_hbm, sent_ref, grad_hbm, acc_ref, clip_ref, conv_ref, grad_ref, sems):
+    copies = [
+        pltpu.make_async_copy(clip_hbm, clip_ref, sems.at[0]),
+        pltpu.make_async_copy(conv_hbm, conv_ref, sems.at[1]),
+        pltpu.make_async_copy(grad_hbm.at[pl.ds(2, 2)], grad_ref.at[pl.ds(2, 2)], sems.at[2]),
+    ]
+    for copy in copies:
+        copy.start()
+    grad_ref[:2] = sent_ref[...]
     first = lax.axis_index("tm") * SLAB
+    for copy in copies:
+        copy.wait()
     start = [clip_rel(clip_ref, first, t) for t in range(SLAB)]
     for s in range(SLAB):
         total = mm(conv_ref[0], grad_ref[s], 0, 0)
@@ -94,14 +105,7 @@
         z_ref[slot, k * CL : (k + 1) * CL, :] = lat_ref[src]
 
 
-def k_first(
-    clip_ref, prev_ref, lat_ref, win_ref, bias_ref, acc_ref,
-    act_ref, slope_ref, part_ref, halo_ref, icg_ref,
-    all_ref, z_ref, wcat_ref, sl_ref, lacc_ref,
-):
-    first = lax.axis_index("tm") * SLAB
-    all_ref[:SLAB] = prev_ref[...]
-    all_ref[SLAB:] = lat_ref[...]
+def set_weights(win_ref, bias_ref, wcat_ref):
     for k in range(TAPS):
         wcat_ref[k * CL : (k + 1) * CL, :] = win_ref[k]
     bias = bias_ref[...]
@@ -114,43 +118,68 @@
     tail = jnp.where(row == 1, mid.astype(F32), tail)
     tail = jnp.where(row == 2, low.astype(F32), tail)
     wcat_ref[TAPS * CL :, :] = tail.astype(BF)
+
+
+def pre_of(clip_ref, first, all_ref, z_ref, wcol, slot, frame):
+    load_taps(clip_ref, first, all_ref, z_ref, slot, frame, SLAB)
+    z_ref[slot, TAPS * CL :, :] = jnp.ones((CL, PX), BF)
+    pre = mm(wcol, z_ref[slot], 1, 0)
+    return pre, 0.5 * jnp.tanh(0.5 * pre) + 0.5
+
+
+def k_first(
+    clip_ref, prev_ref, lat_ref, win_ref, bias_ref, acc_ref,
+    act_ref, part_ref, halo_ref, icg_ref,
+    all_ref, z_ref, wcat_ref, lacc_ref,
+):
+    first = lax.axis_index("tm") * SLAB
+    all_ref[:SLAB] = prev_ref[...]
+    all_ref[SLAB:] = lat_ref[...]
+    set_weights(win_ref, bias_ref, wcat_ref)
     wcol = wcat_ref[...].T
     lacc_ref[...] = jnp.zeros_like(lacc_ref)
-
-    def pre_of(j):
-        load_taps(clip_ref, first, all_ref, z_ref, j, j - 2, SLAB)
-        z_ref[j, TAPS * CL :, :] = jnp.ones((CL, PX), BF)
-        pre = mm(wcol, z_ref[j], 1, 0)
-        sig = 0.5 * jnp.tanh(0.5 * pre) + 0.5
-        act_ref[j] = (pre * sig).astype(BF)
-        return pre, sig
-
-    def before(j, _):
-        pre_of(j)
-        return 0
-
-    def own(j, _):
-        pre, sig = pre_of(j)
-        sl_ref[j - 2] = sig * (1.0 + pre * (1.0 - sig))
-        return 0
-
-    lax.fori_loop(0, 2, before, 0)
-    lax.fori_loop(2, SLAB + 2, own, 0)
     icg = jnp.zeros((E, C), F32)
     for t in range(2):
-        gp = (acc_ref[t] * sl_ref[t]).astype(BF)
+        pre, sig = pre_of(clip_ref, first, all_ref, z_ref, wcol, t, t)
+        act_ref[t] = (pre * sig).astype(BF)
+        gp = (acc_ref[t] * (sig * (1.0 + pre * (1.0 - sig)))).astype(BF)
         back = mm(wcat_ref[...], gp, 1, 0)
         for k in range(TAPS):
             src = source(clip_ref, first, t, k) + 2
             lacc_ref[src] += back[k * CL : (k + 1) * CL]
-        icg = icg + mm(z_ref[t + 2], gp, 1, 1)
+        icg = icg + mm(z_ref[t], gp, 1, 1)
     halo_ref[...] = lacc_ref[:2]
     part_ref[...] = lacc_ref[2:]
     icg_ref[...] = icg
-    slope_ref[...] = sl_ref[2:]
-
-
-def k_weight(clip_ref, grad_ref, act_ref, after_ref, keep_ref, send_ref, acc_ref):
+
+
+def k_rest(
+    clip_ref, prev_ref, lat_ref, win_ref, bias_ref, act01_ref,
+    act_ref, slope_ref, all_ref, z_ref, wcat_ref,
+):
+    first = lax.axis_index("tm") * SLAB
+    all_ref[:SLAB] = prev_ref[...]
+    all_ref[SLAB:] = lat_ref[...]
+    set_weights(win_ref, bias_ref, wcat_ref)
+    wcol = wcat_ref[...].T
+    act_ref[2:4] = act01_ref[...]
+
+    def before(j, _):
+        pre, sig = pre_of(clip_ref, first, all_ref, z_ref, wcol, j, j - 2)
+        act_ref[j] = (pre * sig).astype(BF)
+        return 0
+
+    def own(j, _):
+        pre, sig = pre_of(clip_ref, first, all_ref, z_ref, wcol, j, j)
+        act_ref[j + 2] = (pre * sig).astype(BF)
+        slope_ref[j - 2] = sig * (1.0 + pre * (1.0 - sig))
+        return 0
+
+    lax.fori_loop(0, 2, before, 0)
+    lax.fori_loop(2, SLAB, own, 0)
+
+
+def k_weight(clip_ref, grad_ref, act_ref, keep_ref, send_ref, acc_ref):
     first = lax.axis_index("tm") * SLAB
     core = lax.axis_index("tm") % 2
     for k in range(TAPS):
@@ -176,7 +205,7 @@
 
 def k_second(
     clip_ref, next_ref, lat_ref, win_ref, conv_ref, acc_in_ref, slope_ref, part_ref, halo_ref, icg_in_ref, after_ref,
-    tok_ref, icg_ref, acc_ref, z_ref, wcat_ref, lacc_ref, icg_acc, low_ref,
+    tok0_ref, tok1_ref, tok2_ref, tok3_ref, icg_ref, passed_ref, acc_ref, z_ref, wcat_ref, lacc_ref, icg_acc, low_ref,
 ):
     first = lax.axis_index("tm") * SLAB
     start = [clip_rel(clip_ref, first, SLAB + t) for t in range(2)]
@@ -211,13 +240,22 @@
     r = lax.broadcasted_iota(jnp.int32, (PX, PX), 0)
     c = lax.broadcasted_iota(jnp.int32, (PX, PX), 1)
     pick = (((r & 3) << 7) + (r >> 2) == c).astype(F32).astype(BF)
-    tok_ref[...] = mm(low_ref[...], pick, 1, 0).astype(BF)
+    low_ref[...] = mm(low_ref[...], pick, 1, 0).astype(BF)
+    z = lax.axis_index("seq")
+    for k, ref in enumerate((tok0_ref, tok1_ref, tok2_ref, tok3_ref)):
+        ref[...] = low_ref[pl.ds(pl.multiple_of(lax.rem(z + k, 4) * CL, CL), CL), :]
     for rb in range(4):
         for lb in range(4):
             icg_ref[rb * 4 + lb] = icg_acc[rb * 16 : (rb + 1) * 16, lb * 128 : (lb + 1) * 128].astype(BF)
 
 
-def k_grad(recv_ref, normed_ref, icg_ref, keep_ref, other_ref, pack_ref, tok_ref, raw_ref):
+def k_grad(
+    tok0_ref, tok1_ref, tok2_ref, tok3_ref, normed_ref, icg_ref, keep_ref, other_ref,
+    pack_ref, tok_hbm, raw_ref, recv_ref, tok_ref, sem,
+):
+    z = lax.axis_index("seq")
+    for k, ref in enumerate((tok0_ref, tok1_ref, tok2_ref, tok3_ref)):
+        recv_ref[lax.rem(z + 4 - k, 4)] = ref[...]
     for s in range(4):
         for q in range(EDGE):
             raw_ref[q * CL : (q + 1) * CL, s * 128 : (s + 1) * 128] = recv_ref[
@@ -228,6 +266,8 @@
     order = (((r & 3) << 4) + (r >> 2) == c).astype(F32).astype(BF)
     tok = mm(order, raw_ref[...], 1, 0)
     tok_ref[...] = tok.astype(BF)
+    copy = pltpu.make_async_copy(tok_ref, tok_hbm, sem)
+    copy.start()
     total = jnp.broadcast_to(jnp.sum(tok, axis=1, keepdims=True), (E, 128)).astype(BF)
     for lb in range(D // 512):
         g = mm(tok_ref[...], normed_ref[:, lb * 512 : (lb + 1) * 512], 1, 0).astype(BF)
@@ -244,6 +284,7 @@
             rows = slice(half * 24, half * 24 + 24)
             both = keep_ref[xy * 4 : xy * 4 + 4].astype(F32) + other_ref[xy * 4 : xy * 4 + 4].astype(F32)
             pack_ref[at, 16:, :] = both[:, rows, :].astype(BF)
+    copy.wait()
 
 
 def k_hidden(tok_ref, hidden_ref, wt_ref, mod_ref, out_ref):
@@ -260,16 +301,22 @@
     out_ref[...] = (inv * (ng - m1 - normed * m2)).astype(BF)
 
 
-def k_sum(recv_ref, out_ref, keep_ref, send_ref):
+def k_sum(recv_ref, out_hbm, keep_ref, send_hbm, out_ref, send_ref, sems):
     core = lax.axis_index("tm") % 2
     total = jnp.sum(recv_ref[:, :16, :].astype(F32), axis=0).astype(BF)
     out_ref[...] = jnp.broadcast_to(total[None], out_ref.shape)
+    copy = pltpu.make_async_copy(out_ref, out_hbm, sems.at[0])
+    copy.start()
     sums = [jnp.zeros((24, 128), F32)] * 2
     for d in range(128):
         c = (d // 4) % 2
         sums[c] = sums[c] + recv_ref[d, 16:, :].astype(F32)
     keep_ref[...] = jnp.where(core == 0, sums[0], sums[1])
     send_ref[...] = jnp.where(core == 0, sums[1], sums[0])
+    away = pltpu.make_async_copy(send_ref, send_hbm, sems.at[1])
+    away.start()
+    copy.wait()
+    away.wait()
 
 
 def k_last(all_ref, wt_ref, mod_ref, final_ref, modg_ref, icg_ref, bias_ref):
@@ -296,7 +343,9 @@
         bias_ref[:, lb * 128 : (lb + 1) * 128] = all_ref[96 + 12 + lb].astype(F32)[0:1]
 
 
-def k_weight_out(keep_ref, other_ref, out_ref):
+def k_weight_out(keep_ref, other_ref, wt_ref, mod_ref, out_ref, wt_near_ref, mod_near_ref):
+    wt_near_ref[...] = wt_ref[...]
+    mod_near_ref[...] = mod_ref[...]
     core = lax.axis_index("tm") % 2
     mine, other = keep_ref[...], other_ref[...]
     halves = [jnp.where(core == 0, mine, other), jnp.where(core == 0, other, mine)]
@@ -322,6 +371,10 @@
     return jax.ShapeDtypeStruct(shape, dtype)
 
 
+def pinned(*arrays):
+    return [pltpu.with_memory_space_constraint(a, pltpu.HBM) for a in arrays]
+
+
 def shifted(block, distance):
     n = lax.axis_size("tm")
     route = [(i - distance, i) for i in range(n) if 0 <= i - distance < n]
@@ -340,48 +393,74 @@
     win = conv_in_w.transpose(0, 2, 1)
     wt = final_w.T
     bias = conv_in_b.reshape(1, C)
-    grad_next = shifted(grad_out[:2], -1)
     lat_prev = shifted(latents, 1)
     unit = 2 * C * C * PX
+    grad_sent = grad_out[:2]
+    grad_next = shifted(grad_sent, -1)
     acc = call(
-        k_back, sds((SLAB, C, PX), F32), [SMEM, VMEM, VMEM], mib=16, est=cost(9 * unit, 8 << 20), name="back"
-    )(clip_start, grad_out, conv_w)
-    act, slope, part, halo, icg_part = call(
+        k_back, sds((SLAB, C, PX), F32), [PIN, PIN, VMEM, PIN],
+        [
+            pltpu.SMEM((FRAMES,), jnp.int32), pltpu.VMEM((TAPS, C, C), BF), pltpu.VMEM((SLAB, C, PX), BF),
+            pltpu.SemaphoreType.DMA((3,)),
+        ],
+        mib=16, est=cost(9 * unit, 8 << 20), name="back",
+    )(*pinned(clip_start, conv_w), grad_sent, *pinned(grad_out))
+    act01, part, halo, icg_part = call(
         k_first,
-        (
-            sds((SLAB + 2, C, PX), BF), sds((2, C, PX), F32),
-            sds((SLAB, CL, PX), F32), sds((2, CL, PX), F32), sds((E, C), F32),
-        ),
+        (sds((2, C, PX), BF), sds((SLAB, CL, PX), F32), sds((2, CL, PX), F32), sds((E, C), F32)),
         [SMEM] + [VMEM] * 5,
         [
-            pltpu.VMEM((2 * SLAB, CL, PX), BF), pltpu.VMEM((SLAB + 2, E, PX), BF), pltpu.VMEM((E, C), BF),
-            pltpu.VMEM((SLAB, C, PX), F32), pltpu.VMEM((SLAB + 2, CL, PX), F32),
+            pltpu.VMEM((2 * SLAB, CL, PX), BF), pltpu.VMEM((2, E, PX), BF), pltpu.VMEM((E, C), BF),
+            pltpu.VMEM((SLAB + 2, CL, PX), F32),
         ],
-        mib=24, est=cost(4 * unit, 10 << 20), name="first",
+        mib=16, est=cost(2 * unit, 5 << 20), name="first",
     )(clip_start, lat_prev, latents, win, bias, acc)
     halo_recv = shifted(halo, -1)
-    normed = call(
-        k_prep, sds((NTOK, D), BF), [VMEM, HERE], mib=16, est=cost(10 * NTOK * D, 6 << 20), name="prep"
-    )(hidden, halo)
-    tok_part, icg_blocks = call(
-        k_second, (sds((SLAB * CL, PX), BF), sds((16, 16, 128), BF)), [SMEM] + [VMEM] * 9 + [HERE],
-        [
+    act, slope = call(
+        k_rest, (sds((SLAB + 2, C, PX), BF), sds((2, C, PX), F32)), [SMEM] + [VMEM] * 5,
+        [pltpu.VMEM((2 * SLAB, CL, PX), BF), pltpu.VMEM((SLAB, E, PX), BF), pltpu.VMEM((E, C), BF)],
+        mib=16, est=cost(2 * unit, 8 << 20), name="rest",
+    )(clip_start, lat_prev, latents, win, bias, act01)
+    keep, send = call(
+        k_weight, (sds((32, 2, 48, 128), BF),) * 2, [SMEM] + [VMEM] * 2,
+        [pltpu.VMEM((16, 2, 16, TAPS * C), F32)], mib=16, est=cost(12 * unit, 60 << 20), name="weight",
+    )(clip_start, grad_out, act)
+    piece = sds((CL, PX), BF)
+    half = sds((32, 2, 48, 128), BF)
+    *tok_parts, icg_blocks, send = pl.pallas_call(
+        k_second,
+        out_shape=(piece,) * 4 + (sds((16, 16, 128), BF), half),
+        in_specs=[SMEM] + [VMEM] * 9 + [HERE],
+        out_specs=(VMEM,) * 5 + (HERE,),
+        scratch_shapes=[
             pltpu.VMEM((2, C, PX), F32), pltpu.VMEM((2, E, PX), BF), pltpu.VMEM((TAPS * CL, C), BF),
             pltpu.VMEM((SLAB, CL, PX), F32), pltpu.VMEM((E, C), F32), pltpu.VMEM((SLAB * CL, PX), BF),
         ],
-        mib=16, est=cost(6 * unit, 8 << 20), name="second",
-    )(clip_start, grad_next, latents, win, conv_w, acc, slope, part, halo_recv, icg_part, normed)
-    tok_recv = exchange(tok_part, "seq").reshape(4, CL, PX)
-    keep, send = call(
-        k_weight, (sds((32, 2, 48, 128), BF),) * 2, [SMEM] + [VMEM] * 2 + [HERE],
-        [pltpu.VMEM((16, 2, 16, TAPS * C), F32)], mib=16, est=cost(12 * unit, 7 << 20), name="weight",
-    )(clip_start, grad_out, act, icg_blocks)
+        input_output_aliases={10: 5},
+        compiler_params=params(16),
+        cost_estimate=cost(6 * unit, 8 << 20),
+        name="second",
+    )(clip_start, grad_next, latents, win, conv_w, acc, slope, part, halo_recv, icg_part, send)
+    toks = [tok_parts[0]] + [
+        lax.ppermute(tok_parts[k], "seq", [(i, (i + k) % 4) for i in range(4)]) for k in range(1, 4)
+    ]
     other = swapped(send)
-    pack, tok = call(
-        k_grad, (sds((128, 40, 128), BF), sds((E, NTOK), BF)), [VMEM] * 5,
-        [pltpu.VMEM((E, NTOK), BF)],
-        mib=16, est=cost(2 * NTOK * D * E, 5 << 20), name="grad",
-    )(tok_recv, normed, icg_blocks, keep.reshape(64, 48, 128), other.reshape(64, 48, 128))
+    normed = call(
+        k_prep, sds((NTOK, D), BF), [VMEM, HERE], mib=16, est=cost(10 * NTOK * D, 6 << 20), name="prep"
+    )(hidden, icg_blocks)
+    pack, tok = pl.pallas_call(
+        k_grad,
+        out_shape=(sds((128, 40, 128), BF), pltpu.HBM((E, NTOK), BF)),
+        in_specs=[VMEM] * 8,
+        out_specs=(VMEM, PIN),
+        scratch_shapes=[
+            pltpu.VMEM((E, NTOK), BF), pltpu.VMEM((4, CL, PX), BF), pltpu.VMEM((E, NTOK), BF),
+            pltpu.SemaphoreType.DMA,
+        ],
+        compiler_params=params(16),
+        cost_estimate=cost(2 * NTOK * D * E, 5 << 20),
+        name="grad",
+    )(*toks, normed, icg_blocks, keep.reshape(64, 48, 128), other.reshape(64, 48, 128))
     recv = exchange(pack, BOTH)
     hidden_grad = pl.pallas_call(
         k_hidden,
@@ -398,18 +477,27 @@
         cost_estimate=cost(2 * NTOK * D * E, 6 << 20),
         name="hidden",
     )(tok, hidden, wt, modulation)
-    copies, own, away = call(
-        k_sum, (sds((128, 16, 128), BF), sds((24, 128), F32), sds((24, 128), F32)), [VMEM],
-        mib=16, est=cost(1 << 20, 2 << 20), name="sum",
+    copies, own, away = pl.pallas_call(
+        k_sum,
+        out_shape=(pltpu.HBM((128, 16, 128), BF), sds((24, 128), F32), pltpu.HBM((24, 128), F32)),
+        in_specs=[VMEM],
+        out_specs=(PIN, VMEM, PIN),
+        scratch_shapes=[
+            pltpu.VMEM((128, 16, 128), BF), pltpu.VMEM((24, 128), F32), pltpu.SemaphoreType.DMA((2,)),
+        ],
+        compiler_params=params(16),
+        cost_estimate=cost(1 << 20, 2 << 20),
+        name="sum",
     )(recv)
     everything = exchange(copies, BOTH)
-    weight_grad = call(
-        k_weight_out, sds((TAPS, 4, C), F32), [VMEM] * 2, mib=16, est=cost(1 << 12, 1 << 16), name="weight_out"
-    )(own, swapped(away))
+    weight_grad, wt_near, mod_near = call(
+        k_weight_out, (sds((TAPS, 4, C), F32), sds((E, D), BF), sds((2, D), F32)), [VMEM] * 4,
+        mib=16, est=cost(1 << 12, 1 << 16), name="weight_out",
+    )(own, swapped(away), wt, modulation)
     final_t, mod_grad, icg, bias_grad = call(
         k_last, (sds((E, D), F32), sds((2, D), F32), sds((TAPS * CL, C), F32), sds((1, C), F32)), [VMEM] * 3,
         mib=16, est=cost(1 << 20, 2 << 20), name="last",
-    )(everything, wt, modulation)
+    )(everything, wt_near, mod_near)
     return (
         hidden_grad,
         weight_grad.transpose(1, 0, 2),

time: 102 us -> 92.6 us (0.908)
  blocking collectives: 44.5 us -> 33.5 us
  local copies, waits for them, and re-layouts: 8.74 us -> 2.92 us
  starting transfers between devices: 15.1 us -> 20.9 us
  Pallas kernels: 26.5 us -> 28.9 us
    all_to_all x2 -> x1, blocking collectives: 44.5 us -> 33.5 us  [exchange(): return lax.all_to_all(block, axes, split_axis=0, concat_axis=0, tiled=True)]
    ppermute x0 -> x3, starting transfers between devices: none -> 5.82 us  [local(): lax.ppermute(tok_parts[k], 'seq', [(i, (i + k) % 4) for i in range(4)])]
    unnamed x34 -> x20, local copies, waits for them, and re-layouts: 7.4 us -> 1.63 us
    pallas_call x7 -> x8, Pallas kernels: 16.3 us -> 18.7 us  [the longest x1 4.65 us: local(): call(k_weight, (sds((32, 2, 48, 128), BF),) * 2, [SMEM] + [VMEM] * 2, [pl...]
  transfers between devices with their start and end apart: 6 -> 9, of which waited for: 2 -> 1; matrix products, arithmetic and copies ran while one was open for 0% -> 0% of each run, Pallas kernels for 16% -> 24%
where the time goes in v2:
time: 92.6 us; the launch traced here: 92.1 us
  blocking collectives  33.5 us (36%)
  Pallas kernels  28.9 us (31%)
  starting transfers between devices  20.9 us (23%)
  waiting for transfers between devices  4.88 us (5%)
  local copies, waits for them, and re-layouts  2.92 us (3%)
    all_to_all x1, blocking collectives, exchange(): return lax.all_to_all(block, axes, split_axis=0, concat_axis=0, tiled=True)  33.5 us
    ppermute x3, starting transfers between devices, shifted(): return lax.ppermute(block, 'tm', route)  8.78 us
    ppermute x3, starting transfers between devices, local(): lax.ppermute(tok_parts[k], 'seq', [(i, (i + k) % 4) for i in range(4)])  5.82 us
    pallas_call x1, Pallas kernels, local(): pl.pallas_call(k_hidden, grid=(4,), out_shape=sds((NTOK, D), BF), in_spec...  5.32 us
    all_to_all x1, starting transfers between devices, exchange(): return lax.all_to_all(block, axes, split_axis=0, concat_axis=0, tiled=True)  4.87 us
    all_to_all x1, waiting for transfers between devices, exchange(): return lax.all_to_all(block, axes, split_axis=0, concat_axis=0, tiled=True)  4.86 us
    pallas_call x1, Pallas kernels, local(): call(k_weight, (sds((32, 2, 48, 128), BF),) * 2, [SMEM] + [VMEM] * 2, [pl...  4.65 us
    pallas_call x1, Pallas kernels, local(): call(k_back, sds((SLAB, C, PX), F32), [PIN, PIN, VMEM, PIN], [pltpu.SMEM(...  4.42 us
  transfers between devices with their start and end apart: 9, of which 1 were waited for; matrix products, arithmetic and copies ran while one was open for 0% of the time, Pallas kernels for 24%

profile of v2, /device:TPU:1, one launch (start us, length us, event | category | flops | bytes accessed | tf_op | source)
XLA Modules:
  0.0 92.1 jit_solution(5854291476648501760)
XLA Ops:
  0.6 1.3 %slice.3.sent_ref = bf16[2,512,512]{2,1,0:T(8,128)(2,1)S(1)} slice(bf16[4,512,512]{2,1,0:T(8,128)(2,1)} %grad_ref.1), slice={[0:2], [0:512], [0:512]} | slice | bytes 2097152 | tf_op jit(solution)/shard_map/slice | solution.py:398
  1.9 0.0 copy-start.4
  1.9 0.0 copy-start.5
  2.0 0.0 copy-start.8
  2.0 0.0 copy-start.9
  2.0 3.5 %collective-permute-start = (bf16[2,512,512]{2,1,0:T(8,128)(2,1)S(1)}, bf16[2,512,512]{2,1,0:T(8,128)(2,1)S(1)}, u32[]{:S(2)}, u32[]{:S(2)}) collective-permute-start(bf16[2,512,512]{2,1,0:T(8,128)(2,1)S(1)} %slice.3.sent_ref), channel_id=1, source_target_pairs={{4,0},{8,4},{12,8},{16,12},{20,16},{24,20},{28,24},{32,28},{36,32}... | collective-permute-start | bytes 3145736 | tf_op jit(solution)/shard_map/ppermute | solution.py:381
  5.4 3.2 %collective-permute-start.1 = (bf16[4,16,512]{2,1,0:T(8,128)(2,1)}, bf16[4,16,512]{2,1,0:T(8,128)(2,1)S(1)}, u32[]{:S(2)}, u32[]{:S(2)}) collective-permute-start(bf16[4,16,512]{2,1,0:T(8,128)(2,1)} %lat_ref.5), channel_id=1, source_target_pairs={{0,4},{4,8},{8,12},{12,16},{16,20},{20,24},{24,28},{28,32},{32,36}... | collective-permute-start | bytes 196616 | tf_op jit(solution)/shard_map/ppermute | solution.py:381
  8.6 4.4 %back.1.acc_ref.acc_in_ref = f32[4,512,512]{2,1,0:T(8,128)S(1)} custom-call(s32[128]{0:T(128)} %clip_ref.7, bf16[3,512,512]{2,1,0:T(8,128)(2,1)} %conv_ref.1, bf16[2,512,512]{2,1,0:T(8,128)(2,1)S(1)} %slice.3.sent_ref, bf16[4,512,512]{2,1,0:T(8,128)(2,1)} %grad_ref.1), custom_call_target="tpu_custom_call" | custom-call | flops 2415919104 | bytes 8388608 | tf_op jit(solution)/shard_map/back/pallas_call | solution.py:400
  13.1 0.0 collective-permute-done.1.prev_ref
  13.1 0.0 copy-done.4
  13.1 0.0 copy-done.5
  13.1 0.0 copy-done.8
  13.1 0.0 copy-done.9
  13.1 0.0 copy-start.3
  13.1 2.2 %first.1 = (bf16[2,512,512]{2,1,0:T(8,128)(2,1)S(1)}, f32[4,16,512]{2,1,0:T(8,128)S(1)}, f32[2,16,512]{2,1,0:T(8,128)S(1)}, f32[64,512]{1,0:T(8,128)S(1)}) custom-call(s32[128]{0:T(128)S(1)} %copy-done.9, bf16[4,16,512]{2,1,0:T(8,128)(2,1)S(1)} %collective-permute-done.1.prev_ref, bf16[4,16,512]{2,1,0:T(8,128)(2,1)S(1)} %copy-done.4, ...), custom_call_target="tpu_custom_call" | custom-call | flops 536870912 | bytes 5242880 | tf_op jit(solution)/shard_map/first/pallas_call | solution.py:408
  15.3 2.1 %collective-permute-start.2 = (f32[2,16,512]{2,1,0:T(8,128)S(1)}, f32[2,16,512]{2,1,0:T(8,128)S(1)}, u32[]{:S(2)}, u32[]{:S(2)}) collective-permute-start(f32[2,16,512]{2,1,0:T(8,128)S(1)} %get-tuple-element.35), channel_id=1, source_target_pairs={{4,0},{8,4},{12,8},{16,12},{20,16},{24,20},{28,24},{32,28},{36,32}... | collective-permute-start | bytes 196616 | tf_op jit(solution)/shard_map/ppermute | solution.py:381
  17.4 2.4 %rest.1 = (bf16[6,512,512]{2,1,0:T(8,128)(2,1)S(1)}, f32[2,512,512]{2,1,0:T(8,128)S(1)}) custom-call(s32[128]{0:T(128)S(1)} %copy-done.9, bf16[4,16,512]{2,1,0:T(8,128)(2,1)S(1)} %collective-permute-done.1.prev_ref, bf16[4,16,512]{2,1,0:T(8,128)(2,1)S(1)} %copy-done.4, bf16[3,16,512]{2,1,0:T(8,128)(2,1)S(1)} %bitcast.16, f32[1,512]{1,0:T(1,128)S(1)} %bitcast.19, ...), custom_call_target="tpu_custom_call" | custom-call | flops 536870912 | bytes 8388608 | tf_op jit(solution)/shard_map/rest/pallas_call | solution.py:419
  19.8 0.0 copy-done.3
  19.8 0.0 copy-start.1
  19.9 4.7 %weight.1 = (bf16[32,2,48,128]{3,2,1,0:T(8,128)(2,1)S(1)}, bf16[32,2,48,128]{3,2,1,0:T(8,128)(2,1)S(1)}) custom-call(s32[128]{0:T(128)S(1)} %copy-done.9, bf16[4,512,512]{2,1,0:T(8,128)(2,1)S(1)} %copy-done.3, bf16[6,512,512]{2,1,0:T(8,128)(2,1)S(1)} %get-tuple-element.37.act_ref), custom_call_target="tpu_custom_call" | custom-call | flops 3221225472 | bytes 62914560 | tf_op jit(solution)/shard_map/weight/pallas_call | solution.py:424
  24.5 0.0 collective-permute-done.2.halo_ref
  24.5 0.0 collective-permute-done.next_ref
  24.5 0.0 copy-done.1
  24.5 0.0 copy-start
  24.6 2.5 %second.1 = (bf16[16,512]{1,0:T(8,128)(2,1)S(1)}, bf16[16,512]{1,0:T(8,128)(2,1)S(1)}, bf16[16,512]{1,0:T(8,128)(2,1)S(1)}, bf16[16,512]{1,0:T(8,128)(2,1)S(1)},...) custom-call(s32[128]{0:T(128)S(1)} %copy-done.9, ...), custom_call_target="tpu_custom_call", output_to_operand_aliasing={{5}: (10, {})} | custom-call | flops 1610612736 | bytes 8388608 | tf_op jit(solution)/shard_map/second/pallas_call | solution.py:430
  27.0 0.1 collective-permute-start.6
  27.1 1.8 %collective-permute-start.3 = (bf16[16,512]{1,0:T(8,128)(2,1)S(1)}, bf16[16,512]{1,0:T(8,128)(2,1)S(1)}, u32[]{:S(2)}, u32[]{:S(2)}) collective-permute-start(bf16[16,512]{1,0:T(8,128)(2,1)S(1)} %get-tuple-element.40), channel_id=1, source_target_pairs={{0,1},{1,2},{2,3},{3,0},{4,5},{5,6},{6,7},{7,4},{8,9},{9,10},{10,1... | collective-permute-start | bytes 49160 | tf_op jit(solution)/shard_map/ppermute | solution.py:445
  28.9 3.3 %collective-permute-start.4 = (bf16[16,512]{1,0:T(8,128)(2,1)S(1)}, bf16[16,512]{1,0:T(8,128)(2,1)S(1)}, u32[]{:S(2)}, u32[]{:S(2)}) collective-permute-start(bf16[16,512]{1,0:T(8,128)(2,1)S(1)} %get-tuple-element.41), channel_id=1, source_target_pairs={{0,2},{1,3},{2,0},{3,1},{4,6},{5,7},{6,4},{7,5},{8,10},{9,11},{10,... | collective-permute-start | bytes 49160 | tf_op jit(solution)/shard_map/ppermute | solution.py:445
  32.2 0.7 collective-permute-start.5
  32.9 0.0 copy-done
  32.9 2.6 %prep.1.normed_ref = bf16[512,3072]{1,0:T(8,128)(2,1)S(1)} custom-call(bf16[512,3072]{1,0:T(8,128)(2,1)S(1)} %copy-done, bf16[16,16,128]{2,1,0:T(8,128)(2,1)S(1)} %get-tuple-element.43.after_ref.icg_ref), custom_call_target="tpu_custom_call" | custom-call | flops 15728640 | bytes 6291456 | tf_op jit(solution)/shard_map/prep/pallas_call | solution.py:448
  35.5 0.0 collective-permute-done.3.tok1_ref
  35.5 0.0 collective-permute-done.4.tok2_ref
  35.5 0.0 collective-permute-done.5.tok3_ref
  35.6 0.0 collective-permute-done.6
  35.6 0.9 %grad.1 = (bf16[128,40,128]{2,1,0:T(8,128)(2,1)S(1)}, bf16[64,512]{1,0:T(8,128)(2,1)}) custom-call(bf16[16,512]{1,0:T(8,128)(2,1)S(1)} %get-tuple-element.39.tok0_ref, bf16[16,512]{1,0:T(8,128)(2,1)S(1)} %collective-permute-done.3.tok1_ref, bf16[16,512]{1,0:T(8,128)(2,1)S(1)} %collective-permute-done.4.tok2_ref, ...), custom_call_target="tpu_custom_call" | custom-call | flops 201326592 | bytes 5242880 | tf_op jit(solution)/shard_map/grad/pallas_call | solution.py:451
  36.5 0.0 copy-start.2
  36.5 33.5 %all_to_all.10.recv_ref = bf16[128,40,128]{2,1,0:T(8,128)(2,1)S(1)} all-to-all(bf16[128,40,128]{2,1,0:T(8,128)(2,1)S(1)} %get-tuple-element.47), channel_id=1, replica_groups=mesh['tm'=32,'seq'=4] {'tm','seq'}, dimensions={0} | all-to-all | bytes 2621440 | tf_op jit(solution)/shard_map/all_to_all | solution.py:389
  70.0 1.0 %sum.1 = (bf16[128,16,128]{2,1,0:T(8,128)(2,1)}, f32[24,128]{1,0:T(8,128)S(1)}, f32[24,128]{1,0:T(8,128)}) custom-call(bf16[128,40,128]{2,1,0:T(8,128)(2,1)S(1)} %all_to_all.10.recv_ref), custom_call_target="tpu_custom_call" | custom-call | flops 1048576 | bytes 2097152 | tf_op jit(solution)/shard_map/sum/pallas_call | solution.py:480
  71.0 4.9 %all-to-all-start.1 = ((bf16[128,16,128]{2,1,0:T(8,128)(2,1)}), bf16[128,16,128]{2,1,0:T(8,128)(2,1)}, u32[]{:S(2)}, u32[]{:S(2)}) async-start(bf16[128,16,128]{2,1,0:T(8,128)(2,1)} %get-tuple-element.51), calls=%async_computation.1 | async-start | bytes 1048576 | tf_op jit(solution)/shard_map/all_to_all | solution.py:389
  75.9 1.4 %collective-permute-start.7 = (f32[24,128]{1,0:T(8,128)}, f32[24,128]{1,0:T(8,128)S(1)}, u32[]{:S(2)}, u32[]{:S(2)}) collective-permute-start(f32[24,128]{1,0:T(8,128)} %get-tuple-element.49), channel_id=1, source_target_pairs={{0,4},{4,0},{8,12},{12,8},{16,20},{20,16},{24,28},{28,24},{32,36},... | collective-permute-start | bytes 36872 | tf_op jit(solution)/shard_map/ppermute | solution.py:385
  77.3 0.7 copy-done.6
  78.0 0.8 copy-done.7
  78.9 5.3 %hidden.1 = bf16[512,3072]{1,0:T(8,128)(2,1)} custom-call(bf16[64,512]{1,0:T(8,128)(2,1)S(1)} %copy-done.7, bf16[512,3072]{1,0:T(8,128)(2,1)S(1)} %copy-done, bf16[64,3072]{1,0:T(8,128)(2,1)S(1)} %bitcast.11, f32[2,3072]{1,0:T(2,128)S(1)} %copy-done.6), custom_call_target="tpu_custom_call" | custom-call | flops 201326592 | bytes 6291456 | tf_op jit(solution)/shard_map/hidden/pallas_call | solution.py:465
  84.2 0.0 collective-permute-done.7.other_ref
  84.2 0.6 weight_out.1
  84.8 4.9 %all-to-all-done.1.all_ref = bf16[128,16,128]{2,1,0:T(8,128)(2,1)} async-done(((bf16[128,16,128]{2,1,0:T(8,128)(2,1)}), bf16[128,16,128]{2,1,0:T(8,128)(2,1)}, u32[]{:S(2)}, u32[]{:S(2)}) %all-to-all-start.1) | async-done | bytes 524320 | tf_op jit(solution)/shard_map/all_to_all | solution.py:389
  89.7 2.4 %last.1 = (f32[64,3072]{1,0:T(8,128)}, f32[2,3072]{1,0:T(2,128)}, f32[48,512]{1,0:T(8,128)}, f32[1,512]{1,0:T(1,128)}) custom-call(bf16[128,16,128]{2,1,0:T(8,128)(2,1)} %all-to-all-done.1.all_ref, bf16[64,3072]{1,0:T(8,128)(2,1)S(1)} %get-tuple-element.52.wt_ref, f32[2,3072]{1,0:T(2,128)S(1)} %get-tuple-element.53.mod_ref), custom_call_target="tpu_custom_call" | custom-call | flops 1048576 | bytes 2097152 | tf_op jit(solution)/shard_map/last/pallas_call | solution.py:497
  (3 shorter events, 0.0 us)
Async XLA Ops:
  1.9 11.2 %copy-start.4 = (bf16[4,16,512]{2,1,0:T(8,128)(2,1)S(1)}, bf16[4,16,512]{2,1,0:T(8,128)(2,1)}, u32[]{:S(2)}) copy-start(bf16[4,16,512]{2,1,0:T(8,128)(2,1)} %lat_ref.5) | copy-start | bytes 196612
  1.9 11.1 %copy-start.5 = (bf16[3,512,16]{1,2,0:T(8,128)(2,1)S(1)}, bf16[3,512,16]{1,2,0:T(8,128)(2,1)}, u32[]{:S(2)}) copy-start(bf16[3,512,16]{1,2,0:T(8,128)(2,1)} %param.12) | copy-start | bytes 147460
  2.0 11.1 %copy-start.8 = (f32[512]{0:T(512)S(1)}, f32[512]{0:T(512)}, u32[]{:S(2)}) copy-start(f32[512]{0:T(512)} %param.13) | copy-start | bytes 6148
  2.0 11.1 %copy-start.9 = (s32[128]{0:T(128)S(1)}, s32[128]{0:T(128)}, u32[]{:S(2)}) copy-start(s32[128]{0:T(128)} %clip_ref.7) | copy-start | bytes 1540
  2.0 22.5 %collective-permute-start = (bf16[2,512,512]{2,1,0:T(8,128)(2,1)S(1)}, bf16[2,512,512]{2,1,0:T(8,128)(2,1)S(1)}, u32[]{:S(2)}, u32[]{:S(2)}) collective-permute-start(bf16[2,512,512]{2,1,0:T(8,128)(2,1)S(1)} %slice.3.sent_ref), channel_id=1, source_target_pairs={{4,0},{8,4},{12,8},{16,12},{20,16},{24,20},{28,24},{32,28},{36,32}... | collective-permute-start | bytes 3145736 | tf_op jit(solution)/shard_map/ppermute | solution.py:381
  5.4 7.6 %collective-permute-start.1 = (bf16[4,16,512]{2,1,0:T(8,128)(2,1)}, bf16[4,16,512]{2,1,0:T(8,128)(2,1)S(1)}, u32[]{:S(2)}, u32[]{:S(2)}) collective-permute-start(bf16[4,16,512]{2,1,0:T(8,128)(2,1)} %lat_ref.5), channel_id=1, source_target_pairs={{0,4},{4,8},{8,12},{12,16},{16,20},{20,24},{24,28},{28,32},{32,36}... | collective-permute-start | bytes 196616 | tf_op jit(solution)/shard_map/ppermute | solution.py:381
  13.1 6.7 %copy-start.3 = (bf16[4,512,512]{2,1,0:T(8,128)(2,1)S(1)}, bf16[4,512,512]{2,1,0:T(8,128)(2,1)}, u32[]{:S(2)}) copy-start(bf16[4,512,512]{2,1,0:T(8,128)(2,1)} %grad_ref.1) | copy-start | bytes 6291460
  15.3 9.2 %collective-permute-start.2 = (f32[2,16,512]{2,1,0:T(8,128)S(1)}, f32[2,16,512]{2,1,0:T(8,128)S(1)}, u32[]{:S(2)}, u32[]{:S(2)}) collective-permute-start(f32[2,16,512]{2,1,0:T(8,128)S(1)} %get-tuple-element.35), channel_id=1, source_target_pairs={{4,0},{8,4},{12,8},{16,12},{20,16},{24,20},{28,24},{32,28},{36,32}... | collective-permute-start | bytes 196616 | tf_op jit(solution)/shard_map/ppermute | solution.py:381
  19.8 4.7 %copy-start.1 = (bf16[3,512,512]{2,1,0:T(8,128)(2,1)S(1)}, bf16[3,512,512]{2,1,0:T(8,128)(2,1)}, u32[]{:S(2)}) copy-start(bf16[3,512,512]{2,1,0:T(8,128)(2,1)} %conv_ref.1) | copy-start | bytes 4718596
  24.5 8.4 %copy-start = (bf16[512,3072]{1,0:T(8,128)(2,1)S(1)}, bf16[512,3072]{1,0:T(8,128)(2,1)}, u32[]{:S(2)}) copy-start(bf16[512,3072]{1,0:T(8,128)(2,1)} %hidden_ref.3) | copy-start | bytes 9437188
  27.0 8.5 %collective-permute-start.6 = (bf16[32,2,48,128]{3,2,1,0:T(8,128)(2,1)S(1)}, bf16[32,2,48,128]{3,2,1,0:T(8,128)(2,1)S(1)}, u32[]{:S(2)}, u32[]{:S(2)}) collective-permute-start(bf16[32,2,48,128]{3,2,1,0:T(8,128)(2,1)S(1)} %get-tuple-element.45), channel_id=1, source_target_pairs={{0,4},{4,0},{8,12},{12,8},{16,20},{20,16},{24,28},{28,24},{32,36},... | collective-permute-start | bytes 2359304 | tf_op jit(solution)/shard_map/ppermute | solution.py:385
  27.1 8.4 %collective-permute-start.3 = (bf16[16,512]{1,0:T(8,128)(2,1)S(1)}, bf16[16,512]{1,0:T(8,128)(2,1)S(1)}, u32[]{:S(2)}, u32[]{:S(2)}) collective-permute-start(bf16[16,512]{1,0:T(8,128)(2,1)S(1)} %get-tuple-element.40), channel_id=1, source_target_pairs={{0,1},{1,2},{2,3},{3,0},{4,5},{5,6},{6,7},{7,4},{8,9},{9,10},{10,1... | collective-permute-start | bytes 49160 | tf_op jit(solution)/shard_map/ppermute | solution.py:445
  28.9 6.6 %collective-permute-start.4 = (bf16[16,512]{1,0:T(8,128)(2,1)S(1)}, bf16[16,512]{1,0:T(8,128)(2,1)S(1)}, u32[]{:S(2)}, u32[]{:S(2)}) collective-permute-start(bf16[16,512]{1,0:T(8,128)(2,1)S(1)} %get-tuple-element.41), channel_id=1, source_target_pairs={{0,2},{1,3},{2,0},{3,1},{4,6},{5,7},{6,4},{7,5},{8,10},{9,11},{10,... | collective-permute-start | bytes 49160 | tf_op jit(solution)/shard_map/ppermute | solution.py:445
  32.2 3.3 %collective-permute-start.5 = (bf16[16,512]{1,0:T(8,128)(2,1)S(1)}, bf16[16,512]{1,0:T(8,128)(2,1)S(1)}, u32[]{:S(2)}, u32[]{:S(2)}) collective-permute-start(bf16[16,512]{1,0:T(8,128)(2,1)S(1)} %get-tuple-element.42), channel_id=1, source_target_pairs={{0,3},{1,0},{2,1},{3,2},{4,7},{5,4},{6,5},{7,6},{8,11},{9,8},{10,9... | collective-permute-start | bytes 49160 | tf_op jit(solution)/shard_map/ppermute | solution.py:445
  36.5 40.8 %copy-start.2 = (bf16[3072,64]{0,1:T(8,128)(2,1)S(1)}, bf16[3072,64]{0,1:T(8,128)(2,1)}, u32[]{:S(2)}) copy-start(bf16[3072,64]{0,1:T(8,128)(2,1)} %param.15) | copy-start | bytes 1179652
  71.0 18.6 %all-to-all-start.1 = ((bf16[128,16,128]{2,1,0:T(8,128)(2,1)}), bf16[128,16,128]{2,1,0:T(8,128)(2,1)}, u32[]{:S(2)}, u32[]{:S(2)}) async-start(bf16[128,16,128]{2,1,0:T(8,128)(2,1)} %get-tuple-element.51), calls=%async_computation.1 | async-start | bytes 1048576 | tf_op jit(solution)/shard_map/all_to_all | solution.py:389
  75.9 8.3 %collective-permute-start.7 = (f32[24,128]{1,0:T(8,128)}, f32[24,128]{1,0:T(8,128)S(1)}, u32[]{:S(2)}, u32[]{:S(2)}) collective-permute-start(f32[24,128]{1,0:T(8,128)} %get-tuple-element.49), channel_id=1, source_target_pairs={{0,4},{4,0},{8,12},{12,8},{16,20},{20,16},{24,28},{28,24},{32,36},... | collective-permute-start | bytes 36872 | tf_op jit(solution)/shard_map/ppermute | solution.py:385
  77.3 0.7 copy-start.6
  78.0 0.8 copy-start.7

commit v3 on v2

--- a/solution.py
+++ b/solution.py
@@ -66,19 +66,23 @@
 
 def k_back(clip_hbm, conv_hbm, sent_ref, grad_hbm, acc_ref, clip_ref, conv_ref, grad_ref, sems):
     copies = [
-        pltpu.make_async_copy(clip_hbm, clip_ref, sems.at[0]),
-        pltpu.make_async_copy(conv_hbm, conv_ref, sems.at[1]),
-        pltpu.make_async_copy(grad_hbm.at[pl.ds(2, 2)], grad_ref.at[pl.ds(2, 2)], sems.at[2]),
+        pltpu.make_async_copy(conv_hbm.at[0], conv_ref.at[0], sems.at[0]),
+        pltpu.make_async_copy(clip_hbm, clip_ref, sems.at[1]),
+        pltpu.make_async_copy(conv_hbm.at[pl.ds(1, 2)], conv_ref.at[pl.ds(1, 2)], sems.at[2]),
+        pltpu.make_async_copy(grad_hbm.at[pl.ds(2, 2)], grad_ref.at[pl.ds(2, 2)], sems.at[3]),
     ]
     for copy in copies:
         copy.start()
     grad_ref[:2] = sent_ref[...]
     first = lax.axis_index("tm") * SLAB
-    for copy in copies:
+    copies[0].wait()
+    for s in range(2):
+        acc_ref[s] = mm(conv_ref[0], grad_ref[s], 0, 0)
+    for copy in copies[1:]:
         copy.wait()
     start = [clip_rel(clip_ref, first, t) for t in range(SLAB)]
     for s in range(SLAB):
-        total = mm(conv_ref[0], grad_ref[s], 0, 0)
+        total = acc_ref[s] if s < 2 else mm(conv_ref[0], grad_ref[s], 0, 0)
         for k in range(1, min(TAPS, SLAB - s)):
             total = total + mm(conv_ref[k], only(start[s + k] <= s, grad_ref[s + k]), 0, 0)
         acc_ref[s] = total
@@ -401,9 +405,9 @@
         k_back, sds((SLAB, C, PX), F32), [PIN, PIN, VMEM, PIN],
         [
             pltpu.SMEM((FRAMES,), jnp.int32), pltpu.VMEM((TAPS, C, C), BF), pltpu.VMEM((SLAB, C, PX), BF),
-            pltpu.SemaphoreType.DMA((3,)),
+            pltpu.SemaphoreType.DMA((4,)),
         ],
-        mib=16, est=cost(9 * unit, 8 << 20), name="back",
+        mib=16, est=cost(1 << 10, 1 << 10), name="back",
     )(*pinned(clip_start, conv_w), grad_sent, *pinned(grad_out))
     act01, part, halo, icg_part = call(
         k_first,
@@ -423,7 +427,7 @@
     )(clip_start, lat_prev, latents, win, bias, act01)
     keep, send = call(
         k_weight, (sds((32, 2, 48, 128), BF),) * 2, [SMEM] + [VMEM] * 2,
-        [pltpu.VMEM((16, 2, 16, TAPS * C), F32)], mib=16, est=cost(12 * unit, 60 << 20), name="weight",
+        [pltpu.VMEM((16, 2, 16, TAPS * C), F32)], mib=16, est=cost(50 * unit, 7 << 20), name="weight",
     )(clip_start, grad_out, act)
     piece = sds((CL, PX), BF)
     half = sds((32, 2, 48, 128), BF)

time: 92.6 us -> 91.4 us (0.987)
  transfers between devices with their start and end apart: 9 -> 9, of which waited for: 1 -> 1; matrix products, arithmetic and copies ran while one was open for 0% -> 1% of each run, Pallas kernels for 24% -> 24%
where the time goes in v3:
time: 91.4 us; the launch traced here: 90.8 us
  blocking collectives  33.1 us (36%)
  Pallas kernels  28.4 us (31%)
  starting transfers between devices  20.6 us (23%)
  waiting for transfers between devices  4.88 us (5%)
  local copies, waits for them, and re-layouts  2.92 us (3%)
    all_to_all x1, blocking collectives, exchange(): return lax.all_to_all(block, axes, split_axis=0, concat_axis=0, tiled=True)  33.1 us
    ppermute x3, starting transfers between devices, shifted(): return lax.ppermute(block, 'tm', route)  8.57 us
    ppermute x3, starting transfers between devices, local(): lax.ppermute(tok_parts[k], 'seq', [(i, (i + k) % 4) for i in range(4)])  5.74 us
    pallas_call x1, Pallas kernels, local(): pl.pallas_call(k_hidden, grid=(4,), out_shape=sds((NTOK, D), BF), in_spec...  5.31 us
    all_to_all x1, starting transfers between devices, exchange(): return lax.all_to_all(block, axes, split_axis=0, concat_axis=0, tiled=True)  4.87 us
    all_to_all x1, waiting for transfers between devices, exchange(): return lax.all_to_all(block, axes, split_axis=0, concat_axis=0, tiled=True)  4.86 us
    pallas_call x1, Pallas kernels, local(): call(k_weight, (sds((32, 2, 48, 128), BF),) * 2, [SMEM] + [VMEM] * 2, [pl...  4.67 us
    pallas_call x1, Pallas kernels, local(): call(k_back, sds((SLAB, C, PX), F32), [PIN, PIN, VMEM, PIN], [pltpu.SMEM(...  3.9 us
  transfers between devices with their start and end apart: 9, of which 1 were waited for; matrix products, arithmetic and copies ran while one was open for 1% of the time, Pallas kernels for 24%

profile of v3, /device:TPU:1, one launch (start us, length us, event | category | flops | bytes accessed | tf_op | source)
XLA Modules:
  0.0 90.8 jit_solution(12983315419426066432)
XLA Ops:
  0.6 4.6 %collective-permute-start.1 = (bf16[4,16,512]{2,1,0:T(8,128)(2,1)}, bf16[4,16,512]{2,1,0:T(8,128)(2,1)S(1)}, u32[]{:S(2)}, u32[]{:S(2)}) collective-permute-start(bf16[4,16,512]{2,1,0:T(8,128)(2,1)} %lat_ref.5), channel_id=1, source_target_pairs={{0,4},{4,8},{8,12},{12,16},{16,20},{20,24},{24,28},{28,32},{32,36}... | collective-permute-start | bytes 196616 | tf_op jit(solution)/shard_map/ppermute | solution.py:385
  5.2 1.3 %slice.3.sent_ref = bf16[2,512,512]{2,1,0:T(8,128)(2,1)S(1)} slice(bf16[4,512,512]{2,1,0:T(8,128)(2,1)} %grad_ref.1), slice={[0:2], [0:512], [0:512]} | slice | bytes 2097152 | tf_op jit(solution)/shard_map/slice | solution.py:402
  6.5 0.0 copy-start.4
  6.5 0.0 copy-start.5
  6.6 0.0 copy-start.8
  6.6 0.0 copy-start.9
  6.6 2.1 %collective-permute-start = (bf16[2,512,512]{2,1,0:T(8,128)(2,1)S(1)}, bf16[2,512,512]{2,1,0:T(8,128)(2,1)S(1)}, u32[]{:S(2)}, u32[]{:S(2)}) collective-permute-start(bf16[2,512,512]{2,1,0:T(8,128)(2,1)S(1)} %slice.3.sent_ref), channel_id=1, source_target_pairs={{4,0},{8,4},{12,8},{16,12},{20,16},{24,20},{28,24},{32,28},{36,32}... | collective-permute-start | bytes 3145736 | tf_op jit(solution)/shard_map/ppermute | solution.py:385
  8.6 3.9 %back.1.acc_ref.acc_in_ref = f32[4,512,512]{2,1,0:T(8,128)S(1)} custom-call(s32[128]{0:T(128)} %clip_ref.7, bf16[3,512,512]{2,1,0:T(8,128)(2,1)} %conv_ref.1, bf16[2,512,512]{2,1,0:T(8,128)(2,1)S(1)} %slice.3.sent_ref, bf16[4,512,512]{2,1,0:T(8,128)(2,1)} %grad_ref.1), custom_call_target="tpu_custom_call" | custom-call | flops 1024 | bytes 1024 | tf_op jit(solution)/shard_map/back/pallas_call | solution.py:404
  12.5 0.0 collective-permute-done.1.prev_ref
  12.6 0.0 copy-done.4
  12.6 0.0 copy-done.5
  12.6 0.0 copy-done.8
  12.6 0.0 copy-done.9
  12.6 0.0 copy-start.2
  12.6 2.2 %first.1 = (bf16[2,512,512]{2,1,0:T(8,128)(2,1)S(1)}, f32[4,16,512]{2,1,0:T(8,128)S(1)}, f32[2,16,512]{2,1,0:T(8,128)S(1)}, f32[64,512]{1,0:T(8,128)S(1)}) custom-call(s32[128]{0:T(128)S(1)} %copy-done.8, bf16[4,16,512]{2,1,0:T(8,128)(2,1)S(1)} %collective-permute-done.1.prev_ref, bf16[4,16,512]{2,1,0:T(8,128)(2,1)S(1)} %copy-done.4, ...), custom_call_target="tpu_custom_call" | custom-call | flops 536870912 | bytes 5242880 | tf_op jit(solution)/shard_map/first/pallas_call | solution.py:412
  14.8 1.9 %collective-permute-start.2 = (f32[2,16,512]{2,1,0:T(8,128)S(1)}, f32[2,16,512]{2,1,0:T(8,128)S(1)}, u32[]{:S(2)}, u32[]{:S(2)}) collective-permute-start(f32[2,16,512]{2,1,0:T(8,128)S(1)} %get-tuple-element.35), channel_id=1, source_target_pairs={{4,0},{8,4},{12,8},{16,12},{20,16},{24,20},{28,24},{32,28},{36,32}... | collective-permute-start | bytes 196616 | tf_op jit(solution)/shard_map/ppermute | solution.py:385
  16.7 2.4 %rest.1 = (bf16[6,512,512]{2,1,0:T(8,128)(2,1)S(1)}, f32[2,512,512]{2,1,0:T(8,128)S(1)}) custom-call(s32[128]{0:T(128)S(1)} %copy-done.8, bf16[4,16,512]{2,1,0:T(8,128)(2,1)S(1)} %collective-permute-done.1.prev_ref, bf16[4,16,512]{2,1,0:T(8,128)(2,1)S(1)} %copy-done.4, bf16[3,16,512]{2,1,0:T(8,128)(2,1)S(1)} %bitcast.16, f32[1,512]{1,0:T(1,128)S(1)} %bitcast.19, ...), custom_call_target="tpu_custom_call" | custom-call | flops 536870912 | bytes 8388608 | tf_op jit(solution)/shard_map/rest/pallas_call | solution.py:423
  19.1 0.0 copy-done.2
  19.1 0.0 copy-start.1
  19.1 4.7 %weight.1 = (bf16[32,2,48,128]{3,2,1,0:T(8,128)(2,1)S(1)}, bf16[32,2,48,128]{3,2,1,0:T(8,128)(2,1)S(1)}) custom-call(s32[128]{0:T(128)S(1)} %copy-done.8, bf16[4,512,512]{2,1,0:T(8,128)(2,1)S(1)} %copy-done.2, bf16[6,512,512]{2,1,0:T(8,128)(2,1)S(1)} %get-tuple-element.37.act_ref), custom_call_target="tpu_custom_call" | custom-call | flops 13421772800 | bytes 7340032 | tf_op jit(solution)/shard_map/weight/pallas_call | solution.py:428
  23.8 0.0 collective-permute-done.2.halo_ref
  23.8 0.0 collective-permute-done.next_ref
  23.8 0.0 copy-done.1
  23.8 0.0 copy-start
  23.8 2.5 %second.1 = (bf16[16,512]{1,0:T(8,128)(2,1)S(1)}, bf16[16,512]{1,0:T(8,128)(2,1)S(1)}, bf16[16,512]{1,0:T(8,128)(2,1)S(1)}, bf16[16,512]{1,0:T(8,128)(2,1)S(1)},...) custom-call(s32[128]{0:T(128)S(1)} %copy-done.8, ...), custom_call_target="tpu_custom_call", output_to_operand_aliasing={{5}: (10, {})} | custom-call | flops 1610612736 | bytes 8388608 | tf_op jit(solution)/shard_map/second/pallas_call | solution.py:434
  26.3 0.1 collective-permute-start.6
  26.4 1.7 %collective-permute-start.3 = (bf16[16,512]{1,0:T(8,128)(2,1)S(1)}, bf16[16,512]{1,0:T(8,128)(2,1)S(1)}, u32[]{:S(2)}, u32[]{:S(2)}) collective-permute-start(bf16[16,512]{1,0:T(8,128)(2,1)S(1)} %get-tuple-element.40), channel_id=1, source_target_pairs={{0,1},{1,2},{2,3},{3,0},{4,5},{5,6},{6,7},{7,4},{8,9},{9,10},{10,1... | collective-permute-start | bytes 49160 | tf_op jit(solution)/shard_map/ppermute | solution.py:449
  28.1 3.3 %collective-permute-start.4 = (bf16[16,512]{1,0:T(8,128)(2,1)S(1)}, bf16[16,512]{1,0:T(8,128)(2,1)S(1)}, u32[]{:S(2)}, u32[]{:S(2)}) collective-permute-start(bf16[16,512]{1,0:T(8,128)(2,1)S(1)} %get-tuple-element.41), channel_id=1, source_target_pairs={{0,2},{1,3},{2,0},{3,1},{4,6},{5,7},{6,4},{7,5},{8,10},{9,11},{10,... | collective-permute-start | bytes 49160 | tf_op jit(solution)/shard_map/ppermute | solution.py:449
  31.4 0.7 collective-permute-start.5
  32.1 0.0 copy-done
  32.1 2.6 %prep.1.normed_ref = bf16[512,3072]{1,0:T(8,128)(2,1)S(1)} custom-call(bf16[512,3072]{1,0:T(8,128)(2,1)S(1)} %copy-done, bf16[16,16,128]{2,1,0:T(8,128)(2,1)S(1)} %get-tuple-element.43.after_ref.icg_ref), custom_call_target="tpu_custom_call" | custom-call | flops 15728640 | bytes 6291456 | tf_op jit(solution)/shard_map/prep/pallas_call | solution.py:452
  34.7 0.0 collective-permute-done.3.tok1_ref
  34.7 0.0 collective-permute-done.4.tok2_ref
  34.7 0.0 collective-permute-done.5.tok3_ref
  34.8 0.0 collective-permute-done.6
  34.8 0.9 %grad.1 = (bf16[128,40,128]{2,1,0:T(8,128)(2,1)S(1)}, bf16[64,512]{1,0:T(8,128)(2,1)}) custom-call(bf16[16,512]{1,0:T(8,128)(2,1)S(1)} %get-tuple-element.39.tok0_ref, bf16[16,512]{1,0:T(8,128)(2,1)S(1)} %collective-permute-done.3.tok1_ref, bf16[16,512]{1,0:T(8,128)(2,1)S(1)} %collective-permute-done.4.tok2_ref, ...), custom_call_target="tpu_custom_call" | custom-call | flops 201326592 | bytes 5242880 | tf_op jit(solution)/shard_map/grad/pallas_call | solution.py:455
  35.7 0.0 copy-start.3
  35.7 33.1 %all_to_all.10.recv_ref = bf16[128,40,128]{2,1,0:T(8,128)(2,1)S(1)} all-to-all(bf16[128,40,128]{2,1,0:T(8,128)(2,1)S(1)} %get-tuple-element.47), channel_id=1, replica_groups=mesh['tm'=32,'seq'=4] {'tm','seq'}, dimensions={0} | all-to-all | bytes 2621440 | tf_op jit(solution)/shard_map/all_to_all | solution.py:393
  68.8 1.0 %sum.1 = (bf16[128,16,128]{2,1,0:T(8,128)(2,1)}, f32[24,128]{1,0:T(8,128)S(1)}, f32[24,128]{1,0:T(8,128)}) custom-call(bf16[128,40,128]{2,1,0:T(8,128)(2,1)S(1)} %all_to_all.10.recv_ref), custom_call_target="tpu_custom_call" | custom-call | flops 1048576 | bytes 2097152 | tf_op jit(solution)/shard_map/sum/pallas_call | solution.py:484
  69.8 4.9 %all-to-all-start.1 = ((bf16[128,16,128]{2,1,0:T(8,128)(2,1)}), bf16[128,16,128]{2,1,0:T(8,128)(2,1)}, u32[]{:S(2)}, u32[]{:S(2)}) async-start(bf16[128,16,128]{2,1,0:T(8,128)(2,1)} %get-tuple-element.51), calls=%async_computation.1 | async-start | bytes 1048576 | tf_op jit(solution)/shard_map/all_to_all | solution.py:393
  74.7 1.4 %collective-permute-start.7 = (f32[24,128]{1,0:T(8,128)}, f32[24,128]{1,0:T(8,128)S(1)}, u32[]{:S(2)}, u32[]{:S(2)}) collective-permute-start(f32[24,128]{1,0:T(8,128)} %get-tuple-element.49), channel_id=1, source_target_pairs={{0,4},{4,0},{8,12},{12,8},{16,20},{20,16},{24,28},{28,24},{32,36},... | collective-permute-start | bytes 36872 | tf_op jit(solution)/shard_map/ppermute | solution.py:389
  76.1 0.7 copy-done.6
  76.8 0.8 copy-done.7
  77.6 5.3 %hidden.1 = bf16[512,3072]{1,0:T(8,128)(2,1)} custom-call(bf16[64,512]{1,0:T(8,128)(2,1)S(1)} %copy-done.7, bf16[512,3072]{1,0:T(8,128)(2,1)S(1)} %copy-done, bf16[64,3072]{1,0:T(8,128)(2,1)S(1)} %bitcast.11, f32[2,3072]{1,0:T(2,128)S(1)} %copy-done.6), custom_call_target="tpu_custom_call" | custom-call | flops 201326592 | bytes 6291456 | tf_op jit(solution)/shard_map/hidden/pallas_call | solution.py:469
  82.9 0.0 collective-permute-done.7.other_ref
  82.9 0.6 weight_out.1
  83.6 4.9 %all-to-all-done.1.all_ref = bf16[128,16,128]{2,1,0:T(8,128)(2,1)} async-done(((bf16[128,16,128]{2,1,0:T(8,128)(2,1)}), bf16[128,16,128]{2,1,0:T(8,128)(2,1)}, u32[]{:S(2)}, u32[]{:S(2)}) %all-to-all-start.1) | async-done | bytes 524320 | tf_op jit(solution)/shard_map/all_to_all | solution.py:393
  88.5 2.4 %last.1 = (f32[64,3072]{1,0:T(8,128)}, f32[2,3072]{1,0:T(2,128)}, f32[48,512]{1,0:T(8,128)}, f32[1,512]{1,0:T(1,128)}) custom-call(bf16[128,16,128]{2,1,0:T(8,128)(2,1)} %all-to-all-done.1.all_ref, bf16[64,3072]{1,0:T(8,128)(2,1)S(1)} %get-tuple-element.52.wt_ref, f32[2,3072]{1,0:T(2,128)S(1)} %get-tuple-element.53.mod_ref), custom_call_target="tpu_custom_call" | custom-call | flops 1048576 | bytes 2097152 | tf_op jit(solution)/shard_map/last/pallas_call | solution.py:501
  (3 shorter events, 0.0 us)
Async XLA Ops:
  0.6 11.9 %collective-permute-start.1 = (bf16[4,16,512]{2,1,0:T(8,128)(2,1)}, bf16[4,16,512]{2,1,0:T(8,128)(2,1)S(1)}, u32[]{:S(2)}, u32[]{:S(2)}) collective-permute-start(bf16[4,16,512]{2,1,0:T(8,128)(2,1)} %lat_ref.5), channel_id=1, source_target_pairs={{0,4},{4,8},{8,12},{12,16},{16,20},{20,24},{24,28},{28,32},{32,36}... | collective-permute-start | bytes 196616 | tf_op jit(solution)/shard_map/ppermute | solution.py:385
  6.5 6.0 %copy-start.4 = (bf16[4,16,512]{2,1,0:T(8,128)(2,1)S(1)}, bf16[4,16,512]{2,1,0:T(8,128)(2,1)}, u32[]{:S(2)}) copy-start(bf16[4,16,512]{2,1,0:T(8,128)(2,1)} %lat_ref.5) | copy-start | bytes 196612
  6.5 6.0 %copy-start.5 = (bf16[3,512,16]{1,2,0:T(8,128)(2,1)S(1)}, bf16[3,512,16]{1,2,0:T(8,128)(2,1)}, u32[]{:S(2)}) copy-start(bf16[3,512,16]{1,2,0:T(8,128)(2,1)} %param.12) | copy-start | bytes 147460
  6.6 6.0 %copy-start.8 = (s32[128]{0:T(128)S(1)}, s32[128]{0:T(128)}, u32[]{:S(2)}) copy-start(s32[128]{0:T(128)} %clip_ref.7) | copy-start | bytes 1540
  6.6 6.0 %copy-start.9 = (f32[512]{0:T(512)S(1)}, f32[512]{0:T(512)}, u32[]{:S(2)}) copy-start(f32[512]{0:T(512)} %param.13) | copy-start | bytes 6148
  6.6 17.2 %collective-permute-start = (bf16[2,512,512]{2,1,0:T(8,128)(2,1)S(1)}, bf16[2,512,512]{2,1,0:T(8,128)(2,1)S(1)}, u32[]{:S(2)}, u32[]{:S(2)}) collective-permute-start(bf16[2,512,512]{2,1,0:T(8,128)(2,1)S(1)} %slice.3.sent_ref), channel_id=1, source_target_pairs={{4,0},{8,4},{12,8},{16,12},{20,16},{24,20},{28,24},{32,28},{36,32}... | collective-permute-start | bytes 3145736 | tf_op jit(solution)/shard_map/ppermute | solution.py:385
  12.6 6.5 %copy-start.2 = (bf16[4,512,512]{2,1,0:T(8,128)(2,1)S(1)}, bf16[4,512,512]{2,1,0:T(8,128)(2,1)}, u32[]{:S(2)}) copy-start(bf16[4,512,512]{2,1,0:T(8,128)(2,1)} %grad_ref.1) | copy-start | bytes 6291460
  14.8 9.0 %collective-permute-start.2 = (f32[2,16,512]{2,1,0:T(8,128)S(1)}, f32[2,16,512]{2,1,0:T(8,128)S(1)}, u32[]{:S(2)}, u32[]{:S(2)}) collective-permute-start(f32[2,16,512]{2,1,0:T(8,128)S(1)} %get-tuple-element.35), channel_id=1, source_target_pairs={{4,0},{8,4},{12,8},{16,12},{20,16},{24,20},{28,24},{32,28},{36,32}... | collective-permute-start | bytes 196616 | tf_op jit(solution)/shard_map/ppermute | solution.py:385
  19.1 4.7 %copy-start.1 = (bf16[3,512,512]{2,1,0:T(8,128)(2,1)S(1)}, bf16[3,512,512]{2,1,0:T(8,128)(2,1)}, u32[]{:S(2)}) copy-start(bf16[3,512,512]{2,1,0:T(8,128)(2,1)} %conv_ref.1) | copy-start | bytes 4718596
  23.8 8.3 %copy-start = (bf16[512,3072]{1,0:T(8,128)(2,1)S(1)}, bf16[512,3072]{1,0:T(8,128)(2,1)}, u32[]{:S(2)}) copy-start(bf16[512,3072]{1,0:T(8,128)(2,1)} %hidden_ref.3) | copy-start | bytes 9437188
  26.3 8.5 %collective-permute-start.6 = (bf16[32,2,48,128]{3,2,1,0:T(8,128)(2,1)S(1)}, bf16[32,2,48,128]{3,2,1,0:T(8,128)(2,1)S(1)}, u32[]{:S(2)}, u32[]{:S(2)}) collective-permute-start(bf16[32,2,48,128]{3,2,1,0:T(8,128)(2,1)S(1)} %get-tuple-element.45), channel_id=1, source_target_pairs={{0,4},{4,0},{8,12},{12,8},{16,20},{20,16},{24,28},{28,24},{32,36},... | collective-permute-start | bytes 2359304 | tf_op jit(solution)/shard_map/ppermute | solution.py:389
  26.4 8.3 %collective-permute-start.3 = (bf16[16,512]{1,0:T(8,128)(2,1)S(1)}, bf16[16,512]{1,0:T(8,128)(2,1)S(1)}, u32[]{:S(2)}, u32[]{:S(2)}) collective-permute-start(bf16[16,512]{1,0:T(8,128)(2,1)S(1)} %get-tuple-element.40), channel_id=1, source_target_pairs={{0,1},{1,2},{2,3},{3,0},{4,5},{5,6},{6,7},{7,4},{8,9},{9,10},{10,1... | collective-permute-start | bytes 49160 | tf_op jit(solution)/shard_map/ppermute | solution.py:449
  28.1 6.6 %collective-permute-start.4 = (bf16[16,512]{1,0:T(8,128)(2,1)S(1)}, bf16[16,512]{1,0:T(8,128)(2,1)S(1)}, u32[]{:S(2)}, u32[]{:S(2)}) collective-permute-start(bf16[16,512]{1,0:T(8,128)(2,1)S(1)} %get-tuple-element.41), channel_id=1, source_target_pairs={{0,2},{1,3},{2,0},{3,1},{4,6},{5,7},{6,4},{7,5},{8,10},{9,11},{10,... | collective-permute-start | bytes 49160 | tf_op jit(solution)/shard_map/ppermute | solution.py:449
  31.4 3.3 %collective-permute-start.5 = (bf16[16,512]{1,0:T(8,128)(2,1)S(1)}, bf16[16,512]{1,0:T(8,128)(2,1)S(1)}, u32[]{:S(2)}, u32[]{:S(2)}) collective-permute-start(bf16[16,512]{1,0:T(8,128)(2,1)S(1)} %get-tuple-element.42), channel_id=1, source_target_pairs={{0,3},{1,0},{2,1},{3,2},{4,7},{5,4},{6,5},{7,6},{8,11},{9,8},{10,9... | collective-permute-start | bytes 49160 | tf_op jit(solution)/shard_map/ppermute | solution.py:449
  35.7 40.3 %copy-start.3 = (bf16[3072,64]{0,1:T(8,128)(2,1)S(1)}, bf16[3072,64]{0,1:T(8,128)(2,1)}, u32[]{:S(2)}) copy-start(bf16[3072,64]{0,1:T(8,128)(2,1)} %param.15) | copy-start | bytes 1179652
  69.8 18.6 %all-to-all-start.1 = ((bf16[128,16,128]{2,1,0:T(8,128)(2,1)}), bf16[128,16,128]{2,1,0:T(8,128)(2,1)}, u32[]{:S(2)}, u32[]{:S(2)}) async-start(bf16[128,16,128]{2,1,0:T(8,128)(2,1)} %get-tuple-element.51), calls=%async_computation.1 | async-start | bytes 1048576 | tf_op jit(solution)/shard_map/all_to_all | solution.py:393
  74.7 8.3 %collective-permute-start.7 = (f32[24,128]{1,0:T(8,128)}, f32[24,128]{1,0:T(8,128)S(1)}, u32[]{:S(2)}, u32[]{:S(2)}) collective-permute-start(f32[24,128]{1,0:T(8,128)} %get-tuple-element.49), channel_id=1, source_target_pairs={{0,4},{4,0},{8,12},{12,8},{16,20},{20,16},{24,28},{28,24},{32,36},... | collective-permute-start | bytes 36872 | tf_op jit(solution)/shard_map/ppermute | solution.py:389
  76.1 0.7 copy-start.6
  76.8 0.8 copy-start.7

commit v4 on v3

--- a/solution.py
+++ b/solution.py
@@ -124,29 +124,36 @@
     wcat_ref[TAPS * CL :, :] = tail.astype(BF)
 
 
-def pre_of(clip_ref, first, all_ref, z_ref, wcol, slot, frame):
+def half_of(clip_ref, first, all_ref, z_ref, wcol, slot, frame):
     load_taps(clip_ref, first, all_ref, z_ref, slot, frame, SLAB)
     z_ref[slot, TAPS * CL :, :] = jnp.ones((CL, PX), BF)
-    pre = mm(wcol, z_ref[slot], 1, 0)
-    return pre, 0.5 * jnp.tanh(0.5 * pre) + 0.5
+    h = mm(wcol, z_ref[slot], 1, 0)
+    return h, jnp.tanh(h) + 1.0
+
+
+def slope_of(act, twice):
+    sig = 0.5 * twice
+    return sig + act * (1.0 - sig)
 
 
 def k_first(
     clip_ref, prev_ref, lat_ref, win_ref, bias_ref, acc_ref,
-    act_ref, part_ref, halo_ref, icg_ref,
+    act_ref, part_ref, halo_ref, icg_ref, wcol_ref,
     all_ref, z_ref, wcat_ref, lacc_ref,
 ):
     first = lax.axis_index("tm") * SLAB
     all_ref[:SLAB] = prev_ref[...]
     all_ref[SLAB:] = lat_ref[...]
     set_weights(win_ref, bias_ref, wcat_ref)
-    wcol = wcat_ref[...].T
+    wcol = (wcat_ref[...].astype(F32) * 0.5).astype(BF).T
+    wcol_ref[...] = wcol
     lacc_ref[...] = jnp.zeros_like(lacc_ref)
     icg = jnp.zeros((E, C), F32)
     for t in range(2):
-        pre, sig = pre_of(clip_ref, first, all_ref, z_ref, wcol, t, t)
-        act_ref[t] = (pre * sig).astype(BF)
-        gp = (acc_ref[t] * (sig * (1.0 + pre * (1.0 - sig)))).astype(BF)
+        h, twice = half_of(clip_ref, first, all_ref, z_ref, wcol, t, t)
+        act = h * twice
+        act_ref[t] = act.astype(BF)
+        gp = (acc_ref[t] * slope_of(act, twice)).astype(BF)
         back = mm(wcat_ref[...], gp, 1, 0)
         for k in range(TAPS):
             src = source(clip_ref, first, t, k) + 2
@@ -157,30 +164,20 @@
     icg_ref[...] = icg
 
 
-def k_rest(
-    clip_ref, prev_ref, lat_ref, win_ref, bias_ref, act01_ref,
-    act_ref, slope_ref, all_ref, z_ref, wcat_ref,
-):
+def k_rest(clip_ref, prev_ref, lat_ref, wcol_ref, act01_ref, act_ref, slope_ref, all_ref, z_ref):
     first = lax.axis_index("tm") * SLAB
     all_ref[:SLAB] = prev_ref[...]
     all_ref[SLAB:] = lat_ref[...]
-    set_weights(win_ref, bias_ref, wcat_ref)
-    wcol = wcat_ref[...].T
+    wcol = wcol_ref[...]
     act_ref[2:4] = act01_ref[...]
-
-    def before(j, _):
-        pre, sig = pre_of(clip_ref, first, all_ref, z_ref, wcol, j, j - 2)
-        act_ref[j] = (pre * sig).astype(BF)
-        return 0
-
-    def own(j, _):
-        pre, sig = pre_of(clip_ref, first, all_ref, z_ref, wcol, j, j)
-        act_ref[j + 2] = (pre * sig).astype(BF)
-        slope_ref[j - 2] = sig * (1.0 + pre * (1.0 - sig))
-        return 0
-
-    lax.fori_loop(0, 2, before, 0)
-    lax.fori_loop(2, SLAB, own, 0)
+    for j in range(2):
+        h, twice = half_of(clip_ref, first, all_ref, z_ref, wcol, j, j - 2)
+        act_ref[j] = (h * twice).astype(BF)
+    for j in range(2, SLAB):
+        h, twice = half_of(clip_ref, first, all_ref, z_ref, wcol, j, j)
+        act = h * twice
+        act_ref[j + 2] = act.astype(BF)
+        slope_ref[j - 2] = slope_of(act, twice)
 
 
 def k_weight(clip_ref, grad_ref, act_ref, keep_ref, send_ref, acc_ref):
@@ -241,7 +238,7 @@
     icg_acc[...] = icg
     for f in range(SLAB):
         low_ref[f * CL : (f + 1) * CL, :] = lacc_ref[f].astype(BF)
-    r = lax.broadcasted_iota(jnp.int32, (PX, PX), 0)
+    r = lax.broadcasted_iota(jnp.int32, (PX, 1), 0)
     c = lax.broadcasted_iota(jnp.int32, (PX, PX), 1)
     pick = (((r & 3) << 7) + (r >> 2) == c).astype(F32).astype(BF)
     low_ref[...] = mm(low_ref[...], pick, 1, 0).astype(BF)
@@ -409,9 +406,11 @@
         ],
         mib=16, est=cost(1 << 10, 1 << 10), name="back",
     )(*pinned(clip_start, conv_w), grad_sent, *pinned(grad_out))
-    act01, part, halo, icg_part = call(
+    act01, part, halo, icg_part, wcol = call(
         k_first,
-        (sds((2, C, PX), BF), sds((SLAB, CL, PX), F32), sds((2, CL, PX), F32), sds((E, C), F32)),
+        (
+            sds((2, C, PX), BF), sds((SLAB, CL, PX), F32), sds((2, CL, PX), F32), sds((E, C), F32), sds((C, E), BF),
+        ),
         [SMEM] + [VMEM] * 5,
         [
             pltpu.VMEM((2 * SLAB, CL, PX), BF), pltpu.VMEM((2, E, PX), BF), pltpu.VMEM((E, C), BF),
@@ -421,10 +420,10 @@
     )(clip_start, lat_prev, latents, win, bias, acc)
     halo_recv = shifted(halo, -1)
     act, slope = call(
-        k_rest, (sds((SLAB + 2, C, PX), BF), sds((2, C, PX), F32)), [SMEM] + [VMEM] * 5,
-        [pltpu.VMEM((2 * SLAB, CL, PX), BF), pltpu.VMEM((SLAB, E, PX), BF), pltpu.VMEM((E, C), BF)],
+        k_rest, (sds((SLAB + 2, C, PX), BF), sds((2, C, PX), F32)), [SMEM] + [VMEM] * 4,
+        [pltpu.VMEM((2 * SLAB, CL, PX), BF), pltpu.VMEM((SLAB, E, PX), BF)],
         mib=16, est=cost(2 * unit, 8 << 20), name="rest",
-    )(clip_start, lat_prev, latents, win, bias, act01)
+    )(clip_start, lat_prev, latents, wcol, act01)
     keep, send = call(
         k_weight, (sds((32, 2, 48, 128), BF),) * 2, [SMEM] + [VMEM] * 2,
         [pltpu.VMEM((16, 2, 16, TAPS * C), F32)], mib=16, est=cost(50 * unit, 7 << 20), name="weight",

time: 91.4 us -> 90.9 us (level)
  transfers between devices with their start and end apart: 9 -> 9, of which waited for: 1 -> 2; matrix products, arithmetic and copies ran while one was open for 1% -> 1% of each run, Pallas kernels for 24% -> 23%
where the time goes in v4:
time: 90.9 us; the launch traced here: 90.4 us
  blocking collectives  32.9 us (36%)
  Pallas kernels  27.6 us (30%)
  starting transfers between devices  20.6 us (23%)
  waiting for transfers between devices  5.48 us (6%)
  local copies, waits for them, and re-layouts  2.92 us (3%)
    all_to_all x1, blocking collectives, exchange(): return lax.all_to_all(block, axes, split_axis=0, concat_axis=0, tiled=True)  32.9 us
    ppermute x3, starting transfers between devices, shifted(): return lax.ppermute(block, 'tm', route)  8.57 us
    ppermute x3, starting transfers between devices, local(): lax.ppermute(tok_parts[k], 'seq', [(i, (i + k) % 4) for i in range(4)])  5.74 us
    pallas_call x1, Pallas kernels, local(): pl.pallas_call(k_hidden, grid=(4,), out_shape=sds((NTOK, D), BF), in_spec...  5.32 us
    all_to_all x1, starting transfers between devices, exchange(): return lax.all_to_all(block, axes, split_axis=0, concat_axis=0, tiled=True)  4.87 us
    all_to_all x1, waiting for transfers between devices, exchange(): return lax.all_to_all(block, axes, split_axis=0, concat_axis=0, tiled=True)  4.86 us
    pallas_call x1, Pallas kernels, local(): call(k_weight, (sds((32, 2, 48, 128), BF),) * 2, [SMEM] + [VMEM] * 2, [pl...  4.65 us
    pallas_call x1, Pallas kernels, local(): call(k_back, sds((SLAB, C, PX), F32), [PIN, PIN, VMEM, PIN], [pltpu.SMEM(...  3.9 us
  transfers between devices with their start and end apart: 9, of which 2 were waited for; matrix products, arithmetic and copies ran while one was open for 1% of the time, Pallas kernels for 23%

profile of v4, /device:TPU:1, one launch (start us, length us, event | category | flops | bytes accessed | tf_op | source)
XLA Modules:
  0.0 90.4 jit_solution(12219460297814728536)
XLA Ops:
  0.6 4.6 %collective-permute-start.1 = (bf16[4,16,512]{2,1,0:T(8,128)(2,1)}, bf16[4,16,512]{2,1,0:T(8,128)(2,1)S(1)}, u32[]{:S(2)}, u32[]{:S(2)}) collective-permute-start(bf16[4,16,512]{2,1,0:T(8,128)(2,1)} %lat_ref.5), channel_id=1, source_target_pairs={{0,4},{4,8},{8,12},{12,16},{16,20},{20,24},{24,28},{28,32},{32,36}... | collective-permute-start | bytes 196616 | tf_op jit(solution)/shard_map/ppermute | solution.py:382
  5.2 1.3 %slice.3.sent_ref = bf16[2,512,512]{2,1,0:T(8,128)(2,1)S(1)} slice(bf16[4,512,512]{2,1,0:T(8,128)(2,1)} %grad_ref.1), slice={[0:2], [0:512], [0:512]} | slice | bytes 2097152 | tf_op jit(solution)/shard_map/slice | solution.py:399
  6.5 0.0 copy-start.4
  6.5 0.0 copy-start.5
  6.6 0.0 copy-start.8
  6.6 0.0 copy-start.9
  6.6 2.1 %collective-permute-start = (bf16[2,512,512]{2,1,0:T(8,128)(2,1)S(1)}, bf16[2,512,512]{2,1,0:T(8,128)(2,1)S(1)}, u32[]{:S(2)}, u32[]{:S(2)}) collective-permute-start(bf16[2,512,512]{2,1,0:T(8,128)(2,1)S(1)} %slice.3.sent_ref), channel_id=1, source_target_pairs={{4,0},{8,4},{12,8},{16,12},{20,16},{24,20},{28,24},{32,28},{36,32}... | collective-permute-start | bytes 3145736 | tf_op jit(solution)/shard_map/ppermute | solution.py:382
  8.6 3.9 %back.1.acc_ref.acc_in_ref = f32[4,512,512]{2,1,0:T(8,128)S(1)} custom-call(s32[128]{0:T(128)} %clip_ref.7, bf16[3,512,512]{2,1,0:T(8,128)(2,1)} %conv_ref.1, bf16[2,512,512]{2,1,0:T(8,128)(2,1)S(1)} %slice.3.sent_ref, bf16[4,512,512]{2,1,0:T(8,128)(2,1)} %grad_ref.1), custom_call_target="tpu_custom_call" | custom-call | flops 1024 | bytes 1024 | tf_op jit(solution)/shard_map/back/pallas_call | solution.py:401
  12.5 0.0 collective-permute-done.1.prev_ref
  12.6 0.0 copy-done.4
  12.6 0.0 copy-done.5
  12.6 0.0 copy-done.8
  12.6 0.0 copy-done.9
  12.6 0.0 copy-start.2
  12.6 2.1 %first.1 = (bf16[2,512,512]{2,1,0:T(8,128)(2,1)S(1)}, f32[4,16,512]{2,1,0:T(8,128)S(1)}, f32[2,16,512]{2,1,0:T(8,128)S(1)}, f32[64,512]{1,0:T(8,128)S(1)}, bf16[512,64]{1,0:T(8,128)(2,1)S(1)}) custom-call(s32[128]{0:T(128)S(1)} %copy-done.8, bf16[4,16,512]{2,1,0:T(8,128)(2,1)S(1)} %collective-permute-done.1.prev_ref, bf16[4,16,512]{2,1,0:T(8,128)(2,1)S(1)} %copy-done.4, ...), custom_call_target="tpu_custom_call" | custom-call | flops 536870912 | bytes 5242880 | tf_op jit(solution)/shard_map/first/pallas_call | solution.py:409
  14.7 1.9 %collective-permute-start.2 = (f32[2,16,512]{2,1,0:T(8,128)S(1)}, f32[2,16,512]{2,1,0:T(8,128)S(1)}, u32[]{:S(2)}, u32[]{:S(2)}) collective-permute-start(f32[2,16,512]{2,1,0:T(8,128)S(1)} %get-tuple-element.37), channel_id=1, source_target_pairs={{4,0},{8,4},{12,8},{16,12},{20,16},{24,20},{28,24},{32,28},{36,32}... | collective-permute-start | bytes 196616 | tf_op jit(solution)/shard_map/ppermute | solution.py:382
  16.6 1.6 %rest.1 = (bf16[6,512,512]{2,1,0:T(8,128)(2,1)S(1)}, f32[2,512,512]{2,1,0:T(8,128)S(1)}) custom-call(s32[128]{0:T(128)S(1)} %copy-done.8, bf16[4,16,512]{2,1,0:T(8,128)(2,1)S(1)} %collective-permute-done.1.prev_ref, bf16[4,16,512]{2,1,0:T(8,128)(2,1)S(1)} %copy-done.4, bf16[512,64]{1,0:T(8,128)(2,1)S(1)} %get-tuple-element.33.wcol_ref, ...), custom_call_target="tpu_custom_call" | custom-call | flops 536870912 | bytes 8388608 | tf_op jit(solution)/shard_map/rest/pallas_call | solution.py:422
  18.2 0.0 copy-done.2
  18.3 0.0 copy-start.1
  18.3 4.7 %weight.1 = (bf16[32,2,48,128]{3,2,1,0:T(8,128)(2,1)S(1)}, bf16[32,2,48,128]{3,2,1,0:T(8,128)(2,1)S(1)}) custom-call(s32[128]{0:T(128)S(1)} %copy-done.8, bf16[4,512,512]{2,1,0:T(8,128)(2,1)S(1)} %copy-done.2, bf16[6,512,512]{2,1,0:T(8,128)(2,1)S(1)} %get-tuple-element.39.act_ref), custom_call_target="tpu_custom_call" | custom-call | flops 13421772800 | bytes 7340032 | tf_op jit(solution)/shard_map/weight/pallas_call | solution.py:427
  22.9 0.6 collective-permute-done.2.halo_ref
  23.5 0.0 collective-permute-done.next_ref
  23.5 0.0 copy-done.1
  23.5 2.5 %second.1 = (bf16[16,512]{1,0:T(8,128)(2,1)S(1)}, bf16[16,512]{1,0:T(8,128)(2,1)S(1)}, bf16[16,512]{1,0:T(8,128)(2,1)S(1)}, bf16[16,512]{1,0:T(8,128)(2,1)S(1)},...) custom-call(s32[128]{0:T(128)S(1)} %copy-done.8, ...), custom_call_target="tpu_custom_call", output_to_operand_aliasing={{5}: (10, {})} | custom-call | flops 1610612736 | bytes 8388608 | tf_op jit(solution)/shard_map/second/pallas_call | solution.py:433
  26.0 0.1 collective-permute-start.6
  26.1 1.7 %collective-permute-start.3 = (bf16[16,512]{1,0:T(8,128)(2,1)S(1)}, bf16[16,512]{1,0:T(8,128)(2,1)S(1)}, u32[]{:S(2)}, u32[]{:S(2)}) collective-permute-start(bf16[16,512]{1,0:T(8,128)(2,1)S(1)} %get-tuple-element.42), channel_id=1, source_target_pairs={{0,1},{1,2},{2,3},{3,0},{4,5},{5,6},{6,7},{7,4},{8,9},{9,10},{10,1... | collective-permute-start | bytes 49160 | tf_op jit(solution)/shard_map/ppermute | solution.py:448
  27.8 3.3 %collective-permute-start.4 = (bf16[16,512]{1,0:T(8,128)(2,1)S(1)}, bf16[16,512]{1,0:T(8,128)(2,1)S(1)}, u32[]{:S(2)}, u32[]{:S(2)}) collective-permute-start(bf16[16,512]{1,0:T(8,128)(2,1)S(1)} %get-tuple-element.43), channel_id=1, source_target_pairs={{0,2},{1,3},{2,0},{3,1},{4,6},{5,7},{6,4},{7,5},{8,10},{9,11},{10,... | collective-permute-start | bytes 49160 | tf_op jit(solution)/shard_map/ppermute | solution.py:448
  31.1 0.7 collective-permute-start.5
  31.8 0.0 copy-done
  31.8 2.6 %prep.1.normed_ref = bf16[512,3072]{1,0:T(8,128)(2,1)S(1)} custom-call(bf16[512,3072]{1,0:T(8,128)(2,1)S(1)} %copy-done, bf16[16,16,128]{2,1,0:T(8,128)(2,1)S(1)} %get-tuple-element.45.after_ref.icg_ref), custom_call_target="tpu_custom_call" | custom-call | flops 15728640 | bytes 6291456 | tf_op jit(solution)/shard_map/prep/pallas_call | solution.py:451
  34.4 0.0 collective-permute-done.3.tok1_ref
  34.4 0.0 collective-permute-done.4.tok2_ref
  34.5 0.0 collective-permute-done.5.tok3_ref
  34.5 0.0 collective-permute-done.6
  34.5 0.9 %grad.1 = (bf16[128,40,128]{2,1,0:T(8,128)(2,1)S(1)}, bf16[64,512]{1,0:T(8,128)(2,1)}) custom-call(bf16[16,512]{1,0:T(8,128)(2,1)S(1)} %get-tuple-element.41.tok0_ref, bf16[16,512]{1,0:T(8,128)(2,1)S(1)} %collective-permute-done.3.tok1_ref, bf16[16,512]{1,0:T(8,128)(2,1)S(1)} %collective-permute-done.4.tok2_ref, ...), custom_call_target="tpu_custom_call" | custom-call | flops 201326592 | bytes 5242880 | tf_op jit(solution)/shard_map/grad/pallas_call | solution.py:454
  35.4 0.0 copy-start.3
  35.4 32.9 %all_to_all.10.recv_ref = bf16[128,40,128]{2,1,0:T(8,128)(2,1)S(1)} all-to-all(bf16[128,40,128]{2,1,0:T(8,128)(2,1)S(1)} %get-tuple-element.49), channel_id=1, replica_groups=mesh['tm'=32,'seq'=4] {'tm','seq'}, dimensions={0} | all-to-all | bytes 2621440 | tf_op jit(solution)/shard_map/all_to_all | solution.py:390
  68.4 1.0 %sum.1 = (bf16[128,16,128]{2,1,0:T(8,128)(2,1)}, f32[24,128]{1,0:T(8,128)S(1)}, f32[24,128]{1,0:T(8,128)}) custom-call(bf16[128,40,128]{2,1,0:T(8,128)(2,1)S(1)} %all_to_all.10.recv_ref), custom_call_target="tpu_custom_call" | custom-call | flops 1048576 | bytes 2097152 | tf_op jit(solution)/shard_map/sum/pallas_call | solution.py:483
  69.4 4.9 %all-to-all-start.1 = ((bf16[128,16,128]{2,1,0:T(8,128)(2,1)}), bf16[128,16,128]{2,1,0:T(8,128)(2,1)}, u32[]{:S(2)}, u32[]{:S(2)}) async-start(bf16[128,16,128]{2,1,0:T(8,128)(2,1)} %get-tuple-element.53), calls=%async_computation.1 | async-start | bytes 1048576 | tf_op jit(solution)/shard_map/all_to_all | solution.py:390
  74.3 1.4 %collective-permute-start.7 = (f32[24,128]{1,0:T(8,128)}, f32[24,128]{1,0:T(8,128)S(1)}, u32[]{:S(2)}, u32[]{:S(2)}) collective-permute-start(f32[24,128]{1,0:T(8,128)} %get-tuple-element.51), channel_id=1, source_target_pairs={{0,4},{4,0},{8,12},{12,8},{16,20},{20,16},{24,28},{28,24},{32,36},... | collective-permute-start | bytes 36872 | tf_op jit(solution)/shard_map/ppermute | solution.py:386
  75.6 0.0 copy-done.3
  75.6 0.7 copy-done.6
  76.4 0.8 copy-done.7
  77.2 5.3 %hidden.1 = bf16[512,3072]{1,0:T(8,128)(2,1)} custom-call(bf16[64,512]{1,0:T(8,128)(2,1)S(1)} %copy-done.7, bf16[512,3072]{1,0:T(8,128)(2,1)S(1)} %copy-done, bf16[64,3072]{1,0:T(8,128)(2,1)S(1)} %bitcast.11, f32[2,3072]{1,0:T(2,128)S(1)} %copy-done.6), custom_call_target="tpu_custom_call" | custom-call | flops 201326592 | bytes 6291456 | tf_op jit(solution)/shard_map/hidden/pallas_call | solution.py:468
  82.5 0.0 collective-permute-done.7.other_ref
  82.5 0.6 weight_out.1
  83.2 4.9 %all-to-all-done.1.all_ref = bf16[128,16,128]{2,1,0:T(8,128)(2,1)} async-done(((bf16[128,16,128]{2,1,0:T(8,128)(2,1)}), bf16[128,16,128]{2,1,0:T(8,128)(2,1)}, u32[]{:S(2)}, u32[]{:S(2)}) %all-to-all-start.1) | async-done | bytes 524320 | tf_op jit(solution)/shard_map/all_to_all | solution.py:390
  88.0 2.4 %last.1 = (f32[64,3072]{1,0:T(8,128)}, f32[2,3072]{1,0:T(2,128)}, f32[48,512]{1,0:T(8,128)}, f32[1,512]{1,0:T(1,128)}) custom-call(bf16[128,16,128]{2,1,0:T(8,128)(2,1)} %all-to-all-done.1.all_ref, bf16[64,3072]{1,0:T(8,128)(2,1)S(1)} %get-tuple-element.54.wt_ref, f32[2,3072]{1,0:T(2,128)S(1)} %get-tuple-element.55.mod_ref), custom_call_target="tpu_custom_call" | custom-call | flops 1048576 | bytes 2097152 | tf_op jit(solution)/shard_map/last/pallas_call | solution.py:500
  (3 shorter events, 0.0 us)
Async XLA Ops:
  0.6 11.9 %collective-permute-start.1 = (bf16[4,16,512]{2,1,0:T(8,128)(2,1)}, bf16[4,16,512]{2,1,0:T(8,128)(2,1)S(1)}, u32[]{:S(2)}, u32[]{:S(2)}) collective-permute-start(bf16[4,16,512]{2,1,0:T(8,128)(2,1)} %lat_ref.5), channel_id=1, source_target_pairs={{0,4},{4,8},{8,12},{12,16},{16,20},{20,24},{24,28},{28,32},{32,36}... | collective-permute-start | bytes 196616 | tf_op jit(solution)/shard_map/ppermute | solution.py:382
  6.5 6.0 %copy-start.4 = (bf16[4,16,512]{2,1,0:T(8,128)(2,1)S(1)}, bf16[4,16,512]{2,1,0:T(8,128)(2,1)}, u32[]{:S(2)}) copy-start(bf16[4,16,512]{2,1,0:T(8,128)(2,1)} %lat_ref.5) | copy-start | bytes 196612
  6.5 6.0 %copy-start.5 = (bf16[3,512,16]{1,2,0:T(8,128)(2,1)S(1)}, bf16[3,512,16]{1,2,0:T(8,128)(2,1)}, u32[]{:S(2)}) copy-start(bf16[3,512,16]{1,2,0:T(8,128)(2,1)} %param.12) | copy-start | bytes 147460
  6.6 6.0 %copy-start.8 = (s32[128]{0:T(128)S(1)}, s32[128]{0:T(128)}, u32[]{:S(2)}) copy-start(s32[128]{0:T(128)} %clip_ref.7) | copy-start | bytes 1540
  6.6 6.0 %copy-start.9 = (f32[512]{0:T(512)S(1)}, f32[512]{0:T(512)}, u32[]{:S(2)}) copy-start(f32[512]{0:T(512)} %param.13) | copy-start | bytes 6148
  6.6 17.0 %collective-permute-start = (bf16[2,512,512]{2,1,0:T(8,128)(2,1)S(1)}, bf16[2,512,512]{2,1,0:T(8,128)(2,1)S(1)}, u32[]{:S(2)}, u32[]{:S(2)}) collective-permute-start(bf16[2,512,512]{2,1,0:T(8,128)(2,1)S(1)} %slice.3.sent_ref), channel_id=1, source_target_pairs={{4,0},{8,4},{12,8},{16,12},{20,16},{24,20},{28,24},{32,28},{36,32}... | collective-permute-start | bytes 3145736 | tf_op jit(solution)/shard_map/ppermute | solution.py:382
  12.6 5.6 %copy-start.2 = (bf16[4,512,512]{2,1,0:T(8,128)(2,1)S(1)}, bf16[4,512,512]{2,1,0:T(8,128)(2,1)}, u32[]{:S(2)}) copy-start(bf16[4,512,512]{2,1,0:T(8,128)(2,1)} %grad_ref.1) | copy-start | bytes 6291460
  14.7 8.9 %collective-permute-start.2 = (f32[2,16,512]{2,1,0:T(8,128)S(1)}, f32[2,16,512]{2,1,0:T(8,128)S(1)}, u32[]{:S(2)}, u32[]{:S(2)}) collective-permute-start(f32[2,16,512]{2,1,0:T(8,128)S(1)} %get-tuple-element.37), channel_id=1, source_target_pairs={{4,0},{8,4},{12,8},{16,12},{20,16},{24,20},{28,24},{32,28},{36,32}... | collective-permute-start | bytes 196616 | tf_op jit(solution)/shard_map/ppermute | solution.py:382
  18.3 5.3 %copy-start.1 = (bf16[3,512,512]{2,1,0:T(8,128)(2,1)S(1)}, bf16[3,512,512]{2,1,0:T(8,128)(2,1)}, u32[]{:S(2)}) copy-start(bf16[3,512,512]{2,1,0:T(8,128)(2,1)} %conv_ref.1) | copy-start | bytes 4718596
  23.5 8.3 %copy-start = (bf16[512,3072]{1,0:T(8,128)(2,1)S(1)}, bf16[512,3072]{1,0:T(8,128)(2,1)}, u32[]{:S(2)}) copy-start(bf16[512,3072]{1,0:T(8,128)(2,1)} %hidden_ref.3) | copy-start | bytes 9437188
  26.0 8.5 %collective-permute-start.6 = (bf16[32,2,48,128]{3,2,1,0:T(8,128)(2,1)S(1)}, bf16[32,2,48,128]{3,2,1,0:T(8,128)(2,1)S(1)}, u32[]{:S(2)}, u32[]{:S(2)}) collective-permute-start(bf16[32,2,48,128]{3,2,1,0:T(8,128)(2,1)S(1)} %get-tuple-element.47), channel_id=1, source_target_pairs={{0,4},{4,0},{8,12},{12,8},{16,20},{20,16},{24,28},{28,24},{32,36},... | collective-permute-start | bytes 2359304 | tf_op jit(solution)/shard_map/ppermute | solution.py:386
  26.1 8.3 %collective-permute-start.3 = (bf16[16,512]{1,0:T(8,128)(2,1)S(1)}, bf16[16,512]{1,0:T(8,128)(2,1)S(1)}, u32[]{:S(2)}, u32[]{:S(2)}) collective-permute-start(bf16[16,512]{1,0:T(8,128)(2,1)S(1)} %get-tuple-element.42), channel_id=1, source_target_pairs={{0,1},{1,2},{2,3},{3,0},{4,5},{5,6},{6,7},{7,4},{8,9},{9,10},{10,1... | collective-permute-start | bytes 49160 | tf_op jit(solution)/shard_map/ppermute | solution.py:448
  27.8 6.6 %collective-permute-start.4 = (bf16[16,512]{1,0:T(8,128)(2,1)S(1)}, bf16[16,512]{1,0:T(8,128)(2,1)S(1)}, u32[]{:S(2)}, u32[]{:S(2)}) collective-permute-start(bf16[16,512]{1,0:T(8,128)(2,1)S(1)} %get-tuple-element.43), channel_id=1, source_target_pairs={{0,2},{1,3},{2,0},{3,1},{4,6},{5,7},{6,4},{7,5},{8,10},{9,11},{10,... | collective-permute-start | bytes 49160 | tf_op jit(solution)/shard_map/ppermute | solution.py:448
  31.1 3.3 %collective-permute-start.5 = (bf16[16,512]{1,0:T(8,128)(2,1)S(1)}, bf16[16,512]{1,0:T(8,128)(2,1)S(1)}, u32[]{:S(2)}, u32[]{:S(2)}) collective-permute-start(bf16[16,512]{1,0:T(8,128)(2,1)S(1)} %get-tuple-element.44), channel_id=1, source_target_pairs={{0,3},{1,0},{2,1},{3,2},{4,7},{5,4},{6,5},{7,6},{8,11},{9,8},{10,9... | collective-permute-start | bytes 49160 | tf_op jit(solution)/shard_map/ppermute | solution.py:448
  35.4 40.2 %copy-start.3 = (bf16[3072,64]{0,1:T(8,128)(2,1)S(1)}, bf16[3072,64]{0,1:T(8,128)(2,1)}, u32[]{:S(2)}) copy-start(bf16[3072,64]{0,1:T(8,128)(2,1)} %param.15) | copy-start | bytes 1179652
  69.4 18.6 %all-to-all-start.1 = ((bf16[128,16,128]{2,1,0:T(8,128)(2,1)}), bf16[128,16,128]{2,1,0:T(8,128)(2,1)}, u32[]{:S(2)}, u32[]{:S(2)}) async-start(bf16[128,16,128]{2,1,0:T(8,128)(2,1)} %get-tuple-element.53), calls=%async_computation.1 | async-start | bytes 1048576 | tf_op jit(solution)/shard_map/all_to_all | solution.py:390
  74.3 8.3 %collective-permute-start.7 = (f32[24,128]{1,0:T(8,128)}, f32[24,128]{1,0:T(8,128)S(1)}, u32[]{:S(2)}, u32[]{:S(2)}) collective-permute-start(f32[24,128]{1,0:T(8,128)} %get-tuple-element.51), channel_id=1, source_target_pairs={{0,4},{4,0},{8,12},{12,8},{16,20},{20,16},{24,28},{28,24},{32,36},... | collective-permute-start | bytes 36872 | tf_op jit(solution)/shard_map/ppermute | solution.py:386
  75.6 0.7 copy-start.6
  76.4 0.8 copy-start.7

commit v5 on v4

--- a/solution.py
+++ b/solution.py
@@ -479,7 +479,7 @@
         compiler_params=params(16),
         cost_estimate=cost(2 * NTOK * D * E, 6 << 20),
         name="hidden",
-    )(tok, hidden, wt, modulation)
+    )(*pinned(tok, hidden, wt, modulation))
     copies, own, away = pl.pallas_call(
         k_sum,
         out_shape=(pltpu.HBM((128, 16, 128), BF), sds((24, 128), F32), pltpu.HBM((24, 128), F32)),

time: 90.9 us -> 89.1 us (0.980)
  local copies, waits for them, and re-layouts: 2.92 us -> 1.34 us
  starting transfers between devices: 20.6 us -> 19.5 us
    pallas_call x1, Pallas kernels: 5.32 us -> 7.01 us  [local(): pl.pallas_call(k_hidden, grid=(4,), out_shape=sds((NTOK, D), BF), in_spec...]
    unnamed x20 -> x18, local copies, waits for them, and re-layouts: 1.62 us -> 0.05 us
    pallas_call x1, Pallas kernels: 2.37 us -> 1.32 us  [local(): call(k_last, (sds((E, D), F32), sds((2, D), F32), sds((TAPS * CL, C), F32...]
    all_to_all x1, starting transfers between devices: 4.87 us -> 3.83 us  [exchange(): return lax.all_to_all(block, axes, split_axis=0, concat_axis=0, tiled=True)]
  transfers between devices with their start and end apart: 9 -> 9, of which waited for: 2 -> 2; matrix products, arithmetic and copies ran while one was open for 1% -> 1% of each run, Pallas kernels for 23% -> 25%
where the time goes in v5:
time: 89.1 us; the launch traced here: 88.7 us
  blocking collectives  33 us (37%)
  Pallas kernels  28.2 us (32%)
  starting transfers between devices  19.5 us (22%)
  waiting for transfers between devices  5.77 us (6%)
  local copies, waits for them, and re-layouts  1.34 us (2%)
    all_to_all x1, blocking collectives, exchange(): return lax.all_to_all(block, axes, split_axis=0, concat_axis=0, tiled=True)  33 us
    ppermute x3, starting transfers between devices, shifted(): return lax.ppermute(block, 'tm', route)  8.57 us
    pallas_call x1, Pallas kernels, local(): pl.pallas_call(k_hidden, grid=(4,), out_shape=sds((NTOK, D), BF), in_spec...  7.01 us
    ppermute x3, starting transfers between devices, local(): lax.ppermute(tok_parts[k], 'seq', [(i, (i + k) % 4) for i in range(4)])  5.74 us
    all_to_all x1, waiting for transfers between devices, exchange(): return lax.all_to_all(block, axes, split_axis=0, concat_axis=0, tiled=True)  5.15 us
    pallas_call x1, Pallas kernels, local(): call(k_weight, (sds((32, 2, 48, 128), BF),) * 2, [SMEM] + [VMEM] * 2, [pl...  4.65 us
    pallas_call x1, Pallas kernels, local(): call(k_back, sds((SLAB, C, PX), F32), [PIN, PIN, VMEM, PIN], [pltpu.SMEM(...  3.9 us
    all_to_all x1, starting transfers between devices, exchange(): return lax.all_to_all(block, axes, split_axis=0, concat_axis=0, tiled=True)  3.83 us
  transfers between devices with their start and end apart: 9, of which 2 were waited for; matrix products, arithmetic and copies ran while one was open for 1% of the time, Pallas kernels for 25%

profile of v5, /device:TPU:1, one launch (start us, length us, event | category | flops | bytes accessed | tf_op | source)
XLA Modules:
  0.0 88.7 jit_solution(5435717897817563557)
XLA Ops:
  0.6 4.6 %collective-permute-start.1 = (bf16[4,16,512]{2,1,0:T(8,128)(2,1)}, bf16[4,16,512]{2,1,0:T(8,128)(2,1)S(1)}, u32[]{:S(2)}, u32[]{:S(2)}) collective-permute-start(bf16[4,16,512]{2,1,0:T(8,128)(2,1)} %lat_ref.5), channel_id=1, source_target_pairs={{0,4},{4,8},{8,12},{12,16},{16,20},{20,24},{24,28},{28,32},{32,36}... | collective-permute-start | bytes 196616 | tf_op jit(solution)/shard_map/ppermute | solution.py:382
  5.2 1.3 %slice.3.sent_ref = bf16[2,512,512]{2,1,0:T(8,128)(2,1)S(1)} slice(bf16[4,512,512]{2,1,0:T(8,128)(2,1)} %grad_ref.1), slice={[0:2], [0:512], [0:512]} | slice | bytes 2097152 | tf_op jit(solution)/shard_map/slice | solution.py:399
  6.5 0.0 copy-start.4
  6.5 0.0 copy-start.5
  6.6 0.0 copy-start.7
  6.6 0.0 copy-start.8
  6.6 2.1 %collective-permute-start = (bf16[2,512,512]{2,1,0:T(8,128)(2,1)S(1)}, bf16[2,512,512]{2,1,0:T(8,128)(2,1)S(1)}, u32[]{:S(2)}, u32[]{:S(2)}) collective-permute-start(bf16[2,512,512]{2,1,0:T(8,128)(2,1)S(1)} %slice.3.sent_ref), channel_id=1, source_target_pairs={{4,0},{8,4},{12,8},{16,12},{20,16},{24,20},{28,24},{32,28},{36,32}... | collective-permute-start | bytes 3145736 | tf_op jit(solution)/shard_map/ppermute | solution.py:382
  8.6 3.9 %back.1.acc_ref.acc_in_ref = f32[4,512,512]{2,1,0:T(8,128)S(1)} custom-call(s32[128]{0:T(128)} %clip_ref.7, bf16[3,512,512]{2,1,0:T(8,128)(2,1)} %conv_ref.1, bf16[2,512,512]{2,1,0:T(8,128)(2,1)S(1)} %slice.3.sent_ref, bf16[4,512,512]{2,1,0:T(8,128)(2,1)} %grad_ref.1), custom_call_target="tpu_custom_call" | custom-call | flops 1024 | bytes 1024 | tf_op jit(solution)/shard_map/back/pallas_call | solution.py:401
  12.5 0.0 collective-permute-done.1.prev_ref
  12.6 0.0 copy-done.4
  12.6 0.0 copy-done.5
  12.6 0.0 copy-done.7
  12.6 0.0 copy-done.8
  12.6 0.0 copy-start.2
  12.6 2.1 %first.1 = (bf16[2,512,512]{2,1,0:T(8,128)(2,1)S(1)}, f32[4,16,512]{2,1,0:T(8,128)S(1)}, f32[2,16,512]{2,1,0:T(8,128)S(1)}, f32[64,512]{1,0:T(8,128)S(1)}, bf16[512,64]{1,0:T(8,128)(2,1)S(1)}) custom-call(s32[128]{0:T(128)S(1)} %copy-done.7, bf16[4,16,512]{2,1,0:T(8,128)(2,1)S(1)} %collective-permute-done.1.prev_ref, bf16[4,16,512]{2,1,0:T(8,128)(2,1)S(1)} %copy-done.4, ...), custom_call_target="tpu_custom_call" | custom-call | flops 536870912 | bytes 5242880 | tf_op jit(solution)/shard_map/first/pallas_call | solution.py:409
  14.7 1.9 %collective-permute-start.2 = (f32[2,16,512]{2,1,0:T(8,128)S(1)}, f32[2,16,512]{2,1,0:T(8,128)S(1)}, u32[]{:S(2)}, u32[]{:S(2)}) collective-permute-start(f32[2,16,512]{2,1,0:T(8,128)S(1)} %get-tuple-element.37), channel_id=1, source_target_pairs={{4,0},{8,4},{12,8},{16,12},{20,16},{24,20},{28,24},{32,28},{36,32}... | collective-permute-start | bytes 196616 | tf_op jit(solution)/shard_map/ppermute | solution.py:382
  16.6 1.6 %rest.1 = (bf16[6,512,512]{2,1,0:T(8,128)(2,1)S(1)}, f32[2,512,512]{2,1,0:T(8,128)S(1)}) custom-call(s32[128]{0:T(128)S(1)} %copy-done.7, bf16[4,16,512]{2,1,0:T(8,128)(2,1)S(1)} %collective-permute-done.1.prev_ref, bf16[4,16,512]{2,1,0:T(8,128)(2,1)S(1)} %copy-done.4, bf16[512,64]{1,0:T(8,128)(2,1)S(1)} %get-tuple-element.33.wcol_ref, ...), custom_call_target="tpu_custom_call" | custom-call | flops 536870912 | bytes 8388608 | tf_op jit(solution)/shard_map/rest/pallas_call | solution.py:422
  18.2 0.0 copy-done.2
  18.3 0.0 copy-start.1
  18.3 4.7 %weight.1 = (bf16[32,2,48,128]{3,2,1,0:T(8,128)(2,1)S(1)}, bf16[32,2,48,128]{3,2,1,0:T(8,128)(2,1)S(1)}) custom-call(s32[128]{0:T(128)S(1)} %copy-done.7, bf16[4,512,512]{2,1,0:T(8,128)(2,1)S(1)} %copy-done.2, bf16[6,512,512]{2,1,0:T(8,128)(2,1)S(1)} %get-tuple-element.39.act_ref), custom_call_target="tpu_custom_call" | custom-call | flops 13421772800 | bytes 7340032 | tf_op jit(solution)/shard_map/weight/pallas_call | solution.py:427
  22.9 0.6 collective-permute-done.2.halo_ref
  23.5 0.0 collective-permute-done.next_ref
  23.5 0.0 copy-done.1
  23.5 0.0 copy-start
  23.5 2.5 %second.1 = (bf16[16,512]{1,0:T(8,128)(2,1)S(1)}, bf16[16,512]{1,0:T(8,128)(2,1)S(1)}, bf16[16,512]{1,0:T(8,128)(2,1)S(1)}, bf16[16,512]{1,0:T(8,128)(2,1)S(1)},...) custom-call(s32[128]{0:T(128)S(1)} %copy-done.7, ...), custom_call_target="tpu_custom_call", output_to_operand_aliasing={{5}: (10, {})} | custom-call | flops 1610612736 | bytes 8388608 | tf_op jit(solution)/shard_map/second/pallas_call | solution.py:433
  26.0 0.1 collective-permute-start.6
  26.1 1.7 %collective-permute-start.3 = (bf16[16,512]{1,0:T(8,128)(2,1)S(1)}, bf16[16,512]{1,0:T(8,128)(2,1)S(1)}, u32[]{:S(2)}, u32[]{:S(2)}) collective-permute-start(bf16[16,512]{1,0:T(8,128)(2,1)S(1)} %get-tuple-element.42), channel_id=1, source_target_pairs={{0,1},{1,2},{2,3},{3,0},{4,5},{5,6},{6,7},{7,4},{8,9},{9,10},{10,1... | collective-permute-start | bytes 49160 | tf_op jit(solution)/shard_map/ppermute | solution.py:448
  27.8 3.3 %collective-permute-start.4 = (bf16[16,512]{1,0:T(8,128)(2,1)S(1)}, bf16[16,512]{1,0:T(8,128)(2,1)S(1)}, u32[]{:S(2)}, u32[]{:S(2)}) collective-permute-start(bf16[16,512]{1,0:T(8,128)(2,1)S(1)} %get-tuple-element.43), channel_id=1, source_target_pairs={{0,2},{1,3},{2,0},{3,1},{4,6},{5,7},{6,4},{7,5},{8,10},{9,11},{10,... | collective-permute-start | bytes 49160 | tf_op jit(solution)/shard_map/ppermute | solution.py:448
  31.1 0.7 collective-permute-start.5
  31.8 0.0 copy-done
  31.8 2.6 %prep.1.normed_ref = bf16[512,3072]{1,0:T(8,128)(2,1)S(1)} custom-call(bf16[512,3072]{1,0:T(8,128)(2,1)S(1)} %copy-done, bf16[16,16,128]{2,1,0:T(8,128)(2,1)S(1)} %get-tuple-element.45.after_ref.icg_ref), custom_call_target="tpu_custom_call" | custom-call | flops 15728640 | bytes 6291456 | tf_op jit(solution)/shard_map/prep/pallas_call | solution.py:451
  34.4 0.0 collective-permute-done.3.tok1_ref
  34.4 0.0 collective-permute-done.4.tok2_ref
  34.5 0.0 collective-permute-done.5.tok3_ref
  34.5 0.0 collective-permute-done.6
  34.5 0.9 %grad.1 = (bf16[128,40,128]{2,1,0:T(8,128)(2,1)S(1)}, bf16[64,512]{1,0:T(8,128)(2,1)}) custom-call(bf16[16,512]{1,0:T(8,128)(2,1)S(1)} %get-tuple-element.41.tok0_ref, bf16[16,512]{1,0:T(8,128)(2,1)S(1)} %collective-permute-done.3.tok1_ref, bf16[16,512]{1,0:T(8,128)(2,1)S(1)} %collective-permute-done.4.tok2_ref, ...), custom_call_target="tpu_custom_call" | custom-call | flops 201326592 | bytes 5242880 | tf_op jit(solution)/shard_map/grad/pallas_call | solution.py:454
  35.4 33.0 %all_to_all.10.recv_ref = bf16[128,40,128]{2,1,0:T(8,128)(2,1)S(1)} all-to-all(bf16[128,40,128]{2,1,0:T(8,128)(2,1)S(1)} %get-tuple-element.49), channel_id=1, replica_groups=mesh['tm'=32,'seq'=4] {'tm','seq'}, dimensions={0} | all-to-all | bytes 2621440 | tf_op jit(solution)/shard_map/all_to_all | solution.py:390
  68.4 1.0 %sum.1 = (bf16[128,16,128]{2,1,0:T(8,128)(2,1)}, f32[24,128]{1,0:T(8,128)S(1)}, f32[24,128]{1,0:T(8,128)}) custom-call(bf16[128,40,128]{2,1,0:T(8,128)(2,1)S(1)} %all_to_all.10.recv_ref), custom_call_target="tpu_custom_call" | custom-call | flops 1048576 | bytes 2097152 | tf_op jit(solution)/shard_map/sum/pallas_call | solution.py:483
  69.4 3.8 %all-to-all-start.1 = ((bf16[128,16,128]{2,1,0:T(8,128)(2,1)}), bf16[128,16,128]{2,1,0:T(8,128)(2,1)S(1)}, u32[]{:S(2)}, u32[]{:S(2)}) async-start(bf16[128,16,128]{2,1,0:T(8,128)(2,1)} %get-tuple-element.53), calls=%async_computation.1 | async-start | bytes 1048576 | tf_op jit(solution)/shard_map/all_to_all | solution.py:390
  73.3 1.3 %collective-permute-start.7 = (f32[24,128]{1,0:T(8,128)}, f32[24,128]{1,0:T(8,128)S(1)}, u32[]{:S(2)}, u32[]{:S(2)}) collective-permute-start(f32[24,128]{1,0:T(8,128)} %get-tuple-element.51), channel_id=1, source_target_pairs={{0,4},{4,0},{8,12},{12,8},{16,20},{20,16},{24,28},{28,24},{32,36},... | collective-permute-start | bytes 36872 | tf_op jit(solution)/shard_map/ppermute | solution.py:386
  74.5 0.0 copy-start.3
  74.5 7.0 %hidden.1 = bf16[512,3072]{1,0:T(8,128)(2,1)} custom-call(bf16[64,512]{1,0:T(8,128)(2,1)} %get-tuple-element.48.tok_ref, bf16[512,3072]{1,0:T(8,128)(2,1)} %hidden_ref.3, bf16[64,3072]{1,0:T(8,128)(2,1)} %bitcast.11, f32[2,3072]{1,0:T(2,128)} %mod_ref.3), custom_call_target="tpu_custom_call" | custom-call | flops 201326592 | bytes 6291456 | tf_op jit(solution)/shard_map/hidden/pallas_call | solution.py:468
  81.6 0.0 collective-permute-done.7.other_ref
  81.6 0.0 copy-done.3
  81.6 0.0 copy-done.6
  81.6 0.6 weight_out.1
  82.2 5.1 %all-to-all-done.1.all_ref = bf16[128,16,128]{2,1,0:T(8,128)(2,1)S(1)} async-done(((bf16[128,16,128]{2,1,0:T(8,128)(2,1)}), bf16[128,16,128]{2,1,0:T(8,128)(2,1)S(1)}, u32[]{:S(2)}, u32[]{:S(2)}) %all-to-all-start.1) | async-done | bytes 524320 | tf_op jit(solution)/shard_map/all_to_all | solution.py:390
  87.4 1.3 %last.1 = (f32[64,3072]{1,0:T(8,128)}, f32[2,3072]{1,0:T(2,128)}, f32[48,512]{1,0:T(8,128)}, f32[1,512]{1,0:T(1,128)}) custom-call(bf16[128,16,128]{2,1,0:T(8,128)(2,1)S(1)} %all-to-all-done.1.all_ref, bf16[64,3072]{1,0:T(8,128)(2,1)S(1)} %get-tuple-element.54.wt_ref, f32[2,3072]{1,0:T(2,128)S(1)} %get-tuple-element.55.mod_ref), custom_call_target="tpu_custom_call" | custom-call | flops 1048576 | bytes 2097152 | tf_op jit(solution)/shard_map/last/pallas_call | solution.py:500
  (1 shorter events, 0.0 us)
Async XLA Ops:
  0.6 11.9 %collective-permute-start.1 = (bf16[4,16,512]{2,1,0:T(8,128)(2,1)}, bf16[4,16,512]{2,1,0:T(8,128)(2,1)S(1)}, u32[]{:S(2)}, u32[]{:S(2)}) collective-permute-start(bf16[4,16,512]{2,1,0:T(8,128)(2,1)} %lat_ref.5), channel_id=1, source_target_pairs={{0,4},{4,8},{8,12},{12,16},{16,20},{20,24},{24,28},{28,32},{32,36}... | collective-permute-start | bytes 196616 | tf_op jit(solution)/shard_map/ppermute | solution.py:382
  6.5 6.0 %copy-start.4 = (bf16[4,16,512]{2,1,0:T(8,128)(2,1)S(1)}, bf16[4,16,512]{2,1,0:T(8,128)(2,1)}, u32[]{:S(2)}) copy-start(bf16[4,16,512]{2,1,0:T(8,128)(2,1)} %lat_ref.5) | copy-start | bytes 196612
  6.5 6.0 %copy-start.5 = (bf16[3,512,16]{1,2,0:T(8,128)(2,1)S(1)}, bf16[3,512,16]{1,2,0:T(8,128)(2,1)}, u32[]{:S(2)}) copy-start(bf16[3,512,16]{1,2,0:T(8,128)(2,1)} %param.12) | copy-start | bytes 147460
  6.6 6.0 %copy-start.7 = (s32[128]{0:T(128)S(1)}, s32[128]{0:T(128)}, u32[]{:S(2)}) copy-start(s32[128]{0:T(128)} %clip_ref.7) | copy-start | bytes 1540
  6.6 6.0 %copy-start.8 = (f32[512]{0:T(512)S(1)}, f32[512]{0:T(512)}, u32[]{:S(2)}) copy-start(f32[512]{0:T(512)} %param.13) | copy-start | bytes 6148
  6.6 17.0 %collective-permute-start = (bf16[2,512,512]{2,1,0:T(8,128)(2,1)S(1)}, bf16[2,512,512]{2,1,0:T(8,128)(2,1)S(1)}, u32[]{:S(2)}, u32[]{:S(2)}) collective-permute-start(bf16[2,512,512]{2,1,0:T(8,128)(2,1)S(1)} %slice.3.sent_ref), channel_id=1, source_target_pairs={{4,0},{8,4},{12,8},{16,12},{20,16},{24,20},{28,24},{32,28},{36,32}... | collective-permute-start | bytes 3145736 | tf_op jit(solution)/shard_map/ppermute | solution.py:382
  12.6 5.6 %copy-start.2 = (bf16[4,512,512]{2,1,0:T(8,128)(2,1)S(1)}, bf16[4,512,512]{2,1,0:T(8,128)(2,1)}, u32[]{:S(2)}) copy-start(bf16[4,512,512]{2,1,0:T(8,128)(2,1)} %grad_ref.1) | copy-start | bytes 6291460
  14.7 8.9 %collective-permute-start.2 = (f32[2,16,512]{2,1,0:T(8,128)S(1)}, f32[2,16,512]{2,1,0:T(8,128)S(1)}, u32[]{:S(2)}, u32[]{:S(2)}) collective-permute-start(f32[2,16,512]{2,1,0:T(8,128)S(1)} %get-tuple-element.37), channel_id=1, source_target_pairs={{4,0},{8,4},{12,8},{16,12},{20,16},{24,20},{28,24},{32,28},{36,32}... | collective-permute-start | bytes 196616 | tf_op jit(solution)/shard_map/ppermute | solution.py:382
  18.3 5.3 %copy-start.1 = (bf16[3,512,512]{2,1,0:T(8,128)(2,1)S(1)}, bf16[3,512,512]{2,1,0:T(8,128)(2,1)}, u32[]{:S(2)}) copy-start(bf16[3,512,512]{2,1,0:T(8,128)(2,1)} %conv_ref.1) | copy-start | bytes 4718596
  23.5 8.3 %copy-start = (bf16[512,3072]{1,0:T(8,128)(2,1)S(1)}, bf16[512,3072]{1,0:T(8,128)(2,1)}, u32[]{:S(2)}) copy-start(bf16[512,3072]{1,0:T(8,128)(2,1)} %hidden_ref.3) | copy-start | bytes 9437188
  26.0 8.5 %collective-permute-start.6 = (bf16[32,2,48,128]{3,2,1,0:T(8,128)(2,1)S(1)}, bf16[32,2,48,128]{3,2,1,0:T(8,128)(2,1)S(1)}, u32[]{:S(2)}, u32[]{:S(2)}) collective-permute-start(bf16[32,2,48,128]{3,2,1,0:T(8,128)(2,1)S(1)} %get-tuple-element.47), channel_id=1, source_target_pairs={{0,4},{4,0},{8,12},{12,8},{16,20},{20,16},{24,28},{28,24},{32,36},... | collective-permute-start | bytes 2359304 | tf_op jit(solution)/shard_map/ppermute | solution.py:386
  26.1 8.3 %collective-permute-start.3 = (bf16[16,512]{1,0:T(8,128)(2,1)S(1)}, bf16[16,512]{1,0:T(8,128)(2,1)S(1)}, u32[]{:S(2)}, u32[]{:S(2)}) collective-permute-start(bf16[16,512]{1,0:T(8,128)(2,1)S(1)} %get-tuple-element.42), channel_id=1, source_target_pairs={{0,1},{1,2},{2,3},{3,0},{4,5},{5,6},{6,7},{7,4},{8,9},{9,10},{10,1... | collective-permute-start | bytes 49160 | tf_op jit(solution)/shard_map/ppermute | solution.py:448
  27.8 6.6 %collective-permute-start.4 = (bf16[16,512]{1,0:T(8,128)(2,1)S(1)}, bf16[16,512]{1,0:T(8,128)(2,1)S(1)}, u32[]{:S(2)}, u32[]{:S(2)}) collective-permute-start(bf16[16,512]{1,0:T(8,128)(2,1)S(1)} %get-tuple-element.43), channel_id=1, source_target_pairs={{0,2},{1,3},{2,0},{3,1},{4,6},{5,7},{6,4},{7,5},{8,10},{9,11},{10,... | collective-permute-start | bytes 49160 | tf_op jit(solution)/shard_map/ppermute | solution.py:448
  31.1 3.3 %collective-permute-start.5 = (bf16[16,512]{1,0:T(8,128)(2,1)S(1)}, bf16[16,512]{1,0:T(8,128)(2,1)S(1)}, u32[]{:S(2)}, u32[]{:S(2)}) collective-permute-start(bf16[16,512]{1,0:T(8,128)(2,1)S(1)} %get-tuple-element.44), channel_id=1, source_target_pairs={{0,3},{1,0},{2,1},{3,2},{4,7},{5,4},{6,5},{7,6},{8,11},{9,8},{10,9... | collective-permute-start | bytes 49160 | tf_op jit(solution)/shard_map/ppermute | solution.py:448
  69.4 18.0 %all-to-all-start.1 = ((bf16[128,16,128]{2,1,0:T(8,128)(2,1)}), bf16[128,16,128]{2,1,0:T(8,128)(2,1)S(1)}, u32[]{:S(2)}, u32[]{:S(2)}) async-start(bf16[128,16,128]{2,1,0:T(8,128)(2,1)} %get-tuple-element.53), calls=%async_computation.1 | async-start | bytes 1048576 | tf_op jit(solution)/shard_map/all_to_all | solution.py:390
  73.3 8.3 %collective-permute-start.7 = (f32[24,128]{1,0:T(8,128)}, f32[24,128]{1,0:T(8,128)S(1)}, u32[]{:S(2)}, u32[]{:S(2)}) collective-permute-start(f32[24,128]{1,0:T(8,128)} %get-tuple-element.51), channel_id=1, source_target_pairs={{0,4},{4,0},{8,12},{12,8},{16,20},{20,16},{24,28},{28,24},{32,36},... | collective-permute-start | bytes 36872 | tf_op jit(solution)/shard_map/ppermute | solution.py:386
  74.5 7.0 %copy-start.3 = (bf16[3072,64]{0,1:T(8,128)(2,1)S(1)}, bf16[3072,64]{0,1:T(8,128)(2,1)}, u32[]{:S(2)}) copy-start(bf16[3072,64]{0,1:T(8,128)(2,1)} %param.15) | copy-start | bytes 1179652
  74.5 7.0 %copy-start.6 = (f32[2,3072]{1,0:T(2,128)S(1)}, f32[2,3072]{1,0:T(2,128)}, u32[]{:S(2)}) copy-start(f32[2,3072]{1,0:T(2,128)} %mod_ref.3) | copy-start | bytes 73732

commit v6 on v5

--- a/solution.py
+++ b/solution.py
@@ -159,7 +159,7 @@
             src = source(clip_ref, first, t, k) + 2
             lacc_ref[src] += back[k * CL : (k + 1) * CL]
         icg = icg + mm(z_ref[t], gp, 1, 1)
-    halo_ref[...] = lacc_ref[:2]
+    halo_ref[...] = lacc_ref[:2].astype(BF)
     part_ref[...] = lacc_ref[2:]
     icg_ref[...] = icg
 
@@ -224,7 +224,7 @@
         acc_ref[1] += mm(conv_ref[2], next_ref[0], 0, 0)
 
     lacc_ref[:SLAB] = part_ref[...]
-    lacc_ref[2:SLAB] += halo_ref[...]
+    lacc_ref[2:SLAB] += halo_ref[...].astype(F32)
     icg = icg_in_ref[...]
     for t in range(2):
         gp = (acc_ref[t] * slope_ref[t]).astype(BF)
@@ -409,7 +409,7 @@
     act01, part, halo, icg_part, wcol = call(
         k_first,
         (
-            sds((2, C, PX), BF), sds((SLAB, CL, PX), F32), sds((2, CL, PX), F32), sds((E, C), F32), sds((C, E), BF),
+            sds((2, C, PX), BF), sds((SLAB, CL, PX), F32), sds((2, CL, PX), BF), sds((E, C), F32), sds((C, E), BF),
         ),
         [SMEM] + [VMEM] * 5,
         [

time: 89.1 us -> 88.8 us (level)
  no operation moved by 1% of the time
where the time goes in v6:
time: 88.8 us; the launch traced here: 88.4 us
  blocking collectives  33.1 us (37%)
  Pallas kernels  28.2 us (32%)
  starting transfers between devices  19.5 us (22%)
  waiting for transfers between devices  5.42 us (6%)
  local copies, waits for them, and re-layouts  1.34 us (2%)
    all_to_all x1, blocking collectives, exchange(): return lax.all_to_all(block, axes, split_axis=0, concat_axis=0, tiled=True)  33.1 us
    ppermute x3, starting transfers between devices, shifted(): return lax.ppermute(block, 'tm', route)  8.57 us
    pallas_call x1, Pallas kernels, local(): pl.pallas_call(k_hidden, grid=(4,), out_shape=sds((NTOK, D), BF), in_spec...  7.01 us
    ppermute x3, starting transfers between devices, local(): lax.ppermute(tok_parts[k], 'seq', [(i, (i + k) % 4) for i in range(4)])  5.73 us
    all_to_all x1, waiting for transfers between devices, exchange(): return lax.all_to_all(block, axes, split_axis=0, concat_axis=0, tiled=True)  5.15 us
    pallas_call x1, Pallas kernels, local(): call(k_weight, (sds((32, 2, 48, 128), BF),) * 2, [SMEM] + [VMEM] * 2, [pl...  4.65 us
    pallas_call x1, Pallas kernels, local(): call(k_back, sds((SLAB, C, PX), F32), [PIN, PIN, VMEM, PIN], [pltpu.SMEM(...  3.9 us
    all_to_all x1, starting transfers between devices, exchange(): return lax.all_to_all(block, axes, split_axis=0, concat_axis=0, tiled=True)  3.83 us
  transfers between devices with their start and end apart: 9, of which 2 were waited for; matrix products, arithmetic and copies ran while one was open for 1% of the time, Pallas kernels for 25%

profile of v6, /device:TPU:1, one launch (start us, length us, event | category | flops | bytes accessed | tf_op | source)
XLA Modules:
  0.0 88.4 jit_solution(10027770244618610755)
XLA Ops:
  0.6 4.6 %collective-permute-start.1 = (bf16[4,16,512]{2,1,0:T(8,128)(2,1)}, bf16[4,16,512]{2,1,0:T(8,128)(2,1)S(1)}, u32[]{:S(2)}, u32[]{:S(2)}) collective-permute-start(bf16[4,16,512]{2,1,0:T(8,128)(2,1)} %lat_ref.5), channel_id=1, source_target_pairs={{0,4},{4,8},{8,12},{12,16},{16,20},{20,24},{24,28},{28,32},{32,36}... | collective-permute-start | bytes 196616 | tf_op jit(solution)/shard_map/ppermute | solution.py:382
  5.2 1.3 %slice.3.sent_ref = bf16[2,512,512]{2,1,0:T(8,128)(2,1)S(1)} slice(bf16[4,512,512]{2,1,0:T(8,128)(2,1)} %grad_ref.1), slice={[0:2], [0:512], [0:512]} | slice | bytes 2097152 | tf_op jit(solution)/shard_map/slice | solution.py:399
  6.5 0.0 copy-start.4
  6.5 0.0 copy-start.5
  6.6 0.0 copy-start.7
  6.6 0.0 copy-start.8
  6.6 2.1 %collective-permute-start = (bf16[2,512,512]{2,1,0:T(8,128)(2,1)S(1)}, bf16[2,512,512]{2,1,0:T(8,128)(2,1)S(1)}, u32[]{:S(2)}, u32[]{:S(2)}) collective-permute-start(bf16[2,512,512]{2,1,0:T(8,128)(2,1)S(1)} %slice.3.sent_ref), channel_id=1, source_target_pairs={{4,0},{8,4},{12,8},{16,12},{20,16},{24,20},{28,24},{32,28},{36,32}... | collective-permute-start | bytes 3145736 | tf_op jit(solution)/shard_map/ppermute | solution.py:382
  8.6 3.9 %back.1.acc_ref.acc_in_ref = f32[4,512,512]{2,1,0:T(8,128)S(1)} custom-call(s32[128]{0:T(128)} %clip_ref.7, bf16[3,512,512]{2,1,0:T(8,128)(2,1)} %conv_ref.1, bf16[2,512,512]{2,1,0:T(8,128)(2,1)S(1)} %slice.3.sent_ref, bf16[4,512,512]{2,1,0:T(8,128)(2,1)} %grad_ref.1), custom_call_target="tpu_custom_call" | custom-call | flops 1024 | bytes 1024 | tf_op jit(solution)/shard_map/back/pallas_call | solution.py:401
  12.5 0.0 collective-permute-done.1.prev_ref
  12.6 0.0 copy-done.4
  12.6 0.0 copy-done.5
  12.6 0.0 copy-done.7
  12.6 0.0 copy-done.8
  12.6 0.0 copy-start.2
  12.6 2.0 %first.1 = (bf16[2,512,512]{2,1,0:T(8,128)(2,1)S(1)}, f32[4,16,512]{2,1,0:T(8,128)S(1)}, bf16[2,16,512]{2,1,0:T(8,128)(2,1)S(1)}, f32[64,512]{1,0:T(8,128)S(1)}, bf16[512,64]{1,0:T(8,128)(2,1)S(1)}) custom-call(s32[128]{0:T(128)S(1)} %copy-done.7, bf16[4,16,512]{2,1,0:T(8,128)(2,1)S(1)} %collective-permute-done.1.prev_ref, ...), custom_call_target="tpu_custom_call" | custom-call | flops 536870912 | bytes 5242880 | tf_op jit(solution)/shard_map/first/pallas_call | solution.py:409
  14.7 1.9 %collective-permute-start.2 = (bf16[2,16,512]{2,1,0:T(8,128)(2,1)S(1)}, bf16[2,16,512]{2,1,0:T(8,128)(2,1)S(1)}, u32[]{:S(2)}, u32[]{:S(2)}) collective-permute-start(bf16[2,16,512]{2,1,0:T(8,128)(2,1)S(1)} %get-tuple-element.37), channel_id=1, source_target_pairs={{4,0},{8,4},{12,8},{16,12},{20,16},{24,20},{28,24},{32,28},{36,32}... | collective-permute-start | bytes 98312 | tf_op jit(solution)/shard_map/ppermute | solution.py:382
  16.6 1.6 %rest.1 = (bf16[6,512,512]{2,1,0:T(8,128)(2,1)S(1)}, f32[2,512,512]{2,1,0:T(8,128)S(1)}) custom-call(s32[128]{0:T(128)S(1)} %copy-done.7, bf16[4,16,512]{2,1,0:T(8,128)(2,1)S(1)} %collective-permute-done.1.prev_ref, bf16[4,16,512]{2,1,0:T(8,128)(2,1)S(1)} %copy-done.4, bf16[512,64]{1,0:T(8,128)(2,1)S(1)} %get-tuple-element.33.wcol_ref, ...), custom_call_target="tpu_custom_call" | custom-call | flops 536870912 | bytes 8388608 | tf_op jit(solution)/shard_map/rest/pallas_call | solution.py:422
  18.2 0.0 copy-done.2
  18.3 0.0 copy-start.1
  18.3 4.7 %weight.1 = (bf16[32,2,48,128]{3,2,1,0:T(8,128)(2,1)S(1)}, bf16[32,2,48,128]{3,2,1,0:T(8,128)(2,1)S(1)}) custom-call(s32[128]{0:T(128)S(1)} %copy-done.7, bf16[4,512,512]{2,1,0:T(8,128)(2,1)S(1)} %copy-done.2, bf16[6,512,512]{2,1,0:T(8,128)(2,1)S(1)} %get-tuple-element.39.act_ref), custom_call_target="tpu_custom_call" | custom-call | flops 13421772800 | bytes 7340032 | tf_op jit(solution)/shard_map/weight/pallas_call | solution.py:427
  22.9 0.3 collective-permute-done.2.halo_ref
  23.2 0.0 collective-permute-done.next_ref
  23.2 0.0 copy-done.1
  23.2 0.0 copy-start
  23.2 2.5 %second.1 = (bf16[16,512]{1,0:T(8,128)(2,1)S(1)}, bf16[16,512]{1,0:T(8,128)(2,1)S(1)}, bf16[16,512]{1,0:T(8,128)(2,1)S(1)}, bf16[16,512]{1,0:T(8,128)(2,1)S(1)},...) custom-call(s32[128]{0:T(128)S(1)} %copy-done.7, ...), custom_call_target="tpu_custom_call", output_to_operand_aliasing={{5}: (10, {})} | custom-call | flops 1610612736 | bytes 8388608 | tf_op jit(solution)/shard_map/second/pallas_call | solution.py:433
  25.7 0.1 collective-permute-start.6
  25.8 1.7 %collective-permute-start.3 = (bf16[16,512]{1,0:T(8,128)(2,1)S(1)}, bf16[16,512]{1,0:T(8,128)(2,1)S(1)}, u32[]{:S(2)}, u32[]{:S(2)}) collective-permute-start(bf16[16,512]{1,0:T(8,128)(2,1)S(1)} %get-tuple-element.42), channel_id=1, source_target_pairs={{0,1},{1,2},{2,3},{3,0},{4,5},{5,6},{6,7},{7,4},{8,9},{9,10},{10,1... | collective-permute-start | bytes 49160 | tf_op jit(solution)/shard_map/ppermute | solution.py:448
  27.5 3.3 %collective-permute-start.4 = (bf16[16,512]{1,0:T(8,128)(2,1)S(1)}, bf16[16,512]{1,0:T(8,128)(2,1)S(1)}, u32[]{:S(2)}, u32[]{:S(2)}) collective-permute-start(bf16[16,512]{1,0:T(8,128)(2,1)S(1)} %get-tuple-element.43), channel_id=1, source_target_pairs={{0,2},{1,3},{2,0},{3,1},{4,6},{5,7},{6,4},{7,5},{8,10},{9,11},{10,... | collective-permute-start | bytes 49160 | tf_op jit(solution)/shard_map/ppermute | solution.py:448
  30.8 0.7 collective-permute-start.5
  31.5 0.0 copy-done
  31.5 2.6 %prep.1.normed_ref = bf16[512,3072]{1,0:T(8,128)(2,1)S(1)} custom-call(bf16[512,3072]{1,0:T(8,128)(2,1)S(1)} %copy-done, bf16[16,16,128]{2,1,0:T(8,128)(2,1)S(1)} %get-tuple-element.45.after_ref.icg_ref), custom_call_target="tpu_custom_call" | custom-call | flops 15728640 | bytes 6291456 | tf_op jit(solution)/shard_map/prep/pallas_call | solution.py:451
  34.1 0.0 collective-permute-done.3.tok1_ref
  34.1 0.0 collective-permute-done.4.tok2_ref
  34.1 0.0 collective-permute-done.5.tok3_ref
  34.1 0.0 collective-permute-done.6
  34.1 0.9 %grad.1 = (bf16[128,40,128]{2,1,0:T(8,128)(2,1)S(1)}, bf16[64,512]{1,0:T(8,128)(2,1)}) custom-call(bf16[16,512]{1,0:T(8,128)(2,1)S(1)} %get-tuple-element.41.tok0_ref, bf16[16,512]{1,0:T(8,128)(2,1)S(1)} %collective-permute-done.3.tok1_ref, bf16[16,512]{1,0:T(8,128)(2,1)S(1)} %collective-permute-done.4.tok2_ref, ...), custom_call_target="tpu_custom_call" | custom-call | flops 201326592 | bytes 5242880 | tf_op jit(solution)/shard_map/grad/pallas_call | solution.py:454
  35.1 33.1 %all_to_all.10.recv_ref = bf16[128,40,128]{2,1,0:T(8,128)(2,1)S(1)} all-to-all(bf16[128,40,128]{2,1,0:T(8,128)(2,1)S(1)} %get-tuple-element.49), channel_id=1, replica_groups=mesh['tm'=32,'seq'=4] {'tm','seq'}, dimensions={0} | all-to-all | bytes 2621440 | tf_op jit(solution)/shard_map/all_to_all | solution.py:390
  68.1 1.0 %sum.1 = (bf16[128,16,128]{2,1,0:T(8,128)(2,1)}, f32[24,128]{1,0:T(8,128)S(1)}, f32[24,128]{1,0:T(8,128)}) custom-call(bf16[128,40,128]{2,1,0:T(8,128)(2,1)S(1)} %all_to_all.10.recv_ref), custom_call_target="tpu_custom_call" | custom-call | flops 1048576 | bytes 2097152 | tf_op jit(solution)/shard_map/sum/pallas_call | solution.py:483
  69.2 3.8 %all-to-all-start.1 = ((bf16[128,16,128]{2,1,0:T(8,128)(2,1)}), bf16[128,16,128]{2,1,0:T(8,128)(2,1)S(1)}, u32[]{:S(2)}, u32[]{:S(2)}) async-start(bf16[128,16,128]{2,1,0:T(8,128)(2,1)} %get-tuple-element.53), calls=%async_computation.1 | async-start | bytes 1048576 | tf_op jit(solution)/shard_map/all_to_all | solution.py:390
  73.0 1.3 %collective-permute-start.7 = (f32[24,128]{1,0:T(8,128)}, f32[24,128]{1,0:T(8,128)S(1)}, u32[]{:S(2)}, u32[]{:S(2)}) collective-permute-start(f32[24,128]{1,0:T(8,128)} %get-tuple-element.51), channel_id=1, source_target_pairs={{0,4},{4,0},{8,12},{12,8},{16,20},{20,16},{24,28},{28,24},{32,36},... | collective-permute-start | bytes 36872 | tf_op jit(solution)/shard_map/ppermute | solution.py:386
  74.3 0.0 copy-start.3
  74.3 7.0 %hidden.1 = bf16[512,3072]{1,0:T(8,128)(2,1)} custom-call(bf16[64,512]{1,0:T(8,128)(2,1)} %get-tuple-element.48.tok_ref, bf16[512,3072]{1,0:T(8,128)(2,1)} %hidden_ref.3, bf16[64,3072]{1,0:T(8,128)(2,1)} %bitcast.11, f32[2,3072]{1,0:T(2,128)} %mod_ref.3), custom_call_target="tpu_custom_call" | custom-call | flops 201326592 | bytes 6291456 | tf_op jit(solution)/shard_map/hidden/pallas_call | solution.py:468
  81.3 0.0 collective-permute-done.7.other_ref
  81.3 0.0 copy-done.3
  81.3 0.0 copy-done.6
  81.3 0.6 weight_out.1
  82.0 5.2 %all-to-all-done.1.all_ref = bf16[128,16,128]{2,1,0:T(8,128)(2,1)S(1)} async-done(((bf16[128,16,128]{2,1,0:T(8,128)(2,1)}), bf16[128,16,128]{2,1,0:T(8,128)(2,1)S(1)}, u32[]{:S(2)}, u32[]{:S(2)}) %all-to-all-start.1) | async-done | bytes 524320 | tf_op jit(solution)/shard_map/all_to_all | solution.py:390
  87.1 1.3 %last.1 = (f32[64,3072]{1,0:T(8,128)}, f32[2,3072]{1,0:T(2,128)}, f32[48,512]{1,0:T(8,128)}, f32[1,512]{1,0:T(1,128)}) custom-call(bf16[128,16,128]{2,1,0:T(8,128)(2,1)S(1)} %all-to-all-done.1.all_ref, bf16[64,3072]{1,0:T(8,128)(2,1)S(1)} %get-tuple-element.54.wt_ref, f32[2,3072]{1,0:T(2,128)S(1)} %get-tuple-element.55.mod_ref), custom_call_target="tpu_custom_call" | custom-call | flops 1048576 | bytes 2097152 | tf_op jit(solution)/shard_map/last/pallas_call | solution.py:500
  (1 shorter events, 0.0 us)
Async XLA Ops:
  0.6 11.9 %collective-permute-start.1 = (bf16[4,16,512]{2,1,0:T(8,128)(2,1)}, bf16[4,16,512]{2,1,0:T(8,128)(2,1)S(1)}, u32[]{:S(2)}, u32[]{:S(2)}) collective-permute-start(bf16[4,16,512]{2,1,0:T(8,128)(2,1)} %lat_ref.5), channel_id=1, source_target_pairs={{0,4},{4,8},{8,12},{12,16},{16,20},{20,24},{24,28},{28,32},{32,36}... | collective-permute-start | bytes 196616 | tf_op jit(solution)/shard_map/ppermute | solution.py:382
  6.5 6.0 %copy-start.4 = (bf16[4,16,512]{2,1,0:T(8,128)(2,1)S(1)}, bf16[4,16,512]{2,1,0:T(8,128)(2,1)}, u32[]{:S(2)}) copy-start(bf16[4,16,512]{2,1,0:T(8,128)(2,1)} %lat_ref.5) | copy-start | bytes 196612
  6.5 6.0 %copy-start.5 = (bf16[3,512,16]{1,2,0:T(8,128)(2,1)S(1)}, bf16[3,512,16]{1,2,0:T(8,128)(2,1)}, u32[]{:S(2)}) copy-start(bf16[3,512,16]{1,2,0:T(8,128)(2,1)} %param.12) | copy-start | bytes 147460
  6.6 6.0 %copy-start.7 = (s32[128]{0:T(128)S(1)}, s32[128]{0:T(128)}, u32[]{:S(2)}) copy-start(s32[128]{0:T(128)} %clip_ref.7) | copy-start | bytes 1540
  6.6 6.0 %copy-start.8 = (f32[512]{0:T(512)S(1)}, f32[512]{0:T(512)}, u32[]{:S(2)}) copy-start(f32[512]{0:T(512)} %param.13) | copy-start | bytes 6148
  6.6 16.6 %collective-permute-start = (bf16[2,512,512]{2,1,0:T(8,128)(2,1)S(1)}, bf16[2,512,512]{2,1,0:T(8,128)(2,1)S(1)}, u32[]{:S(2)}, u32[]{:S(2)}) collective-permute-start(bf16[2,512,512]{2,1,0:T(8,128)(2,1)S(1)} %slice.3.sent_ref), channel_id=1, source_target_pairs={{4,0},{8,4},{12,8},{16,12},{20,16},{24,20},{28,24},{32,28},{36,32}... | collective-permute-start | bytes 3145736 | tf_op jit(solution)/shard_map/ppermute | solution.py:382
  12.6 5.6 %copy-start.2 = (bf16[4,512,512]{2,1,0:T(8,128)(2,1)S(1)}, bf16[4,512,512]{2,1,0:T(8,128)(2,1)}, u32[]{:S(2)}) copy-start(bf16[4,512,512]{2,1,0:T(8,128)(2,1)} %grad_ref.1) | copy-start | bytes 6291460
  14.7 8.5 %collective-permute-start.2 = (bf16[2,16,512]{2,1,0:T(8,128)(2,1)S(1)}, bf16[2,16,512]{2,1,0:T(8,128)(2,1)S(1)}, u32[]{:S(2)}, u32[]{:S(2)}) collective-permute-start(bf16[2,16,512]{2,1,0:T(8,128)(2,1)S(1)} %get-tuple-element.37), channel_id=1, source_target_pairs={{4,0},{8,4},{12,8},{16,12},{20,16},{24,20},{28,24},{32,28},{36,32}... | collective-permute-start | bytes 98312 | tf_op jit(solution)/shard_map/ppermute | solution.py:382
  18.3 4.9 %copy-start.1 = (bf16[3,512,512]{2,1,0:T(8,128)(2,1)S(1)}, bf16[3,512,512]{2,1,0:T(8,128)(2,1)}, u32[]{:S(2)}) copy-start(bf16[3,512,512]{2,1,0:T(8,128)(2,1)} %conv_ref.1) | copy-start | bytes 4718596
  23.2 8.3 %copy-start = (bf16[512,3072]{1,0:T(8,128)(2,1)S(1)}, bf16[512,3072]{1,0:T(8,128)(2,1)}, u32[]{:S(2)}) copy-start(bf16[512,3072]{1,0:T(8,128)(2,1)} %hidden_ref.3) | copy-start | bytes 9437188
  25.7 8.5 %collective-permute-start.6 = (bf16[32,2,48,128]{3,2,1,0:T(8,128)(2,1)S(1)}, bf16[32,2,48,128]{3,2,1,0:T(8,128)(2,1)S(1)}, u32[]{:S(2)}, u32[]{:S(2)}) collective-permute-start(bf16[32,2,48,128]{3,2,1,0:T(8,128)(2,1)S(1)} %get-tuple-element.47), channel_id=1, source_target_pairs={{0,4},{4,0},{8,12},{12,8},{16,20},{20,16},{24,28},{28,24},{32,36},... | collective-permute-start | bytes 2359304 | tf_op jit(solution)/shard_map/ppermute | solution.py:386
  25.8 8.3 %collective-permute-start.3 = (bf16[16,512]{1,0:T(8,128)(2,1)S(1)}, bf16[16,512]{1,0:T(8,128)(2,1)S(1)}, u32[]{:S(2)}, u32[]{:S(2)}) collective-permute-start(bf16[16,512]{1,0:T(8,128)(2,1)S(1)} %get-tuple-element.42), channel_id=1, source_target_pairs={{0,1},{1,2},{2,3},{3,0},{4,5},{5,6},{6,7},{7,4},{8,9},{9,10},{10,1... | collective-permute-start | bytes 49160 | tf_op jit(solution)/shard_map/ppermute | solution.py:448
  27.5 6.6 %collective-permute-start.4 = (bf16[16,512]{1,0:T(8,128)(2,1)S(1)}, bf16[16,512]{1,0:T(8,128)(2,1)S(1)}, u32[]{:S(2)}, u32[]{:S(2)}) collective-permute-start(bf16[16,512]{1,0:T(8,128)(2,1)S(1)} %get-tuple-element.43), channel_id=1, source_target_pairs={{0,2},{1,3},{2,0},{3,1},{4,6},{5,7},{6,4},{7,5},{8,10},{9,11},{10,... | collective-permute-start | bytes 49160 | tf_op jit(solution)/shard_map/ppermute | solution.py:448
  30.8 3.3 %collective-permute-start.5 = (bf16[16,512]{1,0:T(8,128)(2,1)S(1)}, bf16[16,512]{1,0:T(8,128)(2,1)S(1)}, u32[]{:S(2)}, u32[]{:S(2)}) collective-permute-start(bf16[16,512]{1,0:T(8,128)(2,1)S(1)} %get-tuple-element.44), channel_id=1, source_target_pairs={{0,3},{1,0},{2,1},{3,2},{4,7},{5,4},{6,5},{7,6},{8,11},{9,8},{10,9... | collective-permute-start | bytes 49160 | tf_op jit(solution)/shard_map/ppermute | solution.py:448
  69.2 18.0 %all-to-all-start.1 = ((bf16[128,16,128]{2,1,0:T(8,128)(2,1)}), bf16[128,16,128]{2,1,0:T(8,128)(2,1)S(1)}, u32[]{:S(2)}, u32[]{:S(2)}) async-start(bf16[128,16,128]{2,1,0:T(8,128)(2,1)} %get-tuple-element.53), calls=%async_computation.1 | async-start | bytes 1048576 | tf_op jit(solution)/shard_map/all_to_all | solution.py:390
  73.0 8.3 %collective-permute-start.7 = (f32[24,128]{1,0:T(8,128)}, f32[24,128]{1,0:T(8,128)S(1)}, u32[]{:S(2)}, u32[]{:S(2)}) collective-permute-start(f32[24,128]{1,0:T(8,128)} %get-tuple-element.51), channel_id=1, source_target_pairs={{0,4},{4,0},{8,12},{12,8},{16,20},{20,16},{24,28},{28,24},{32,36},... | collective-permute-start | bytes 36872 | tf_op jit(solution)/shard_map/ppermute | solution.py:386
  74.3 7.0 %copy-start.3 = (bf16[3072,64]{0,1:T(8,128)(2,1)S(1)}, bf16[3072,64]{0,1:T(8,128)(2,1)}, u32[]{:S(2)}) copy-start(bf16[3072,64]{0,1:T(8,128)(2,1)} %param.15) | copy-start | bytes 1179652
  74.3 7.0 %copy-start.6 = (f32[2,3072]{1,0:T(2,128)S(1)}, f32[2,3072]{1,0:T(2,128)}, u32[]{:S(2)}) copy-start(f32[2,3072]{1,0:T(2,128)} %mod_ref.3) | copy-start | bytes 73732

commit v7 on v6

--- a/solution.py
+++ b/solution.py
@@ -449,7 +449,7 @@
     ]
     other = swapped(send)
     normed = call(
-        k_prep, sds((NTOK, D), BF), [VMEM, HERE], mib=16, est=cost(10 * NTOK * D, 6 << 20), name="prep"
+        k_prep, sds((NTOK, D), BF), [VMEM, HERE], mib=16, est=cost(50 * unit, 6 << 20), name="prep"
     )(hidden, icg_blocks)
     pack, tok = pl.pallas_call(
         k_grad,

time: 88.8 us -> 88.3 us (level)
  transfers between devices with their start and end apart: 9 -> 9, of which waited for: 2 -> 2; matrix products, arithmetic and copies ran while one was open for 1% -> 1% of each run, Pallas kernels for 25% -> 26%
where the time goes in v7:
time: 88.3 us; the launch traced here: 87.6 us
  blocking collectives  32.3 us (37%)
  Pallas kernels  28.2 us (32%)
  starting transfers between devices  19.4 us (22%)
  waiting for transfers between devices  5.42 us (6%)
  local copies, waits for them, and re-layouts  1.34 us (2%)
    all_to_all x1, blocking collectives, exchange(): return lax.all_to_all(block, axes, split_axis=0, concat_axis=0, tiled=True)  32.3 us
    ppermute x3, starting transfers between devices, shifted(): return lax.ppermute(block, 'tm', route)  8.57 us
    pallas_call x1, Pallas kernels, local(): pl.pallas_call(k_hidden, grid=(4,), out_shape=sds((NTOK, D), BF), in_spec...  7.01 us
    ppermute x3, starting transfers between devices, local(): lax.ppermute(tok_parts[k], 'seq', [(i, (i + k) % 4) for i in range(4)])  5.73 us
    all_to_all x1, waiting for transfers between devices, exchange(): return lax.all_to_all(block, axes, split_axis=0, concat_axis=0, tiled=True)  5.15 us
    pallas_call x1, Pallas kernels, local(): call(k_weight, (sds((32, 2, 48, 128), BF),) * 2, [SMEM] + [VMEM] * 2, [pl...  4.65 us
    pallas_call x1, Pallas kernels, local(): call(k_back, sds((SLAB, C, PX), F32), [PIN, PIN, VMEM, PIN], [pltpu.SMEM(...  3.9 us
    all_to_all x1, starting transfers between devices, exchange(): return lax.all_to_all(block, axes, split_axis=0, concat_axis=0, tiled=True)  3.83 us
  transfers between devices with their start and end apart: 9, of which 2 were waited for; matrix products, arithmetic and copies ran while one was open for 1% of the time, Pallas kernels for 26%

profile of v7, /device:TPU:1, one launch (start us, length us, event | category | flops | bytes accessed | tf_op | source)
XLA Modules:
  0.0 87.6 jit_solution(6859204800904212504)
XLA Ops:
  0.6 4.6 %collective-permute-start.1 = (bf16[4,16,512]{2,1,0:T(8,128)(2,1)}, bf16[4,16,512]{2,1,0:T(8,128)(2,1)S(1)}, u32[]{:S(2)}, u32[]{:S(2)}) collective-permute-start(bf16[4,16,512]{2,1,0:T(8,128)(2,1)} %lat_ref.5), channel_id=1, source_target_pairs={{0,4},{4,8},{8,12},{12,16},{16,20},{20,24},{24,28},{28,32},{32,36}... | collective-permute-start | bytes 196616 | tf_op jit(solution)/shard_map/ppermute | solution.py:382
  5.2 1.3 %slice.3.sent_ref = bf16[2,512,512]{2,1,0:T(8,128)(2,1)S(1)} slice(bf16[4,512,512]{2,1,0:T(8,128)(2,1)} %grad_ref.1), slice={[0:2], [0:512], [0:512]} | slice | bytes 2097152 | tf_op jit(solution)/shard_map/slice | solution.py:399
  6.5 0.0 copy-start.4
  6.5 0.0 copy-start.5
  6.6 0.0 copy-start.7
  6.6 0.0 copy-start.8
  6.6 2.1 %collective-permute-start = (bf16[2,512,512]{2,1,0:T(8,128)(2,1)S(1)}, bf16[2,512,512]{2,1,0:T(8,128)(2,1)S(1)}, u32[]{:S(2)}, u32[]{:S(2)}) collective-permute-start(bf16[2,512,512]{2,1,0:T(8,128)(2,1)S(1)} %slice.3.sent_ref), channel_id=1, source_target_pairs={{4,0},{8,4},{12,8},{16,12},{20,16},{24,20},{28,24},{32,28},{36,32}... | collective-permute-start | bytes 3145736 | tf_op jit(solution)/shard_map/ppermute | solution.py:382
  8.6 3.9 %back.1.acc_ref.acc_in_ref = f32[4,512,512]{2,1,0:T(8,128)S(1)} custom-call(s32[128]{0:T(128)} %clip_ref.7, bf16[3,512,512]{2,1,0:T(8,128)(2,1)} %conv_ref.1, bf16[2,512,512]{2,1,0:T(8,128)(2,1)S(1)} %slice.3.sent_ref, bf16[4,512,512]{2,1,0:T(8,128)(2,1)} %grad_ref.1), custom_call_target="tpu_custom_call" | custom-call | flops 1024 | bytes 1024 | tf_op jit(solution)/shard_map/back/pallas_call | solution.py:401
  12.5 0.0 collective-permute-done.1.prev_ref
  12.6 0.0 copy-done.4
  12.6 0.0 copy-done.5
  12.6 0.0 copy-done.7
  12.6 0.0 copy-done.8
  12.6 0.0 copy-start.1
  12.6 2.0 %first.1 = (bf16[2,512,512]{2,1,0:T(8,128)(2,1)S(1)}, f32[4,16,512]{2,1,0:T(8,128)S(1)}, bf16[2,16,512]{2,1,0:T(8,128)(2,1)S(1)}, f32[64,512]{1,0:T(8,128)S(1)}, bf16[512,64]{1,0:T(8,128)(2,1)S(1)}) custom-call(s32[128]{0:T(128)S(1)} %copy-done.7, bf16[4,16,512]{2,1,0:T(8,128)(2,1)S(1)} %collective-permute-done.1.prev_ref, ...), custom_call_target="tpu_custom_call" | custom-call | flops 536870912 | bytes 5242880 | tf_op jit(solution)/shard_map/first/pallas_call | solution.py:409
  14.7 1.9 %collective-permute-start.2 = (bf16[2,16,512]{2,1,0:T(8,128)(2,1)S(1)}, bf16[2,16,512]{2,1,0:T(8,128)(2,1)S(1)}, u32[]{:S(2)}, u32[]{:S(2)}) collective-permute-start(bf16[2,16,512]{2,1,0:T(8,128)(2,1)S(1)} %get-tuple-element.37), channel_id=1, source_target_pairs={{4,0},{8,4},{12,8},{16,12},{20,16},{24,20},{28,24},{32,28},{36,32}... | collective-permute-start | bytes 98312 | tf_op jit(solution)/shard_map/ppermute | solution.py:382
  16.6 1.6 %rest.1 = (bf16[6,512,512]{2,1,0:T(8,128)(2,1)S(1)}, f32[2,512,512]{2,1,0:T(8,128)S(1)}) custom-call(s32[128]{0:T(128)S(1)} %copy-done.7, bf16[4,16,512]{2,1,0:T(8,128)(2,1)S(1)} %collective-permute-done.1.prev_ref, bf16[4,16,512]{2,1,0:T(8,128)(2,1)S(1)} %copy-done.4, bf16[512,64]{1,0:T(8,128)(2,1)S(1)} %get-tuple-element.33.wcol_ref, ...), custom_call_target="tpu_custom_call" | custom-call | flops 536870912 | bytes 8388608 | tf_op jit(solution)/shard_map/rest/pallas_call | solution.py:422
  18.2 0.0 copy-done.1
  18.3 0.0 copy-start
  18.3 4.7 %weight.1 = (bf16[32,2,48,128]{3,2,1,0:T(8,128)(2,1)S(1)}, bf16[32,2,48,128]{3,2,1,0:T(8,128)(2,1)S(1)}) custom-call(s32[128]{0:T(128)S(1)} %copy-done.7, bf16[4,512,512]{2,1,0:T(8,128)(2,1)S(1)} %copy-done.1, bf16[6,512,512]{2,1,0:T(8,128)(2,1)S(1)} %get-tuple-element.39.act_ref), custom_call_target="tpu_custom_call" | custom-call | flops 13421772800 | bytes 7340032 | tf_op jit(solution)/shard_map/weight/pallas_call | solution.py:427
  22.9 0.3 collective-permute-done.2.halo_ref
  23.2 0.0 collective-permute-done.next_ref
  23.2 0.0 copy-done
  23.2 0.0 copy-start.2
  23.2 2.5 %second.1 = (bf16[16,512]{1,0:T(8,128)(2,1)S(1)}, bf16[16,512]{1,0:T(8,128)(2,1)S(1)}, bf16[16,512]{1,0:T(8,128)(2,1)S(1)}, bf16[16,512]{1,0:T(8,128)(2,1)S(1)},...) custom-call(s32[128]{0:T(128)S(1)} %copy-done.7, ...), custom_call_target="tpu_custom_call", output_to_operand_aliasing={{5}: (10, {})} | custom-call | flops 1610612736 | bytes 8388608 | tf_op jit(solution)/shard_map/second/pallas_call | solution.py:433
  25.7 1.7 %collective-permute-start.3 = (bf16[16,512]{1,0:T(8,128)(2,1)S(1)}, bf16[16,512]{1,0:T(8,128)(2,1)S(1)}, u32[]{:S(2)}, u32[]{:S(2)}) collective-permute-start(bf16[16,512]{1,0:T(8,128)(2,1)S(1)} %get-tuple-element.42), channel_id=1, source_target_pairs={{0,1},{1,2},{2,3},{3,0},{4,5},{5,6},{6,7},{7,4},{8,9},{9,10},{10,1... | collective-permute-start | bytes 49160 | tf_op jit(solution)/shard_map/ppermute | solution.py:448
  27.4 3.3 %collective-permute-start.4 = (bf16[16,512]{1,0:T(8,128)(2,1)S(1)}, bf16[16,512]{1,0:T(8,128)(2,1)S(1)}, u32[]{:S(2)}, u32[]{:S(2)}) collective-permute-start(bf16[16,512]{1,0:T(8,128)(2,1)S(1)} %get-tuple-element.43), channel_id=1, source_target_pairs={{0,2},{1,3},{2,0},{3,1},{4,6},{5,7},{6,4},{7,5},{8,10},{9,11},{10,... | collective-permute-start | bytes 49160 | tf_op jit(solution)/shard_map/ppermute | solution.py:448
  30.7 0.7 collective-permute-start.5
  31.4 0.0 collective-permute-start.6
  31.4 0.0 copy-done.2
  31.4 2.6 %prep.1.normed_ref = bf16[512,3072]{1,0:T(8,128)(2,1)S(1)} custom-call(bf16[512,3072]{1,0:T(8,128)(2,1)S(1)} %copy-done.2, bf16[16,16,128]{2,1,0:T(8,128)(2,1)S(1)} %get-tuple-element.45.after_ref.icg_ref), custom_call_target="tpu_custom_call" | custom-call | flops 13421772800 | bytes 6291456 | tf_op jit(solution)/shard_map/prep/pallas_call | solution.py:451
  34.0 0.0 collective-permute-done.3.tok1_ref
  34.0 0.0 collective-permute-done.4.tok2_ref
  34.0 0.0 collective-permute-done.5.tok3_ref
  34.0 0.0 collective-permute-done.6
  34.0 0.9 %grad.1 = (bf16[128,40,128]{2,1,0:T(8,128)(2,1)S(1)}, bf16[64,512]{1,0:T(8,128)(2,1)}) custom-call(bf16[16,512]{1,0:T(8,128)(2,1)S(1)} %get-tuple-element.41.tok0_ref, bf16[16,512]{1,0:T(8,128)(2,1)S(1)} %collective-permute-done.3.tok1_ref, bf16[16,512]{1,0:T(8,128)(2,1)S(1)} %collective-permute-done.4.tok2_ref, ...), custom_call_target="tpu_custom_call" | custom-call | flops 201326592 | bytes 5242880 | tf_op jit(solution)/shard_map/grad/pallas_call | solution.py:454
  35.0 32.3 %all_to_all.10.recv_ref = bf16[128,40,128]{2,1,0:T(8,128)(2,1)S(1)} all-to-all(bf16[128,40,128]{2,1,0:T(8,128)(2,1)S(1)} %get-tuple-element.49), channel_id=1, replica_groups=mesh['tm'=32,'seq'=4] {'tm','seq'}, dimensions={0} | all-to-all | bytes 2621440 | tf_op jit(solution)/shard_map/all_to_all | solution.py:390
  67.3 1.0 %sum.1 = (bf16[128,16,128]{2,1,0:T(8,128)(2,1)}, f32[24,128]{1,0:T(8,128)S(1)}, f32[24,128]{1,0:T(8,128)}) custom-call(bf16[128,40,128]{2,1,0:T(8,128)(2,1)S(1)} %all_to_all.10.recv_ref), custom_call_target="tpu_custom_call" | custom-call | flops 1048576 | bytes 2097152 | tf_op jit(solution)/shard_map/sum/pallas_call | solution.py:483
  68.3 3.8 %all-to-all-start.1 = ((bf16[128,16,128]{2,1,0:T(8,128)(2,1)}), bf16[128,16,128]{2,1,0:T(8,128)(2,1)S(1)}, u32[]{:S(2)}, u32[]{:S(2)}) async-start(bf16[128,16,128]{2,1,0:T(8,128)(2,1)} %get-tuple-element.53), calls=%async_computation.1 | async-start | bytes 1048576 | tf_op jit(solution)/shard_map/all_to_all | solution.py:390
  72.2 1.3 %collective-permute-start.7 = (f32[24,128]{1,0:T(8,128)}, f32[24,128]{1,0:T(8,128)S(1)}, u32[]{:S(2)}, u32[]{:S(2)}) collective-permute-start(f32[24,128]{1,0:T(8,128)} %get-tuple-element.51), channel_id=1, source_target_pairs={{0,4},{4,0},{8,12},{12,8},{16,20},{20,16},{24,28},{28,24},{32,36},... | collective-permute-start | bytes 36872 | tf_op jit(solution)/shard_map/ppermute | solution.py:386
  73.5 0.0 copy-start.3
  73.5 7.0 %hidden.1 = bf16[512,3072]{1,0:T(8,128)(2,1)} custom-call(bf16[64,512]{1,0:T(8,128)(2,1)} %get-tuple-element.48.tok_ref, bf16[512,3072]{1,0:T(8,128)(2,1)} %hidden_ref.3, bf16[64,3072]{1,0:T(8,128)(2,1)} %bitcast.11, f32[2,3072]{1,0:T(2,128)} %mod_ref.3), custom_call_target="tpu_custom_call" | custom-call | flops 201326592 | bytes 6291456 | tf_op jit(solution)/shard_map/hidden/pallas_call | solution.py:468
  80.5 0.0 collective-permute-done.7.other_ref
  80.5 0.0 copy-done.3
  80.5 0.0 copy-done.6
  80.5 0.6 weight_out.1
  81.1 5.1 %all-to-all-done.1.all_ref = bf16[128,16,128]{2,1,0:T(8,128)(2,1)S(1)} async-done(((bf16[128,16,128]{2,1,0:T(8,128)(2,1)}), bf16[128,16,128]{2,1,0:T(8,128)(2,1)S(1)}, u32[]{:S(2)}, u32[]{:S(2)}) %all-to-all-start.1) | async-done | bytes 524320 | tf_op jit(solution)/shard_map/all_to_all | solution.py:390
  86.3 1.3 %last.1 = (f32[64,3072]{1,0:T(8,128)}, f32[2,3072]{1,0:T(2,128)}, f32[48,512]{1,0:T(8,128)}, f32[1,512]{1,0:T(1,128)}) custom-call(bf16[128,16,128]{2,1,0:T(8,128)(2,1)S(1)} %all-to-all-done.1.all_ref, bf16[64,3072]{1,0:T(8,128)(2,1)S(1)} %get-tuple-element.54.wt_ref, f32[2,3072]{1,0:T(2,128)S(1)} %get-tuple-element.55.mod_ref), custom_call_target="tpu_custom_call" | custom-call | flops 1048576 | bytes 2097152 | tf_op jit(solution)/shard_map/last/pallas_call | solution.py:500
  (1 shorter events, 0.0 us)
Async XLA Ops:
  0.6 11.9 %collective-permute-start.1 = (bf16[4,16,512]{2,1,0:T(8,128)(2,1)}, bf16[4,16,512]{2,1,0:T(8,128)(2,1)S(1)}, u32[]{:S(2)}, u32[]{:S(2)}) collective-permute-start(bf16[4,16,512]{2,1,0:T(8,128)(2,1)} %lat_ref.5), channel_id=1, source_target_pairs={{0,4},{4,8},{8,12},{12,16},{16,20},{20,24},{24,28},{28,32},{32,36}... | collective-permute-start | bytes 196616 | tf_op jit(solution)/shard_map/ppermute | solution.py:382
  6.5 6.0 %copy-start.4 = (bf16[4,16,512]{2,1,0:T(8,128)(2,1)S(1)}, bf16[4,16,512]{2,1,0:T(8,128)(2,1)}, u32[]{:S(2)}) copy-start(bf16[4,16,512]{2,1,0:T(8,128)(2,1)} %lat_ref.5) | copy-start | bytes 196612
  6.5 6.0 %copy-start.5 = (bf16[3,512,16]{1,2,0:T(8,128)(2,1)S(1)}, bf16[3,512,16]{1,2,0:T(8,128)(2,1)}, u32[]{:S(2)}) copy-start(bf16[3,512,16]{1,2,0:T(8,128)(2,1)} %param.12) | copy-start | bytes 147460
  6.6 6.0 %copy-start.7 = (s32[128]{0:T(128)S(1)}, s32[128]{0:T(128)}, u32[]{:S(2)}) copy-start(s32[128]{0:T(128)} %clip_ref.7) | copy-start | bytes 1540
  6.6 6.0 %copy-start.8 = (f32[512]{0:T(512)S(1)}, f32[512]{0:T(512)}, u32[]{:S(2)}) copy-start(f32[512]{0:T(512)} %param.13) | copy-start | bytes 6148
  6.6 16.6 %collective-permute-start = (bf16[2,512,512]{2,1,0:T(8,128)(2,1)S(1)}, bf16[2,512,512]{2,1,0:T(8,128)(2,1)S(1)}, u32[]{:S(2)}, u32[]{:S(2)}) collective-permute-start(bf16[2,512,512]{2,1,0:T(8,128)(2,1)S(1)} %slice.3.sent_ref), channel_id=1, source_target_pairs={{4,0},{8,4},{12,8},{16,12},{20,16},{24,20},{28,24},{32,28},{36,32}... | collective-permute-start | bytes 3145736 | tf_op jit(solution)/shard_map/ppermute | solution.py:382
  12.6 5.6 %copy-start.1 = (bf16[4,512,512]{2,1,0:T(8,128)(2,1)S(1)}, bf16[4,512,512]{2,1,0:T(8,128)(2,1)}, u32[]{:S(2)}) copy-start(bf16[4,512,512]{2,1,0:T(8,128)(2,1)} %grad_ref.1) | copy-start | bytes 6291460
  14.7 8.5 %collective-permute-start.2 = (bf16[2,16,512]{2,1,0:T(8,128)(2,1)S(1)}, bf16[2,16,512]{2,1,0:T(8,128)(2,1)S(1)}, u32[]{:S(2)}, u32[]{:S(2)}) collective-permute-start(bf16[2,16,512]{2,1,0:T(8,128)(2,1)S(1)} %get-tuple-element.37), channel_id=1, source_target_pairs={{4,0},{8,4},{12,8},{16,12},{20,16},{24,20},{28,24},{32,28},{36,32}... | collective-permute-start | bytes 98312 | tf_op jit(solution)/shard_map/ppermute | solution.py:382
  18.3 4.9 %copy-start = (bf16[3,512,512]{2,1,0:T(8,128)(2,1)S(1)}, bf16[3,512,512]{2,1,0:T(8,128)(2,1)}, u32[]{:S(2)}) copy-start(bf16[3,512,512]{2,1,0:T(8,128)(2,1)} %conv_ref.1) | copy-start | bytes 4718596
  23.2 8.2 %copy-start.2 = (bf16[512,3072]{1,0:T(8,128)(2,1)S(1)}, bf16[512,3072]{1,0:T(8,128)(2,1)}, u32[]{:S(2)}) copy-start(bf16[512,3072]{1,0:T(8,128)(2,1)} %hidden_ref.3) | copy-start | bytes 9437188
  25.7 8.3 %collective-permute-start.3 = (bf16[16,512]{1,0:T(8,128)(2,1)S(1)}, bf16[16,512]{1,0:T(8,128)(2,1)S(1)}, u32[]{:S(2)}, u32[]{:S(2)}) collective-permute-start(bf16[16,512]{1,0:T(8,128)(2,1)S(1)} %get-tuple-element.42), channel_id=1, source_target_pairs={{0,1},{1,2},{2,3},{3,0},{4,5},{5,6},{6,7},{7,4},{8,9},{9,10},{10,1... | collective-permute-start | bytes 49160 | tf_op jit(solution)/shard_map/ppermute | solution.py:448
  27.4 6.6 %collective-permute-start.4 = (bf16[16,512]{1,0:T(8,128)(2,1)S(1)}, bf16[16,512]{1,0:T(8,128)(2,1)S(1)}, u32[]{:S(2)}, u32[]{:S(2)}) collective-permute-start(bf16[16,512]{1,0:T(8,128)(2,1)S(1)} %get-tuple-element.43), channel_id=1, source_target_pairs={{0,2},{1,3},{2,0},{3,1},{4,6},{5,7},{6,4},{7,5},{8,10},{9,11},{10,... | collective-permute-start | bytes 49160 | tf_op jit(solution)/shard_map/ppermute | solution.py:448
  30.7 3.3 %collective-permute-start.5 = (bf16[16,512]{1,0:T(8,128)(2,1)S(1)}, bf16[16,512]{1,0:T(8,128)(2,1)S(1)}, u32[]{:S(2)}, u32[]{:S(2)}) collective-permute-start(bf16[16,512]{1,0:T(8,128)(2,1)S(1)} %get-tuple-element.44), channel_id=1, source_target_pairs={{0,3},{1,0},{2,1},{3,2},{4,7},{5,4},{6,5},{7,6},{8,11},{9,8},{10,9... | collective-permute-start | bytes 49160 | tf_op jit(solution)/shard_map/ppermute | solution.py:448
  31.4 2.6 %collective-permute-start.6 = (bf16[32,2,48,128]{3,2,1,0:T(8,128)(2,1)S(1)}, bf16[32,2,48,128]{3,2,1,0:T(8,128)(2,1)S(1)}, u32[]{:S(2)}, u32[]{:S(2)}) collective-permute-start(bf16[32,2,48,128]{3,2,1,0:T(8,128)(2,1)S(1)} %get-tuple-element.47), channel_id=1, source_target_pairs={{0,4},{4,0},{8,12},{12,8},{16,20},{20,16},{24,28},{28,24},{32,36},... | collective-permute-start | bytes 2359304 | tf_op jit(solution)/shard_map/ppermute | solution.py:386
  68.3 18.0 %all-to-all-start.1 = ((bf16[128,16,128]{2,1,0:T(8,128)(2,1)}), bf16[128,16,128]{2,1,0:T(8,128)(2,1)S(1)}, u32[]{:S(2)}, u32[]{:S(2)}) async-start(bf16[128,16,128]{2,1,0:T(8,128)(2,1)} %get-tuple-element.53), calls=%async_computation.1 | async-start | bytes 1048576 | tf_op jit(solution)/shard_map/all_to_all | solution.py:390
  72.2 8.3 %collective-permute-start.7 = (f32[24,128]{1,0:T(8,128)}, f32[24,128]{1,0:T(8,128)S(1)}, u32[]{:S(2)}, u32[]{:S(2)}) collective-permute-start(f32[24,128]{1,0:T(8,128)} %get-tuple-element.51), channel_id=1, source_target_pairs={{0,4},{4,0},{8,12},{12,8},{16,20},{20,16},{24,28},{28,24},{32,36},... | collective-permute-start | bytes 36872 | tf_op jit(solution)/shard_map/ppermute | solution.py:386
  73.5 7.0 %copy-start.3 = (bf16[3072,64]{0,1:T(8,128)(2,1)S(1)}, bf16[3072,64]{0,1:T(8,128)(2,1)}, u32[]{:S(2)}) copy-start(bf16[3072,64]{0,1:T(8,128)(2,1)} %param.15) | copy-start | bytes 1179652
  73.5 7.0 %copy-start.6 = (f32[2,3072]{1,0:T(2,128)S(1)}, f32[2,3072]{1,0:T(2,128)}, u32[]{:S(2)}) copy-start(f32[2,3072]{1,0:T(2,128)} %mod_ref.3) | copy-start | bytes 73732
